TPU v7x, 32 devices: a whole 2x2x4 slice. The times are simulated.
32 devices in a mesh: grp: 2 (over y), row: 16 (over z, x, core).
Axes of the slice: x: 2, y: 2, z: 4, core: 2. Of those that a mesh axis runs over, the one named last changes fastest.
Arguments:
- pair_acts: bfloat16 [96, 48, 128], P(('grp', 'row')), parts along dimension 0, may hold values from -24 to 24, as said below
- token_count: int32 [2], P('grp'), parts along dimension 0, may hold values from 24 to 48
- input_gain: float32 [128], replicated, may hold values from 0.1 to 1.9
- input_bias: float32 [128], replicated, may hold values from -3 to 3
- project_weight: bfloat16 [128, 64], replicated, may hold values from -0.5 to 0.5
- gate_weight: bfloat16 [128, 128], replicated, may hold values from -0.5 to 0.5
- output_norm_gain: float32 [16], replicated, may hold values from 0.1 to 1.9
- output_shift_bias: float32 [16], replicated, may hold values from -3 to 3
- output_weight: bfloat16 [16, 128], replicated, may hold values from -1.5 to 1.5
- update_grad: bfloat16 [96, 48, 128], P(('grp', 'row')), parts along dimension 0, may hold values from -6 to 6
Outputs:
- update: bfloat16 [96, 48, 128], P(('grp', 'row')), parts along dimension 0
- pair_grad: float32 [96, 48, 128], P(('grp', 'row')), parts along dimension 0
- project_grad: float32 [256, 64], P('grp'), parts along dimension 0
- gate_grad: float32 [256, 128], P('grp'), parts along dimension 0
- output_grad: float32 [32, 128], P('grp'), parts along dimension 0
There are 2 independent parts, one for each index of `grp`. A program takes and returns all parts, laid end to end along the dimension named above; an argument that names none is the same for every part. Nothing has to cross between parts.
Inputs may be any that keep to these rules, and one draw needn't show every extreme that they name: `pair_acts`: pair activations; channel scales differ.
All inputs are finite; a program needn't handle non-finite values.
Results may differ from a plain program's by a relative error of at most 0.0085.
Values may be sent and summed in bfloat16 or wider, within the bound.
No kernel may reach another device: no remote copies, remote signals or barrier semaphores. Data moves between devices by JAX's collectives and lax.ppermute only.
A program may use at most 64 MiB of HBM per device.

v0:
```python
import jax
import jax.numpy as jnp
from jax import lax
from jax.sharding import PartitionSpec as P


def layer_normalize(values, norm_gain, norm_bias, reduce_axis):
    average = jnp.mean(values, axis=reduce_axis, keepdims=True)
    centered = values - average
    variance = jnp.mean(centered * centered, axis=reduce_axis, keepdims=True)
    inv_std = lax.rsqrt(variance + 1e-05)
    normed = centered * inv_std
    return (normed * norm_gain + norm_bias, normed, inv_std)


def norm_backward_pass(upstream, normed, inv_std, norm_gain, reduce_axis):
    scaled = upstream * norm_gain
    first = jnp.mean(scaled, axis=reduce_axis, keepdims=True)
    second = jnp.mean(scaled * normed, axis=reduce_axis, keepdims=True)
    return inv_std * (scaled - first - normed * second)


def body(
    pair_acts,
    token_count,
    input_gain,
    input_bias,
    project_weight,
    gate_weight,
    output_norm_gain,
    output_shift_bias,
    output_weight,
    update_grad,
):
    single_float_format = jnp.float32
    brain_float_sixteen = jnp.bfloat16
    row_count, length, channels = pair_acts.shape
    hidden = output_weight.shape[0]
    row_start = lax.axis_index("row") * row_count
    live_limit = token_count[0]
    row_live = (row_start + jnp.arange(row_count, dtype=jnp.int32) < live_limit).astype(
        single_float_format
    )
    col_live = (jnp.arange(length, dtype=jnp.int32) < live_limit).astype(single_float_format)
    live_mask = row_live[:, None] * col_live[None, :]
    zn32, zhat, zscale = layer_normalize(
        pair_acts.astype(single_float_format), input_gain, input_bias, -1
    )
    normed_pair = zn32.astype(brain_float_sixteen)
    projected = jnp.einsum(
        "rkd,de->erk", normed_pair, project_weight, preferred_element_type=single_float_format
    ).reshape(4, hidden, row_count, length)
    gate_left = jax.nn.sigmoid(projected[1])
    gate_right = jax.nn.sigmoid(projected[3])
    left_panel = (live_mask * gate_left * projected[0]).astype(brain_float_sixteen)
    right_panel = (live_mask * gate_right * projected[2]).astype(brain_float_sixteen)
    stacked = jnp.stack([left_panel, right_panel], axis=1)
    columns = lax.all_to_all(stacked, "row", split_axis=0, concat_axis=2, tiled=True)
    left_cols = columns[:, 0]
    right_cols = columns[:, 1]
    products = jnp.einsum(
        "cik,cjk->cij", left_cols, right_cols, preferred_element_type=single_float_format
    ).astype(brain_float_sixteen)
    triangle_product = lax.all_to_all(products, "row", split_axis=1, concat_axis=0, tiled=True)
    normed_input_single, standardized_input, input_inverse_scale = layer_normalize(
        triangle_product.astype(single_float_format),
        output_norm_gain[:, None, None],
        output_shift_bias[:, None, None],
        0,
    )
    normed_tri = normed_input_single.astype(brain_float_sixteen)
    mixed = jnp.einsum(
        "crk,cd->rkd", normed_tri, output_weight, preferred_element_type=single_float_format
    )
    gate_out = jax.nn.sigmoid(
        jnp.einsum(
            "rkd,de->rke", normed_pair, gate_weight, preferred_element_type=single_float_format
        )
    )
    update = (gate_out * mixed).astype(brain_float_sixteen)
    cotangent = update_grad.astype(single_float_format)
    mixed_grad = (cotangent * gate_out).astype(brain_float_sixteen)
    gate_logit_grad = (cotangent * mixed * gate_out * (1.0 - gate_out)).astype(brain_float_sixteen)
    output_terms = jnp.einsum(
        "crk,rkd->cd", normed_tri, mixed_grad, preferred_element_type=single_float_format
    )
    triangle_normed_gradient = jnp.einsum(
        "rkd,cd->crk", mixed_grad, output_weight, preferred_element_type=single_float_format
    )
    triangle_gradient = norm_backward_pass(
        triangle_normed_gradient,
        standardized_input,
        input_inverse_scale,
        output_norm_gain[:, None, None],
        0,
    ).astype(brain_float_sixteen)
    grad_cols = lax.all_to_all(triangle_gradient, "row", split_axis=0, concat_axis=1, tiled=True)
    left_col_grad = jnp.einsum(
        "cij,cjk->cik", grad_cols, right_cols, preferred_element_type=single_float_format
    ).astype(brain_float_sixteen)
    right_col_grad = jnp.einsum(
        "cij,cik->cjk", grad_cols, left_cols, preferred_element_type=single_float_format
    ).astype(brain_float_sixteen)
    returned = lax.all_to_all(
        jnp.stack([left_col_grad, right_col_grad], axis=1),
        "row",
        split_axis=2,
        concat_axis=0,
        tiled=True,
    )
    left_grad = returned[:, 0].astype(single_float_format)
    right_grad = returned[:, 1].astype(single_float_format)
    project_terms = jnp.stack(
        [
            left_grad * live_mask * gate_left,
            left_grad * live_mask * projected[0] * gate_left * (1.0 - gate_left),
            right_grad * live_mask * gate_right,
            right_grad * live_mask * projected[2] * gate_right * (1.0 - gate_right),
        ]
    )
    project_terms = project_terms.astype(brain_float_sixteen).reshape(4 * hidden, row_count, length)
    project_part = jnp.einsum(
        "rkd,erk->de", normed_pair, project_terms, preferred_element_type=single_float_format
    )
    gate_part = jnp.einsum(
        "rkd,rke->de", normed_pair, gate_logit_grad, preferred_element_type=single_float_format
    )
    totals = lax.psum((project_part, gate_part, output_terms), "row")
    project_grad = totals[0] / length
    gate_grad = totals[1] / length
    output_grad = totals[2] / length
    normed_grad = jnp.einsum(
        "erk,de->rkd", project_terms, project_weight, preferred_element_type=single_float_format
    ) + jnp.einsum(
        "rke,de->rkd", gate_logit_grad, gate_weight, preferred_element_type=single_float_format
    )
    pair_grad = norm_backward_pass(normed_grad, zhat, zscale, input_gain, -1)
    return (update, pair_grad, project_grad, gate_grad, output_grad)


def solution(mesh):
    in_specs = (
        P(("grp", "row"), None, None),
        P("grp"),
        P(),
        P(),
        P(),
        P(),
        P(),
        P(),
        P(),
        P(("grp", "row"), None, None),
    )
    out_specs = (
        P(("grp", "row"), None, None),
        P(("grp", "row"), None, None),
        P("grp", None),
        P("grp", None),
        P("grp", None),
    )
    return jax.shard_map(body, mesh=mesh, in_specs=in_specs, out_specs=out_specs, check_vma=False)
```

profile of v0, /device:TPU:1, one launch (start us, length us, event | category | flops | bytes accessed | tf_op | source)
XLA Modules:
  0.0 151.4 jit_solution(1068883461417984955)
XLA Ops:
  7.9 0.9 convert_reduce_fusion
  9.1 0.4 copy-done.3
  10.2 13.0 %all_to_all.54 = bf16[16,2,144]{2,1,0:T(2,128)(2,1)S(1)} all-to-all(bf16[16,2,144]{2,1,0:T(2,128)(2,1)S(1)} %reshape.186), channel_id=1, replica_groups=mesh['grp'=2,'row'=16] {'row'}, dimensions={0} | all-to-all | bytes 18432 | tf_op jit(solution)/shard_map/all_to_all | solution.py:58
  23.5 0.6 copy.48
  24.1 4.0 %all-to-all-start.1 = ((bf16[1,48,48]{2,0,1:T(2,128)(2,1)}), bf16[1,48,48]{2,0,1:T(2,128)(2,1)S(1)}, u32[]{:S(2)}, u32[]{:S(2)}) async-start(bf16[1,48,48]{2,0,1:T(2,128)(2,1)} %copy.48), calls=%async_computation.1 | async-start | bytes 49152 | tf_op jit(solution)/shard_map/all_to_all | solution.py:64
  28.4 5.7 %all-to-all-done.1 = bf16[1,48,48]{2,0,1:T(2,128)(2,1)S(1)} async-done(((bf16[1,48,48]{2,0,1:T(2,128)(2,1)}), bf16[1,48,48]{2,0,1:T(2,128)(2,1)S(1)}, u32[]{:S(2)}, u32[]{:S(2)}) %all-to-all-start.1) | async-done | bytes 4640 | tf_op jit(solution)/shard_map/all_to_all | solution.py:64
  34.3 0.7 copy-done.2
  35.2 0.6 copy-done.6
  35.9 0.6 copy.50
  36.5 0.8 fusion.22
  37.4 4.1 %all-to-all-start.2 = ((bf16[16,3,48]{2,1,0:T(4,128)(2,1)}), bf16[16,3,48]{2,1,0:T(4,128)(2,1)S(1)}, u32[]{:S(2)}, u32[]{:S(2)}) async-start(bf16[16,3,48]{2,1,0:T(4,128)(2,1)} %copy.50), calls=%async_computation.2 | async-start | bytes 32768 | tf_op jit(solution)/shard_map/all_to_all | solution.py:97
  41.4 0.9 convolution_bitcast_fusion.1
  42.3 5.0 %all-to-all-done.2 = bf16[16,3,48]{2,1,0:T(4,128)(2,1)S(1)} async-done(((bf16[16,3,48]{2,1,0:T(4,128)(2,1)}), bf16[16,3,48]{2,1,0:T(4,128)(2,1)S(1)}, u32[]{:S(2)}, u32[]{:S(2)}) %all-to-all-start.2) | async-done | bytes 4640 | tf_op jit(solution)/shard_map/all_to_all | solution.py:97
  47.7 0.7 reshape.188
  48.4 4.0 %all-to-all-start.3 = ((bf16[16,2,144]{2,1,0:T(2,128)(2,1)}), bf16[16,2,144]{2,1,0:T(2,128)(2,1)S(1)}, u32[]{:S(2)}, u32[]{:S(2)}) async-start(bf16[16,2,144]{2,1,0:T(2,128)(2,1)} %reshape.188), calls=%async_computation.3 | async-start | bytes 32768 | tf_op jit(solution)/shard_map/all_to_all | solution.py:104
  52.7 0.5 all-reduce.3.cloned.1.call-update
  53.2 5.2 %all-to-all-done.3 = bf16[16,2,144]{2,1,0:T(2,128)(2,1)S(1)} async-done(((bf16[16,2,144]{2,1,0:T(2,128)(2,1)}), bf16[16,2,144]{2,1,0:T(2,128)(2,1)S(1)}, u32[]{:S(2)}, u32[]{:S(2)}) %all-to-all-start.3) | async-done | bytes 9248 | tf_op jit(solution)/shard_map/all_to_all | solution.py:104
  59.4 53.5 %all-reduce = (f32[128,64]{0,1:T(8,128)S(1)}, f32[16,128]{1,0:T(8,128)S(1)}) all-reduce(f32[128,64]{0,1:T(8,128)S(1)} %convolution_bitcast_fusion.2, f32[16,128]{1,0:T(8,128)S(1)} %convolution_bitcast_fusion.3), channel_id=1, replica_groups=mesh['grp'=2,'row'=16] {'row'}, use_global_device_ids=true, to_apply=%region_8.0 | all-reduce | flops 10240 | bytes 81920 | tf_op jit(solution)/shard_map/psum | solution.py:128
  112.9 0.6 broadcast_multiply_fusion.1
  113.5 0.3 fusion.69
  113.8 0.8 fusion.17
  114.6 0.6 broadcast_multiply_fusion.2
  115.2 27.9 %all-reduce.3.cloned.1.call-done = f32[128,128]{1,0:T(8,128)} async-done(((f32[128,128]{1,0:T(8,128)}), f32[128,128]{1,0:T(8,128)}) %all-reduce.3.cloned.1.call-update) | async-done | bytes 65552 | tf_op jit(solution)/shard_map/psum | solution.py:128
  143.1 1.5 broadcast_multiply_fusion
  (55 shorter events, 3.5 us)
Async XLA Ops:
  7.2 21.0 %copy-start = (bf16[128,128]{1,0:T(8,128)(2,1)S(1)}, bf16[128,128]{1,0:T(8,128)(2,1)}, u32[]{:S(2)}) copy-start(bf16[128,128]{1,0:T(8,128)(2,1)} %param.15) | copy-start | bytes 98308
  7.2 1.6 %copy-start.1 = (bf16[3,48,128]{2,1,0:T(8,128)(2,1)S(1)}, bf16[3,48,128]{2,1,0:T(8,128)(2,1)}, u32[]{:S(2)}) copy-start(bf16[3,48,128]{2,1,0:T(8,128)(2,1)} %param.10) | copy-start | bytes 110596
  8.8 0.7 copy-start.3
  9.0 0.7 copy-start.7
  9.0 0.7 copy-start.8
  24.1 10.0 %all-to-all-start.1 = ((bf16[1,48,48]{2,0,1:T(2,128)(2,1)}), bf16[1,48,48]{2,0,1:T(2,128)(2,1)S(1)}, u32[]{:S(2)}, u32[]{:S(2)}) async-start(bf16[1,48,48]{2,0,1:T(2,128)(2,1)} %copy.48), calls=%async_computation.1 | async-start | bytes 49152 | tf_op jit(solution)/shard_map/all_to_all | solution.py:64
  34.2 0.8 copy-start.2
  34.3 0.7 copy-start.5
  34.3 0.7 copy-start.4
  35.2 0.7 copy-start.6
  37.4 10.0 %all-to-all-start.2 = ((bf16[16,3,48]{2,1,0:T(4,128)(2,1)}), bf16[16,3,48]{2,1,0:T(4,128)(2,1)S(1)}, u32[]{:S(2)}, u32[]{:S(2)}) async-start(bf16[16,3,48]{2,1,0:T(4,128)(2,1)} %copy.50), calls=%async_computation.2 | async-start | bytes 32768 | tf_op jit(solution)/shard_map/all_to_all | solution.py:97
  48.4 10.0 %all-to-all-start.3 = ((bf16[16,2,144]{2,1,0:T(2,128)(2,1)}), bf16[16,2,144]{2,1,0:T(2,128)(2,1)S(1)}, u32[]{:S(2)}, u32[]{:S(2)}) async-start(bf16[16,2,144]{2,1,0:T(2,128)(2,1)} %reshape.188), calls=%async_computation.3 | async-start | bytes 32768 | tf_op jit(solution)/shard_map/all_to_all | solution.py:104
  52.5 90.6 %all-reduce.3.cloned.1.call-start = ((), (), s32[]{:S(2)}) async-start(), calls=%async_computation.4 | async-start | bytes 131072 | tf_op jit(solution)/shard_map/psum | solution.py:128
Sparse Core Ops, SparseCore 0:
  57.3 85.7 all-reduce.2
where the time goes:
time: 153 us; the launch traced here: 151 us
  blocking collectives  66.5 us (43%)
  waiting for transfers between devices  44.3 us (29%)
  between operations  15 us (10%)
  starting transfers between devices  12.2 us (8%)
  other arithmetic  5.19 us (3%)
  local copies, waits for them, and re-layouts  4.61 us (3%)
  matrix products  3.66 us (2%)
    psum x1, blocking collectives, body(): totals = lax.psum((project_part, gate_part, output_terms), 'row')  53.5 us
    psum x1, waiting for transfers between devices, body(): totals = lax.psum((project_part, gate_part, output_terms), 'row')  27.9 us
    all_to_all x1, blocking collectives, body(): lax.all_to_all(stacked, 'row', split_axis=0, concat_axis=2, tiled=True)  13 us
    all_to_all x1, waiting for transfers between devices, body(): lax.all_to_all(products, 'row', split_axis=1, concat_axis=0, tiled=True)  5.71 us
    all_to_all x1, waiting for transfers between devices, body(): lax.all_to_all(jnp.stack([left_col_grad, right_col_grad], axis=1), 'row',...  5.19 us
    all_to_all x1, waiting for transfers between devices, body(): lax.all_to_all(triangle_gradient, 'row', split_axis=0, concat_axis=1, til...  5 us
    all_to_all x1, starting transfers between devices, body(): lax.all_to_all(triangle_gradient, 'row', split_axis=0, concat_axis=1, til...  4.07 us
    all_to_all x1, starting transfers between devices, body(): lax.all_to_all(products, 'row', split_axis=1, concat_axis=0, tiled=True)  4.04 us
  transfers between devices with their start and end apart: 4, of which 4 were waited for; matrix products, arithmetic and copies ran while one was open for 3% of the time, Pallas kernels for 0%

commit v1 on v0

--- a/solution.py
+++ b/solution.py
@@ -1,7 +1,276 @@
+import functools
+
 import jax
 import jax.numpy as jnp
 from jax import lax
+from jax.experimental import pallas as pl
+from jax.experimental.pallas import tpu as pltpu
 from jax.sharding import PartitionSpec as P
+
+LANES = 128
+WHOLE_BYTES = 4 << 20
+
+NN = (((1,), (0,)), ((), ()))
+NT = (((1,), (1,)), ((), ()))
+TN = (((0,), (0,)), ((), ()))
+
+
+def dot(a, b, dims=NN):
+    return lax.dot_general(a, b, dims, preferred_element_type=jnp.float32)
+
+
+def dot_split(a, b):
+    high = a.astype(jnp.bfloat16)
+    low = (a - high.astype(jnp.float32)).astype(jnp.bfloat16)
+    return dot(high, b) + dot(low, b)
+
+
+def iota(shape, dim):
+    return lax.broadcasted_iota(jnp.int32, shape, dim)
+
+
+def zero_one(condition):
+    return jnp.where(condition, 1.0, 0.0).astype(jnp.bfloat16)
+
+
+def sigmoid(v):
+    return 1.0 / (1.0 + jnp.exp(-v))
+
+
+def normalize(v, axis=-1):
+    centered = v - jnp.mean(v, axis=axis, keepdims=True)
+    s = lax.rsqrt(jnp.mean(centered * centered, axis=axis, keepdims=True) + 1e-05)
+    return centered * s, s
+
+
+def crop_kernel(
+    n,
+    hidden,
+    mine_ref,
+    other_ref,
+    own_ref,
+    count_ref,
+    gain_ref,
+    bias_ref,
+    project_ref,
+    gate_ref,
+    out_gain_ref,
+    out_bias_ref,
+    out_weight_ref,
+    update_ref,
+    pair_ref,
+    project_grad_ref,
+    gate_grad_ref,
+    out_grad_ref,
+    zn_ref,
+    ug_ref,
+    upd_ref,
+    dgo_ref,
+    dp_ref,
+    dpt_ref,
+):
+    f32, bf16 = jnp.float32, jnp.bfloat16
+    per = LANES // hidden
+    groups = n // per
+    wide = n * hidden
+    me = lax.axis_index("row")
+    parity = lax.rem(me, 2)
+    blocks = 2 * mine_ref.shape[0]
+    rows = n // blocks
+    half = rows * n
+    count = count_ref[0]
+    gain, bias = gain_ref[...], bias_ref[...]
+
+    for block in range(blocks):
+        swap = parity != block % 2
+        for r in range(rows):
+            i = block * rows + r
+            g, p = i // per, i % per
+            here, there = pl.ds(r * n, n), pl.ds(half + r * n, n)
+            v = jnp.where(swap, other_ref[block // 2, here, :], mine_ref[block // 2, here, :])
+            zhat, _ = normalize(v.astype(f32))
+            zn_ref[p, pl.ds(g * n, n), :] = (zhat * gain + bias).astype(bf16)
+            ug_ref[p, pl.ds(g * n, n), :] = jnp.where(
+                swap, other_ref[block // 2, there, :], mine_ref[block // 2, there, :]
+            )
+
+    kinds = 4 * LANES
+    a, b = iota((4 * hidden, kinds), 0), iota((4 * hidden, kinds), 1)
+    spread = zero_one((a // hidden == b // LANES) & (a % hidden == b % hidden))
+    tiled = dot(project_ref[...], spread).astype(bf16)
+    place = (iota((LANES, kinds), 1) % LANES) // hidden
+    projected = jnp.zeros((groups * n, kinds), f32)
+    for p in range(per):
+        projected += dot(zn_ref[p], jnp.where(place == p, tiled, jnp.zeros_like(tiled)))
+    row_k = jnp.concatenate([iota((n, LANES), 0)] * groups, axis=0)
+    row_g = jnp.concatenate([jnp.full((n, LANES), g * per, jnp.int32) for g in range(groups)], axis=0)
+    row_i = row_g + iota((groups * n, LANES), 1) // hidden
+    mask = jnp.where((row_i < count) & (row_k < count), 1.0, 0.0)
+    value_left, value_right = projected[:, :LANES], projected[:, 2 * LANES : 3 * LANES]
+    gate_left = sigmoid(projected[:, LANES : 2 * LANES])
+    gate_right = sigmoid(projected[:, 3 * LANES :])
+    mask_left, mask_right = mask * gate_left, mask * gate_right
+
+    def lanes(flat):
+        return jnp.concatenate([flat[g * n : (g + 1) * n] for g in range(groups)], axis=1)
+
+    def flatten(rowed):
+        return jnp.concatenate([rowed[:, g * LANES : (g + 1) * LANES] for g in range(groups)], axis=0)
+
+    left = lanes((mask_left * value_left).astype(bf16))
+    right = lanes((mask_right * value_right).astype(bf16))
+
+    same = iota((LANES, wide), 0) % hidden == iota((LANES, wide), 1) % hidden
+    pick = zero_one(iota((per, LANES), 0) == iota((per, LANES), 1) // hidden)
+    parts = []
+    for g in range(groups):
+        cross = dot(right[:, g * LANES : (g + 1) * LANES], left, TN).astype(bf16)
+        parts.append(dot(pick, jnp.where(same, cross, jnp.zeros_like(cross))))
+    x = flatten(jnp.concatenate(parts, axis=0))
+
+    mean = jnp.where(iota((LANES, LANES), 0) // hidden == iota((LANES, LANES), 1) // hidden, 1.0 / hidden, 0.0)
+    mean = mean.astype(bf16)
+    out_gain = jnp.concatenate([out_gain_ref[...]] * per, axis=1)
+    out_bias = jnp.concatenate([out_bias_ref[...]] * per, axis=1)
+    centered = x - dot(x.astype(bf16), mean)
+    xs = lax.rsqrt(dot_split(centered * centered, mean) + 1e-05)
+    xhat = centered * xs
+    xn = (xhat * out_gain + out_bias).astype(bf16)
+
+    out_weight = jnp.concatenate([out_weight_ref[...]] * per, axis=0)
+    at = iota((LANES, LANES), 0) // hidden
+    gate_weight = gate_ref[...]
+    gate_grad = jnp.zeros((LANES, LANES), f32)
+    out_grad = jnp.zeros((hidden, LANES), f32)
+    dxn = jnp.zeros((groups * n, LANES), f32)
+    for p in range(per):
+        zn = zn_ref[p]
+        weight = jnp.where(at == p, out_weight, jnp.zeros_like(out_weight))
+        y = dot(xn, weight)
+        go = sigmoid(dot(zn, gate_weight))
+        upd_ref[p] = (go * y).astype(bf16)
+        cotangent = ug_ref[p].astype(f32)
+        dy = (cotangent * go).astype(bf16)
+        dgo = (cotangent * y * go * (1.0 - go)).astype(bf16)
+        dgo_ref[p] = dgo
+        gate_grad += dot(zn, dgo, TN)
+        out_grad += dot(xn, dy, TN)[p * hidden : (p + 1) * hidden]
+        dxn += dot(dy, weight, NT)
+    gate_grad_ref[...] = gate_grad / n
+    out_grad_ref[...] = out_grad / n
+
+    u = out_gain * dxn
+    dx = xs * (u - dot_split(u, mean) - xhat * dot_split(u * xhat, mean))
+    dx = lanes(dx.astype(bf16))
+
+    repeat = zero_one(iota((LANES, per), 0) // hidden == iota((LANES, per), 1))
+    dleft = jnp.zeros((n, wide), f32)
+    dright = []
+    for g in range(groups):
+        spread_dx = dot(repeat, dx[g * per : (g + 1) * per]).astype(bf16)
+        diagonal = jnp.where(same, spread_dx, jnp.zeros_like(spread_dx))
+        dleft += dot(right[:, g * LANES : (g + 1) * LANES], diagonal)
+        dright.append(dot(left, diagonal, NT))
+    dleft = flatten(dleft.astype(bf16)).astype(f32)
+    dright = jnp.concatenate(dright, axis=0).astype(bf16).astype(f32)
+    dp = [
+        dleft * mask_left,
+        dleft * mask_left * value_left * (1.0 - gate_left),
+        dright * mask_right,
+        dright * mask_right * value_right * (1.0 - gate_right),
+    ]
+    dp = jnp.concatenate([d.astype(bf16) for d in dp], axis=1)
+    dp_ref[...] = dp
+    dpt_ref[...] = dp.T
+    project_grad = jnp.zeros((4 * hidden, LANES), f32)
+    for p in range(per):
+        at_p = [dpt_ref[pl.ds(kind * LANES + p * hidden, hidden), :] for kind in range(4)]
+        project_grad += dot(jnp.concatenate(at_p, axis=0), zn_ref[p])
+    project_grad_ref[...] = project_grad.T / n
+
+    place = (iota((n, kinds), 1) % LANES) // hidden
+    for r in range(rows):
+        i = me * rows + r
+        g, p = lax.div(i, per), lax.rem(i, per)
+        where = pl.ds(pl.multiple_of(g * n, 16), n)
+        update_ref[r] = upd_ref[p, where, :]
+        dp_row = dp_ref[where, :]
+        dp_row = jnp.where(place == p, dp_row, jnp.zeros_like(dp_row))
+        dzn = dot(dp_row, tiled, NT) + dot(dgo_ref[p, where, :], gate_weight, NT)
+        zhat, zs = normalize(own_ref[r].astype(f32))
+        u = gain * dzn
+        first = jnp.mean(u, axis=-1, keepdims=True)
+        second = jnp.mean(u * zhat, axis=-1, keepdims=True)
+        pair_ref[r] = zs * (u - first - zhat * second)
+
+
+def body_whole(
+    devices,
+    pair_acts,
+    token_count,
+    input_gain,
+    input_bias,
+    project_weight,
+    gate_weight,
+    output_norm_gain,
+    output_shift_bias,
+    output_weight,
+    update_grad,
+):
+    rows, n, channels = pair_acts.shape
+    hidden = output_weight.shape[0]
+    half = rows * n
+    chips = devices // 2
+    send = jnp.concatenate(
+        [pair_acts.reshape(half, channels), update_grad.reshape(half, channels)], axis=0
+    )
+    send = jnp.broadcast_to(send[None], (chips,) + send.shape)
+    mine = lax.all_to_all(
+        send,
+        "row",
+        split_axis=0,
+        concat_axis=0,
+        tiled=True,
+        axis_index_groups=[[2 * chip + core for chip in range(chips)] for core in range(2)],
+    )
+    other = lax.ppermute(mine, "row", [(i, i ^ 1) for i in range(devices)])
+    per = LANES // hidden
+    tall = n // per * n
+    f32, bf16 = jnp.float32, jnp.bfloat16
+    vmem = pl.BlockSpec(memory_space=pltpu.VMEM)
+    return pl.pallas_call(
+        functools.partial(crop_kernel, n, hidden),
+        out_shape=(
+            jax.ShapeDtypeStruct((rows, n, channels), bf16),
+            jax.ShapeDtypeStruct((rows, n, channels), f32),
+            jax.ShapeDtypeStruct((channels, 4 * hidden), f32),
+            jax.ShapeDtypeStruct((channels, channels), f32),
+            jax.ShapeDtypeStruct((hidden, channels), f32),
+        ),
+        in_specs=[vmem] * 3 + [pl.BlockSpec(memory_space=pltpu.SMEM)] + [vmem] * 7,
+        out_specs=(vmem,) * 5,
+        scratch_shapes=[
+            pltpu.VMEM((per, tall, channels), bf16),
+            pltpu.VMEM((per, tall, channels), bf16),
+            pltpu.VMEM((per, tall, channels), bf16),
+            pltpu.VMEM((per, tall, channels), bf16),
+            pltpu.VMEM((tall, 4 * LANES), bf16),
+            pltpu.VMEM((4 * LANES, tall), bf16),
+        ],
+        compiler_params=pltpu.CompilerParams(vmem_limit_bytes=32 << 20),
+    )(
+        mine,
+        other,
+        pair_acts,
+        token_count,
+        input_gain[None],
+        input_bias[None],
+        project_weight,
+        gate_weight,
+        output_norm_gain[None],
+        output_shift_bias[None],
+        output_weight,
+    )
 
 
 def layer_normalize(values, norm_gain, norm_bias, reduce_axis):
@@ -138,6 +407,24 @@
     return (update, pair_grad, project_grad, gate_grad, output_grad)
 
 
+def fits_whole(mesh, args):
+    pair_acts, output_weight = args[0], args[8]
+    devices = mesh.shape["row"]
+    length, channels = pair_acts.shape[0] // mesh.shape["grp"], pair_acts.shape[2]
+    hidden = output_weight.shape[0]
+    return (
+        channels == LANES
+        and hidden % 16 == 0
+        and LANES % hidden == 0
+        and length % (LANES // hidden) == 0
+        and (LANES // hidden) % 8 == 0
+        and length % 16 == 0
+        and devices % 2 == 0
+        and length % devices == 0
+        and 2 * pair_acts.dtype.itemsize * length * length * channels <= WHOLE_BYTES
+    )
+
+
 def solution(mesh):
     in_specs = (
         P(("grp", "row"), None, None),
@@ -158,4 +445,10 @@
         P("grp", None),
         P("grp", None),
     )
-    return jax.shard_map(body, mesh=mesh, in_specs=in_specs, out_specs=out_specs, check_vma=False)
+    devices = mesh.shape["row"]
+
+    def run(*args):
+        crop = functools.partial(body_whole, devices) if fits_whole(mesh, args) else body
+        return jax.shard_map(crop, mesh=mesh, in_specs=in_specs, out_specs=out_specs, check_vma=False)(*args)
+
+    return run

time: 153 us -> 37.1 us (0.24)
  blocking collectives: 66.5 us -> 21.9 us
  waiting for transfers between devices: 44.3 us -> 0.83 us
  between operations: 15 us -> 1.36 us
  starting transfers between devices: 12.2 us -> 1.83 us
  Pallas kernels: 0 us -> 8.23 us
  other arithmetic: 5.19 us -> 0.79 us
  matrix products: 3.66 us -> 0 us
  local copies, waits for them, and re-layouts: 4.61 us -> 1.57 us
    psum x1 -> x0, blocking collectives: 53.5 us -> none  [body(): totals = lax.psum((project_part, gate_part, output_terms), 'row')]
    psum x1 -> x0, waiting for transfers between devices: 27.9 us -> none  [body(): totals = lax.psum((project_part, gate_part, output_terms), 'row')]
    all_to_all x3 -> x0, waiting for transfers between devices: 15.9 us -> none  [the longest x1 5.71 us: body(): lax.all_to_all(products, 'row', split_axis=1, concat_axis=0, tiled=True)]
    all_to_all x3 -> x0, starting transfers between devices: 12.1 us -> none  [the longest x1 4.07 us: body(): lax.all_to_all(triangle_gradient, 'row', split_axis=0, concat_axis=1, til...]
    all_to_all x1, blocking collectives: 13 us -> 21.9 us  [body_whole(): lax.all_to_all(send, 'row', split_axis=0, concat_axis=0, tiled=True, axis...]
    pallas_call x0 -> x1, Pallas kernels: none -> 8.23 us  [body_whole(): pl.pallas_call(functools.partial(crop_kernel, n, hidden), out_shape=(jax....]
    dot_general x12 -> x0, matrix products: 3.66 us -> none  [the longest x1 0.92 us: body(): jnp.einsum('rkd,rke->de', normed_pair, gate_logit_grad, preferred_element...]
    div x8 -> x0, other arithmetic: 2.72 us -> none  [the longest x1 1.47 us: body(): gate_grad = totals[1] / length]
  transfers between devices with their start and end apart: 4 -> 1, of which waited for: 4 -> 1; matrix products, arithmetic and copies ran while one was open for 3% -> 0% of each run, Pallas kernels for 0% -> 0%
where the time goes in v1:
time: 37.1 us; the launch traced here: 36.5 us
  blocking collectives  21.9 us (59%)
  Pallas kernels  8.23 us (22%)
  starting transfers between devices  1.83 us (5%)
  local copies, waits for them, and re-layouts  1.57 us (4%)
  between operations  1.36 us (4%)
  waiting for transfers between devices  0.83 us (2%)
  other arithmetic  0.79 us (2%)
    all_to_all x1, blocking collectives, body_whole(): lax.all_to_all(send, 'row', split_axis=0, concat_axis=0, tiled=True, axis...  21.9 us
    pallas_call x1, Pallas kernels, body_whole(): pl.pallas_call(functools.partial(crop_kernel, n, hidden), out_shape=(jax....  8.23 us
    ppermute x1, starting transfers between devices, body_whole(): other = lax.ppermute(mine, 'row', [(i, i ^ 1) for i in range(devices)])  1.83 us
    ppermute x1, waiting for transfers between devices, body_whole(): other = lax.ppermute(mine, 'row', [(i, i ^ 1) for i in range(devices)])  0.83 us
    concatenate x1, other arithmetic, body_whole(): jnp.concatenate([pair_acts.reshape(half, channels), update_grad.reshape(h...  0.79 us
    unnamed x17, local copies, waits for them, and re-layouts  0.79 us
  transfers between devices with their start and end apart: 1, of which 1 were waited for; matrix products, arithmetic and copies ran while one was open for 0% of the time, Pallas kernels for 0%

profile of v1, /device:TPU:1, one launch (start us, length us, event | category | flops | bytes accessed | tf_op | source)
XLA Modules:
  0.0 36.5 jit_solution(17246148596636673815)
XLA Ops:
  0.6 0.8 %pad_maximum_fusion = bf16[288,128]{1,0:T(8,128)(2,1)S(1)} fusion(bf16[144,128]{1,0:T(8,128)(2,1)} %bitcast.11, bf16[144,128]{1,0:T(8,128)(2,1)} %bitcast.6), kind=kLoop, calls=%fused_computation | loop fusion | flops 147456 | bytes 147456 | tf_op jit(solution)/shard_map/concatenate | solution.py:224
  1.4 0.1 broadcast_in_dim.18
  1.5 0.0 copy-start.7
  1.5 0.0 copy-start.1
  1.5 21.9 %all_to_all.5.mine_ref = bf16[8,288,128]{2,1,0:T(8,128)(2,1)S(1)} all-to-all(bf16[8,288,128]{2,1,0:T(8,128)(2,1)S(1)} %broadcast_in_dim.18), channel_id=1, replica_groups={{0,2,4,6,8,10,12,14},{1,3,5,7,9,11,13,15},{16,18,20,22,24,26,28,30},{17..., dimensions={0} | all-to-all | bytes 1179648 | tf_op jit(solution)/shard_map/all_to_all | solution.py:228
  23.4 0.0 copy-start
  23.4 1.8 %collective-permute-start = (bf16[8,288,128]{2,1,0:T(8,128)(2,1)S(1)}, bf16[8,288,128]{2,1,0:T(8,128)(2,1)S(1)}, u32[]{:S(2)}, u32[]{:S(2)}) collective-permute-start(bf16[8,288,128]{2,1,0:T(8,128)(2,1)S(1)} %all_to_all.5.mine_ref), channel_id=1, source_target_pairs={{0,1},{1,0},{2,3},{3,2},{4,5},{5,4},{6,7},{7,6},{8,9},{9,8},{10,11... | collective-permute-start | bytes 1769480 | tf_op jit(solution)/shard_map/ppermute | solution.py:236
  25.9 0.0 copy-done.7
  25.9 0.0 copy-start.6
  25.9 0.1 copy.15.project_ref
  26.0 0.0 copy-start.2
  26.0 0.8 %collective-permute-done.other_ref = bf16[8,288,128]{2,1,0:T(8,128)(2,1)S(1)} collective-permute-done((bf16[8,288,128]{2,1,0:T(8,128)(2,1)S(1)}, bf16[8,288,128]{2,1,0:T(8,128)(2,1)S(1)}, u32[]{:S(2)}, u32[]{:S(2)}) %collective-permute-start) | collective-permute-done | bytes 589856 | tf_op jit(solution)/shard_map/ppermute | solution.py:236
  26.8 0.0 copy-start.3
  26.8 0.0 copy-start.4
  26.8 0.0 copy-start.5
  26.8 0.0 copy-done.1
  26.9 0.0 copy-done
  26.9 0.0 copy-done.6
  26.9 0.0 copy-done.2
  26.9 0.6 %copy-done.3 = f32[128]{0:T(128)S(1)} copy-done((f32[128]{0:T(128)S(1)}, f32[128]{0:T(128)}, u32[]{:S(2)}) %copy-start.3) | copy-done | bytes 536
  27.5 0.0 copy-done.4
  27.5 0.0 copy-done.5
  27.5 8.2 %shard_map.137 = (bf16[3,48,128]{2,1,0:T(8,128)(2,1)}, f32[3,48,128]{2,1,0:T(8,128)}, f32[128,64]{1,0:T(8,128)S(1)}, f32[128,128]{1,0:T(8,128)}, f32[16,128]{1,0:T(8,128)}) custom-call(bf16[8,288,128]{2,1,0:T(8,128)(2,1)S(1)} %all_to_all.5.mine_ref, bf16[8,288,128]{2,1,0:T(8,128)(2,1)S(1)} %collective-permute-done.other_ref, ...), custom_call_target="tpu_custom_call" | custom-call | tf_op jit(solution)/shard_map/pallas_call | solution.py:241
  35.8 0.7 %copy.16 = f32[128,64]{0,1:T(8,128)} copy(f32[128,64]{1,0:T(8,128)S(1)} %get-tuple-element.7) | data formatting | bytes 65536 | tf_op jit(solution)/shard_map/pallas_call | solution.py:241
Async XLA Ops:
  1.5 24.4 %copy-start.7 = (bf16[128,64]{0,1:T(8,128)(2,1)S(1)}, bf16[128,64]{0,1:T(8,128)(2,1)}, u32[]{:S(2)}) copy-start(bf16[128,64]{0,1:T(8,128)(2,1)} %param.14) | copy-start | bytes 49156
  1.5 25.3 %copy-start.1 = (bf16[128,128]{1,0:T(8,128)(2,1)S(1)}, bf16[128,128]{1,0:T(8,128)(2,1)}, u32[]{:S(2)}) copy-start(bf16[128,128]{1,0:T(8,128)(2,1)} %gate_ref.1) | copy-start | bytes 98308
  23.4 3.5 %copy-start = (bf16[3,48,128]{2,1,0:T(8,128)(2,1)S(1)}, bf16[3,48,128]{2,1,0:T(8,128)(2,1)}, u32[]{:S(2)}) copy-start(bf16[3,48,128]{2,1,0:T(8,128)(2,1)} %own_ref.1) | copy-start | bytes 110596
  23.4 3.5 %collective-permute-start = (bf16[8,288,128]{2,1,0:T(8,128)(2,1)S(1)}, bf16[8,288,128]{2,1,0:T(8,128)(2,1)S(1)}, u32[]{:S(2)}, u32[]{:S(2)}) collective-permute-start(bf16[8,288,128]{2,1,0:T(8,128)(2,1)S(1)} %all_to_all.5.mine_ref), channel_id=1, source_target_pairs={{0,1},{1,0},{2,3},{3,2},{4,5},{5,4},{6,7},{7,6},{8,9},{9,8},{10,11... | collective-permute-start | bytes 1769480 | tf_op jit(solution)/shard_map/ppermute | solution.py:236
  25.9 1.0 %copy-start.6 = (f32[16]{0:T(128)S(1)}, f32[16]{0:T(128)}, u32[]{:S(2)}) copy-start(f32[16]{0:T(128)} %param.17) | copy-start | bytes 196
  26.0 0.9 %copy-start.2 = (bf16[16,128]{1,0:T(8,128)(2,1)S(1)}, bf16[16,128]{1,0:T(8,128)(2,1)}, u32[]{:S(2)}) copy-start(bf16[16,128]{1,0:T(8,128)(2,1)} %out_weight_ref.1) | copy-start | bytes 12292
  26.8 0.7 %copy-start.3 = (f32[128]{0:T(128)S(1)}, f32[128]{0:T(128)}, u32[]{:S(2)}) copy-start(f32[128]{0:T(128)} %param.12) | copy-start | bytes 1540
  26.8 0.7 %copy-start.4 = (f32[128]{0:T(128)S(1)}, f32[128]{0:T(128)}, u32[]{:S(2)}) copy-start(f32[128]{0:T(128)} %param.13) | copy-start | bytes 1540
  26.8 0.7 %copy-start.5 = (f32[16]{0:T(128)S(1)}, f32[16]{0:T(128)}, u32[]{:S(2)}) copy-start(f32[16]{0:T(128)} %param.16) | copy-start | bytes 196

commit v2 on v1

--- a/solution.py
+++ b/solution.py
@@ -46,53 +46,31 @@
 def crop_kernel(
     n,
     hidden,
-    mine_ref,
-    other_ref,
-    own_ref,
-    count_ref,
-    gain_ref,
-    bias_ref,
-    project_ref,
-    gate_ref,
-    out_gain_ref,
-    out_bias_ref,
-    out_weight_ref,
-    update_ref,
-    pair_ref,
-    project_grad_ref,
-    gate_grad_ref,
-    out_grad_ref,
-    zn_ref,
-    ug_ref,
-    upd_ref,
-    dgo_ref,
-    dp_ref,
-    dpt_ref,
+    blocks,
+    *refs,
 ):
+    block_refs, refs = refs[:blocks], refs[blocks:]
+    count_ref, gain_ref, bias_ref, project_ref, gate_ref = refs[:5]
+    out_gain_ref, out_bias_ref, out_weight_ref = refs[5:8]
+    update_ref, pair_ref, project_grad_ref, gate_grad_ref, out_grad_ref = refs[8:13]
+    zn_ref, ug_ref, upd_ref, dgo_ref, dp_ref, dpt_ref = refs[13:]
     f32, bf16 = jnp.float32, jnp.bfloat16
     per = LANES // hidden
     groups = n // per
     wide = n * hidden
     me = lax.axis_index("row")
-    parity = lax.rem(me, 2)
-    blocks = 2 * mine_ref.shape[0]
     rows = n // blocks
     half = rows * n
     count = count_ref[0]
     gain, bias = gain_ref[...], bias_ref[...]
 
-    for block in range(blocks):
-        swap = parity != block % 2
+    for d, block_ref in enumerate(block_refs):
         for r in range(rows):
-            i = block * rows + r
-            g, p = i // per, i % per
-            here, there = pl.ds(r * n, n), pl.ds(half + r * n, n)
-            v = jnp.where(swap, other_ref[block // 2, here, :], mine_ref[block // 2, here, :])
-            zhat, _ = normalize(v.astype(f32))
-            zn_ref[p, pl.ds(g * n, n), :] = (zhat * gain + bias).astype(bf16)
-            ug_ref[p, pl.ds(g * n, n), :] = jnp.where(
-                swap, other_ref[block // 2, there, :], mine_ref[block // 2, there, :]
-            )
+            i = (me ^ d) * rows + r
+            p, where = lax.rem(i, per), pl.ds(pl.multiple_of(lax.div(i, per) * n, 16), n)
+            zhat, _ = normalize(block_ref[pl.ds(r * n, n), :].astype(f32))
+            zn_ref[p, where, :] = (zhat * gain + bias).astype(bf16)
+            ug_ref[p, where, :] = block_ref[pl.ds(half + r * n, n), :]
 
     kinds = 4 * LANES
     a, b = iota((4 * hidden, kinds), 0), iota((4 * hidden, kinds), 1)
@@ -197,7 +175,7 @@
         dp_row = dp_ref[where, :]
         dp_row = jnp.where(place == p, dp_row, jnp.zeros_like(dp_row))
         dzn = dot(dp_row, tiled, NT) + dot(dgo_ref[p, where, :], gate_weight, NT)
-        zhat, zs = normalize(own_ref[r].astype(f32))
+        zhat, zs = normalize(block_refs[0][pl.ds(r * n, n), :].astype(f32))
         u = gain * dzn
         first = jnp.mean(u, axis=-1, keepdims=True)
         second = jnp.mean(u * zhat, axis=-1, keepdims=True)
@@ -220,26 +198,21 @@
     rows, n, channels = pair_acts.shape
     hidden = output_weight.shape[0]
     half = rows * n
-    chips = devices // 2
     send = jnp.concatenate(
         [pair_acts.reshape(half, channels), update_grad.reshape(half, channels)], axis=0
     )
-    send = jnp.broadcast_to(send[None], (chips,) + send.shape)
-    mine = lax.all_to_all(
-        send,
-        "row",
-        split_axis=0,
-        concat_axis=0,
-        tiled=True,
-        axis_index_groups=[[2 * chip + core for chip in range(chips)] for core in range(2)],
-    )
-    other = lax.ppermute(mine, "row", [(i, i ^ 1) for i in range(devices)])
+    blocks = {0: send}
+    step = devices // 2
+    while step:
+        pairs = [(i, i ^ step) for i in range(devices)]
+        blocks.update({d ^ step: lax.ppermute(blocks[d], "row", pairs) for d in list(blocks)})
+        step //= 2
     per = LANES // hidden
     tall = n // per * n
     f32, bf16 = jnp.float32, jnp.bfloat16
     vmem = pl.BlockSpec(memory_space=pltpu.VMEM)
     return pl.pallas_call(
-        functools.partial(crop_kernel, n, hidden),
+        functools.partial(crop_kernel, n, hidden, devices),
         out_shape=(
             jax.ShapeDtypeStruct((rows, n, channels), bf16),
             jax.ShapeDtypeStruct((rows, n, channels), f32),
@@ -247,7 +220,7 @@
             jax.ShapeDtypeStruct((channels, channels), f32),
             jax.ShapeDtypeStruct((hidden, channels), f32),
         ),
-        in_specs=[vmem] * 3 + [pl.BlockSpec(memory_space=pltpu.SMEM)] + [vmem] * 7,
+        in_specs=[vmem] * devices + [pl.BlockSpec(memory_space=pltpu.SMEM)] + [vmem] * 7,
         out_specs=(vmem,) * 5,
         scratch_shapes=[
             pltpu.VMEM((per, tall, channels), bf16),
@@ -259,9 +232,7 @@
         ],
         compiler_params=pltpu.CompilerParams(vmem_limit_bytes=32 << 20),
     )(
-        mine,
-        other,
-        pair_acts,
+        *[blocks[d] for d in range(devices)],
         token_count,
         input_gain[None],
         input_bias[None],
@@ -419,7 +390,7 @@
         and length % (LANES // hidden) == 0
         and (LANES // hidden) % 8 == 0
         and length % 16 == 0
-        and devices % 2 == 0
+        and devices & (devices - 1) == 0
         and length % devices == 0
         and 2 * pair_acts.dtype.itemsize * length * length * channels <= WHOLE_BYTES
     )

time: 37.1 us -> 29.1 us (0.78)
  blocking collectives: 21.9 us -> 0 us
  starting transfers between devices: 1.83 us -> 15.9 us
    all_to_all x1 -> x0, blocking collectives: 21.9 us -> none  [body_whole(): lax.all_to_all(send, 'row', split_axis=0, concat_axis=0, tiled=True, axis...]
    ppermute x1 -> x15, starting transfers between devices: 1.83 us -> 15.9 us  [body_whole(): lax.ppermute(blocks[d], 'row', pairs)]
    unnamed x17 -> x15, local copies, waits for them, and re-layouts: 0.79 us -> 0.82 us
    ppermute x1 -> x15, waiting for transfers between devices: 0.83 us -> 0.82 us  [body_whole(): lax.ppermute(blocks[d], 'row', pairs)]
  transfers between devices with their start and end apart: 1 -> 15, of which waited for: 1 -> 3; matrix products, arithmetic and copies ran while one was open for 0% -> 0% of each run, Pallas kernels for 0% -> 0%
where the time goes in v2:
time: 29.1 us; the launch traced here: 28.5 us
  starting transfers between devices  15.9 us (55%)
  Pallas kernels  8.19 us (28%)
  local copies, waits for them, and re-layouts  1.52 us (5%)
  between operations  1.36 us (5%)
  waiting for transfers between devices  0.82 us (3%)
  other arithmetic  0.8 us (3%)
    ppermute x15, starting transfers between devices, body_whole(): lax.ppermute(blocks[d], 'row', pairs)  15.9 us
    pallas_call x1, Pallas kernels, body_whole(): pl.pallas_call(functools.partial(crop_kernel, n, hidden, devices), out_sh...  8.19 us
    unnamed x15, local copies, waits for them, and re-layouts  0.82 us
    ppermute x15, waiting for transfers between devices, body_whole(): lax.ppermute(blocks[d], 'row', pairs)  0.82 us
    concatenate x1, other arithmetic, body_whole(): jnp.concatenate([pair_acts.reshape(half, channels), update_grad.reshape(h...  0.8 us
    pallas_call x1, local copies, waits for them, and re-layouts, body_whole(): pl.pallas_call(functools.partial(crop_kernel, n, hidden, devices), out_sh...  0.7 us
  transfers between devices with their start and end apart: 15, of which 3 were waited for; matrix products, arithmetic and copies ran while one was open for 0% of the time, Pallas kernels for 0%

profile of v2, /device:TPU:1, one launch (start us, length us, event | category | flops | bytes accessed | tf_op | source)
XLA Modules:
  0.0 28.5 jit_solution(10353320420895241340)
XLA Ops:
  0.6 0.8 %pad_maximum_fusion.refs_0_ = bf16[288,128]{1,0:T(8,128)(2,1)S(1)} fusion(bf16[144,128]{1,0:T(8,128)(2,1)} %bitcast.10, bf16[144,128]{1,0:T(8,128)(2,1)} %bitcast.11), kind=kLoop, calls=%fused_computation | loop fusion | flops 147456 | bytes 147456 | tf_op jit(solution)/shard_map/concatenate | solution.py:201
  1.4 3.2 %collective-permute-start.7 = (bf16[288,128]{1,0:T(8,128)(2,1)S(1)}, bf16[288,128]{1,0:T(8,128)(2,1)S(1)}, u32[]{:S(2)}, u32[]{:S(2)}) collective-permute-start(bf16[288,128]{1,0:T(8,128)(2,1)S(1)} %pad_maximum_fusion.refs_0_), channel_id=1, source_target_pairs={{0,8},{1,9},{2,10},{3,11},{4,12},{5,13},{6,14},{7,15},{8,0},{9,1},... | collective-permute-start | bytes 221192 | tf_op jit(solution)/shard_map/ppermute | solution.py:208
  4.6 1.3 %collective-permute-start.3 = (bf16[288,128]{1,0:T(8,128)(2,1)S(1)}, bf16[288,128]{1,0:T(8,128)(2,1)S(1)}, u32[]{:S(2)}, u32[]{:S(2)}) collective-permute-start(bf16[288,128]{1,0:T(8,128)(2,1)S(1)} %pad_maximum_fusion.refs_0_), channel_id=1, source_target_pairs={{0,4},{1,5},{2,6},{3,7},{4,0},{5,1},{6,2},{7,3},{8,12},{9,13},{10,... | collective-permute-start | bytes 221192 | tf_op jit(solution)/shard_map/ppermute | solution.py:208
  5.9 1.2 %collective-permute-start.1 = (bf16[288,128]{1,0:T(8,128)(2,1)S(1)}, bf16[288,128]{1,0:T(8,128)(2,1)S(1)}, u32[]{:S(2)}, u32[]{:S(2)}) collective-permute-start(bf16[288,128]{1,0:T(8,128)(2,1)S(1)} %pad_maximum_fusion.refs_0_), channel_id=1, source_target_pairs={{0,2},{1,3},{2,0},{3,1},{4,6},{5,7},{6,4},{7,5},{8,10},{9,11},{10,... | collective-permute-start | bytes 221192 | tf_op jit(solution)/shard_map/ppermute | solution.py:208
  7.1 1.5 %collective-permute-start = (bf16[288,128]{1,0:T(8,128)(2,1)S(1)}, bf16[288,128]{1,0:T(8,128)(2,1)S(1)}, u32[]{:S(2)}, u32[]{:S(2)}) collective-permute-start(bf16[288,128]{1,0:T(8,128)(2,1)S(1)} %pad_maximum_fusion.refs_0_), channel_id=1, source_target_pairs={{0,1},{1,0},{2,3},{3,2},{4,5},{5,4},{6,7},{7,6},{8,9},{9,8},{10,11... | collective-permute-start | bytes 221192 | tf_op jit(solution)/shard_map/ppermute | solution.py:208
  8.7 0.2 collective-permute-start.11
  8.9 1.2 %collective-permute-start.9 = (bf16[288,128]{1,0:T(8,128)(2,1)S(1)}, bf16[288,128]{1,0:T(8,128)(2,1)S(1)}, u32[]{:S(2)}, u32[]{:S(2)}) collective-permute-start(bf16[288,128]{1,0:T(8,128)(2,1)S(1)} %collective-permute-done.7.refs_8_), channel_id=1, source_target_pairs={{0,2},{1,3},{2,0},{3,1},{4,6},{5,7},{6,4},{7,5},{8,10},{9,11},{10,... | collective-permute-start | bytes 221192 | tf_op jit(solution)/shard_map/ppermute | solution.py:208
  10.1 1.7 %collective-permute-start.8 = (bf16[288,128]{1,0:T(8,128)(2,1)S(1)}, bf16[288,128]{1,0:T(8,128)(2,1)S(1)}, u32[]{:S(2)}, u32[]{:S(2)}) collective-permute-start(bf16[288,128]{1,0:T(8,128)(2,1)S(1)} %collective-permute-done.7.refs_8_), channel_id=1, source_target_pairs={{0,1},{1,0},{2,3},{3,2},{4,5},{5,4},{6,7},{7,6},{8,9},{9,8},{10,11... | collective-permute-start | bytes 221192 | tf_op jit(solution)/shard_map/ppermute | solution.py:208
  11.8 0.3 collective-permute-start.5
  12.0 1.0 %collective-permute-start.4 = (bf16[288,128]{1,0:T(8,128)(2,1)S(1)}, bf16[288,128]{1,0:T(8,128)(2,1)S(1)}, u32[]{:S(2)}, u32[]{:S(2)}) collective-permute-start(bf16[288,128]{1,0:T(8,128)(2,1)S(1)} %collective-permute-done.3.refs_4_), channel_id=1, source_target_pairs={{0,1},{1,0},{2,3},{3,2},{4,5},{5,4},{6,7},{7,6},{8,9},{9,8},{10,11... | collective-permute-start | bytes 221192 | tf_op jit(solution)/shard_map/ppermute | solution.py:208
  13.0 0.6 %collective-permute-start.13 = (bf16[288,128]{1,0:T(8,128)(2,1)S(1)}, bf16[288,128]{1,0:T(8,128)(2,1)S(1)}, u32[]{:S(2)}, u32[]{:S(2)}) collective-permute-start(bf16[288,128]{1,0:T(8,128)(2,1)S(1)} %collective-permute-done.11.refs_12_), channel_id=1, source_target_pairs={{0,2},{1,3},{2,0},{3,1},{4,6},{5,7},{6,4},{7,5},{8,10},{9,11},{10,... | collective-permute-start | bytes 221192 | tf_op jit(solution)/shard_map/ppermute | solution.py:208
  13.6 1.6 %collective-permute-start.2 = (bf16[288,128]{1,0:T(8,128)(2,1)S(1)}, bf16[288,128]{1,0:T(8,128)(2,1)S(1)}, u32[]{:S(2)}, u32[]{:S(2)}) collective-permute-start(bf16[288,128]{1,0:T(8,128)(2,1)S(1)} %collective-permute-done.1.refs_2_), channel_id=1, source_target_pairs={{0,1},{1,0},{2,3},{3,2},{4,5},{5,4},{6,7},{7,6},{8,9},{9,8},{10,11... | collective-permute-start | bytes 221192 | tf_op jit(solution)/shard_map/ppermute | solution.py:208
  15.2 0.1 collective-permute-start.12
  15.3 0.3 %collective-permute-done.5.refs_6_ = bf16[288,128]{1,0:T(8,128)(2,1)S(1)} collective-permute-done((bf16[288,128]{1,0:T(8,128)(2,1)S(1)}, bf16[288,128]{1,0:T(8,128)(2,1)S(1)}, u32[]{:S(2)}, u32[]{:S(2)}) %collective-permute-start.5) | collective-permute-done | bytes 73760 | tf_op jit(solution)/shard_map/ppermute | solution.py:208
  15.6 1.2 %collective-permute-start.10 = (bf16[288,128]{1,0:T(8,128)(2,1)S(1)}, bf16[288,128]{1,0:T(8,128)(2,1)S(1)}, u32[]{:S(2)}, u32[]{:S(2)}) collective-permute-start(bf16[288,128]{1,0:T(8,128)(2,1)S(1)} %collective-permute-done.9.refs_10_), channel_id=1, source_target_pairs={{0,1},{1,0},{2,3},{3,2},{4,5},{5,4},{6,7},{7,6},{8,9},{9,8},{10,11... | collective-permute-start | bytes 221192 | tf_op jit(solution)/shard_map/ppermute | solution.py:208
  16.8 0.4 %collective-permute-done.13.refs_14_ = bf16[288,128]{1,0:T(8,128)(2,1)S(1)} collective-permute-done((bf16[288,128]{1,0:T(8,128)(2,1)S(1)}, bf16[288,128]{1,0:T(8,128)(2,1)S(1)}, u32[]{:S(2)}, u32[]{:S(2)}) %collective-permute-start.13) | collective-permute-done | bytes 73760 | tf_op jit(solution)/shard_map/ppermute | solution.py:208
  17.2 0.8 %collective-permute-start.14 = (bf16[288,128]{1,0:T(8,128)(2,1)S(1)}, bf16[288,128]{1,0:T(8,128)(2,1)S(1)}, u32[]{:S(2)}, u32[]{:S(2)}) collective-permute-start(bf16[288,128]{1,0:T(8,128)(2,1)S(1)} %collective-permute-done.13.refs_14_), channel_id=1, source_target_pairs={{0,1},{1,0},{2,3},{3,2},{4,5},{5,4},{6,7},{7,6},{8,9},{9,8},{10,11... | collective-permute-start | bytes 221192 | tf_op jit(solution)/shard_map/ppermute | solution.py:208
  18.7 0.1 copy.15.refs_19_
  18.9 0.1 collective-permute-done.14.refs_15_
  19.0 0.5 %copy-done.1 = bf16[16,128]{1,0:T(8,128)(2,1)S(1)} copy-done((bf16[16,128]{1,0:T(8,128)(2,1)S(1)}, bf16[16,128]{1,0:T(8,128)(2,1)}, u32[]{:S(2)}) %copy-start.1) | copy-done | bytes 4120
  19.5 0.1 copy-done.5
  19.6 0.0 copy-done.2
  19.7 8.2 %shard_map.137 = (bf16[3,48,128]{2,1,0:T(8,128)(2,1)}, f32[3,48,128]{2,1,0:T(8,128)}, f32[128,64]{1,0:T(8,128)S(1)}, f32[128,128]{1,0:T(8,128)}, f32[16,128]{1,0:T(8,128)}) custom-call(bf16[288,128]{1,0:T(8,128)(2,1)S(1)} %pad_maximum_fusion.refs_0_, bf16[288,128]{1,0:T(8,128)(2,1)S(1)} %collective-permute-done.refs_1_, ...), custom_call_target="tpu_custom_call" | custom-call | tf_op jit(solution)/shard_map/pallas_call | solution.py:214
  27.8 0.7 %copy.16 = f32[128,64]{0,1:T(8,128)} copy(f32[128,64]{1,0:T(8,128)S(1)} %get-tuple-element.7) | data formatting | bytes 65536 | tf_op jit(solution)/shard_map/pallas_call | solution.py:214
  (24 shorter events, 0.1 us)
Async XLA Ops:
  0.6 18.1 %copy-start.6 = (bf16[128,64]{0,1:T(8,128)(2,1)S(1)}, bf16[128,64]{0,1:T(8,128)(2,1)}, u32[]{:S(2)}) copy-start(bf16[128,64]{0,1:T(8,128)(2,1)} %param.14) | copy-start | bytes 49156
  1.4 17.5 %copy-start = (bf16[128,128]{1,0:T(8,128)(2,1)S(1)}, bf16[128,128]{1,0:T(8,128)(2,1)}, u32[]{:S(2)}) copy-start(bf16[128,128]{1,0:T(8,128)(2,1)} %refs_20_.1) | copy-start | bytes 98308
  1.4 7.2 %collective-permute-start.7 = (bf16[288,128]{1,0:T(8,128)(2,1)S(1)}, bf16[288,128]{1,0:T(8,128)(2,1)S(1)}, u32[]{:S(2)}, u32[]{:S(2)}) collective-permute-start(bf16[288,128]{1,0:T(8,128)(2,1)S(1)} %pad_maximum_fusion.refs_0_), channel_id=1, source_target_pairs={{0,8},{1,9},{2,10},{3,11},{4,12},{5,13},{6,14},{7,15},{8,0},{9,1},... | collective-permute-start | bytes 221192 | tf_op jit(solution)/shard_map/ppermute | solution.py:208
  4.6 5.5 %collective-permute-start.3 = (bf16[288,128]{1,0:T(8,128)(2,1)S(1)}, bf16[288,128]{1,0:T(8,128)(2,1)S(1)}, u32[]{:S(2)}, u32[]{:S(2)}) collective-permute-start(bf16[288,128]{1,0:T(8,128)(2,1)S(1)} %pad_maximum_fusion.refs_0_), channel_id=1, source_target_pairs={{0,4},{1,5},{2,6},{3,7},{4,0},{5,1},{6,2},{7,3},{8,12},{9,13},{10,... | collective-permute-start | bytes 221192 | tf_op jit(solution)/shard_map/ppermute | solution.py:208
  5.9 5.8 %collective-permute-start.1 = (bf16[288,128]{1,0:T(8,128)(2,1)S(1)}, bf16[288,128]{1,0:T(8,128)(2,1)S(1)}, u32[]{:S(2)}, u32[]{:S(2)}) collective-permute-start(bf16[288,128]{1,0:T(8,128)(2,1)S(1)} %pad_maximum_fusion.refs_0_), channel_id=1, source_target_pairs={{0,2},{1,3},{2,0},{3,1},{4,6},{5,7},{6,4},{7,5},{8,10},{9,11},{10,... | collective-permute-start | bytes 221192 | tf_op jit(solution)/shard_map/ppermute | solution.py:208
  7.1 4.9 %collective-permute-start = (bf16[288,128]{1,0:T(8,128)(2,1)S(1)}, bf16[288,128]{1,0:T(8,128)(2,1)S(1)}, u32[]{:S(2)}, u32[]{:S(2)}) collective-permute-start(bf16[288,128]{1,0:T(8,128)(2,1)S(1)} %pad_maximum_fusion.refs_0_), channel_id=1, source_target_pairs={{0,1},{1,0},{2,3},{3,2},{4,5},{5,4},{6,7},{7,6},{8,9},{9,8},{10,11... | collective-permute-start | bytes 221192 | tf_op jit(solution)/shard_map/ppermute | solution.py:208
  8.7 4.4 %collective-permute-start.11 = (bf16[288,128]{1,0:T(8,128)(2,1)S(1)}, bf16[288,128]{1,0:T(8,128)(2,1)S(1)}, u32[]{:S(2)}, u32[]{:S(2)}) collective-permute-start(bf16[288,128]{1,0:T(8,128)(2,1)S(1)} %collective-permute-done.7.refs_8_), channel_id=1, source_target_pairs={{0,4},{1,5},{2,6},{3,7},{4,0},{5,1},{6,2},{7,3},{8,12},{9,13},{10,... | collective-permute-start | bytes 221192 | tf_op jit(solution)/shard_map/ppermute | solution.py:208
  8.9 4.7 %collective-permute-start.9 = (bf16[288,128]{1,0:T(8,128)(2,1)S(1)}, bf16[288,128]{1,0:T(8,128)(2,1)S(1)}, u32[]{:S(2)}, u32[]{:S(2)}) collective-permute-start(bf16[288,128]{1,0:T(8,128)(2,1)S(1)} %collective-permute-done.7.refs_8_), channel_id=1, source_target_pairs={{0,2},{1,3},{2,0},{3,1},{4,6},{5,7},{6,4},{7,5},{8,10},{9,11},{10,... | collective-permute-start | bytes 221192 | tf_op jit(solution)/shard_map/ppermute | solution.py:208
  10.1 5.1 %collective-permute-start.8 = (bf16[288,128]{1,0:T(8,128)(2,1)S(1)}, bf16[288,128]{1,0:T(8,128)(2,1)S(1)}, u32[]{:S(2)}, u32[]{:S(2)}) collective-permute-start(bf16[288,128]{1,0:T(8,128)(2,1)S(1)} %collective-permute-done.7.refs_8_), channel_id=1, source_target_pairs={{0,1},{1,0},{2,3},{3,2},{4,5},{5,4},{6,7},{7,6},{8,9},{9,8},{10,11... | collective-permute-start | bytes 221192 | tf_op jit(solution)/shard_map/ppermute | solution.py:208
  11.8 3.8 %collective-permute-start.5 = (bf16[288,128]{1,0:T(8,128)(2,1)S(1)}, bf16[288,128]{1,0:T(8,128)(2,1)S(1)}, u32[]{:S(2)}, u32[]{:S(2)}) collective-permute-start(bf16[288,128]{1,0:T(8,128)(2,1)S(1)} %collective-permute-done.3.refs_4_), channel_id=1, source_target_pairs={{0,2},{1,3},{2,0},{3,1},{4,6},{5,7},{6,4},{7,5},{8,10},{9,11},{10,... | collective-permute-start | bytes 221192 | tf_op jit(solution)/shard_map/ppermute | solution.py:208
  12.0 4.8 %collective-permute-start.4 = (bf16[288,128]{1,0:T(8,128)(2,1)S(1)}, bf16[288,128]{1,0:T(8,128)(2,1)S(1)}, u32[]{:S(2)}, u32[]{:S(2)}) collective-permute-start(bf16[288,128]{1,0:T(8,128)(2,1)S(1)} %collective-permute-done.3.refs_4_), channel_id=1, source_target_pairs={{0,1},{1,0},{2,3},{3,2},{4,5},{5,4},{6,7},{7,6},{8,9},{9,8},{10,11... | collective-permute-start | bytes 221192 | tf_op jit(solution)/shard_map/ppermute | solution.py:208
  13.0 4.2 %collective-permute-start.13 = (bf16[288,128]{1,0:T(8,128)(2,1)S(1)}, bf16[288,128]{1,0:T(8,128)(2,1)S(1)}, u32[]{:S(2)}, u32[]{:S(2)}) collective-permute-start(bf16[288,128]{1,0:T(8,128)(2,1)S(1)} %collective-permute-done.11.refs_12_), channel_id=1, source_target_pairs={{0,2},{1,3},{2,0},{3,1},{4,6},{5,7},{6,4},{7,5},{8,10},{9,11},{10,... | collective-permute-start | bytes 221192 | tf_op jit(solution)/shard_map/ppermute | solution.py:208
  13.6 5.2 %collective-permute-start.2 = (bf16[288,128]{1,0:T(8,128)(2,1)S(1)}, bf16[288,128]{1,0:T(8,128)(2,1)S(1)}, u32[]{:S(2)}, u32[]{:S(2)}) collective-permute-start(bf16[288,128]{1,0:T(8,128)(2,1)S(1)} %collective-permute-done.1.refs_2_), channel_id=1, source_target_pairs={{0,1},{1,0},{2,3},{3,2},{4,5},{5,4},{6,7},{7,6},{8,9},{9,8},{10,11... | collective-permute-start | bytes 221192 | tf_op jit(solution)/shard_map/ppermute | solution.py:208
  15.2 3.6 %collective-permute-start.12 = (bf16[288,128]{1,0:T(8,128)(2,1)S(1)}, bf16[288,128]{1,0:T(8,128)(2,1)S(1)}, u32[]{:S(2)}, u32[]{:S(2)}) collective-permute-start(bf16[288,128]{1,0:T(8,128)(2,1)S(1)} %collective-permute-done.11.refs_12_), channel_id=1, source_target_pairs={{0,1},{1,0},{2,3},{3,2},{4,5},{5,4},{6,7},{7,6},{8,9},{9,8},{10,11... | collective-permute-start | bytes 221192 | tf_op jit(solution)/shard_map/ppermute | solution.py:208
  15.6 3.3 %collective-permute-start.10 = (bf16[288,128]{1,0:T(8,128)(2,1)S(1)}, bf16[288,128]{1,0:T(8,128)(2,1)S(1)}, u32[]{:S(2)}, u32[]{:S(2)}) collective-permute-start(bf16[288,128]{1,0:T(8,128)(2,1)S(1)} %collective-permute-done.9.refs_10_), channel_id=1, source_target_pairs={{0,1},{1,0},{2,3},{3,2},{4,5},{5,4},{6,7},{7,6},{8,9},{9,8},{10,11... | collective-permute-start | bytes 221192 | tf_op jit(solution)/shard_map/ppermute | solution.py:208
  16.8 2.0 %collective-permute-start.6 = (bf16[288,128]{1,0:T(8,128)(2,1)S(1)}, bf16[288,128]{1,0:T(8,128)(2,1)S(1)}, u32[]{:S(2)}, u32[]{:S(2)}) collective-permute-start(bf16[288,128]{1,0:T(8,128)(2,1)S(1)} %collective-permute-done.5.refs_6_), channel_id=1, source_target_pairs={{0,1},{1,0},{2,3},{3,2},{4,5},{5,4},{6,7},{7,6},{8,9},{9,8},{10,11... | collective-permute-start | bytes 221192 | tf_op jit(solution)/shard_map/ppermute | solution.py:208
  17.2 1.7 %collective-permute-start.14 = (bf16[288,128]{1,0:T(8,128)(2,1)S(1)}, bf16[288,128]{1,0:T(8,128)(2,1)S(1)}, u32[]{:S(2)}, u32[]{:S(2)}) collective-permute-start(bf16[288,128]{1,0:T(8,128)(2,1)S(1)} %collective-permute-done.13.refs_14_), channel_id=1, source_target_pairs={{0,1},{1,0},{2,3},{3,2},{4,5},{5,4},{6,7},{7,6},{8,9},{9,8},{10,11... | collective-permute-start | bytes 221192 | tf_op jit(solution)/shard_map/ppermute | solution.py:208
  18.8 0.7 %copy-start.1 = (bf16[16,128]{1,0:T(8,128)(2,1)S(1)}, bf16[16,128]{1,0:T(8,128)(2,1)}, u32[]{:S(2)}) copy-start(bf16[16,128]{1,0:T(8,128)(2,1)} %refs_23_.1) | copy-start | bytes 12292
  19.0 0.7 %copy-start.5 = (f32[16]{0:T(128)S(1)}, f32[16]{0:T(128)}, u32[]{:S(2)}) copy-start(f32[16]{0:T(128)} %param.17) | copy-start | bytes 196
  19.0 0.7 %copy-start.2 = (f32[128]{0:T(128)S(1)}, f32[128]{0:T(128)}, u32[]{:S(2)}) copy-start(f32[128]{0:T(128)} %param.12) | copy-start | bytes 1540
  19.0 0.7 %copy-start.3 = (f32[128]{0:T(128)S(1)}, f32[128]{0:T(128)}, u32[]{:S(2)}) copy-start(f32[128]{0:T(128)} %param.13) | copy-start | bytes 1540
  19.0 0.7 %copy-start.4 = (f32[16]{0:T(128)S(1)}, f32[16]{0:T(128)}, u32[]{:S(2)}) copy-start(f32[16]{0:T(128)} %param.16) | copy-start | bytes 196

commit v3 on v2

--- a/solution.py
+++ b/solution.py
@@ -8,6 +8,7 @@
 from jax.sharding import PartitionSpec as P
 
 LANES = 128
+KINDS = 4
 WHOLE_BYTES = 4 << 20
 
 NN = (((1,), (0,)), ((), ()))
@@ -34,56 +35,90 @@
 
 
 def sigmoid(v):
-    return 1.0 / (1.0 + jnp.exp(-v))
-
-
-def normalize(v, axis=-1):
-    centered = v - jnp.mean(v, axis=axis, keepdims=True)
-    s = lax.rsqrt(jnp.mean(centered * centered, axis=axis, keepdims=True) + 1e-05)
+    return 0.5 * jnp.tanh(0.5 * v) + 0.5
+
+
+def normalize(v):
+    centered = v - jnp.mean(v, axis=-1, keepdims=True)
+    s = lax.rsqrt(jnp.mean(centered * centered, axis=-1, keepdims=True) + 1e-05)
     return centered * s, s
 
 
-def crop_kernel(
-    n,
-    hidden,
-    blocks,
-    *refs,
-):
+def norm_tiles(n, block_refs, gain, bias, zn_ref):
+    per = zn_ref.shape[0]
+    rows = block_refs[0].shape[0] // (2 * n)
+    for t in range(len(block_refs) * rows):
+        v = block_refs[t // rows][pl.ds(t % rows * n, n), :].astype(jnp.float32)
+        zn_ref[t % per, pl.ds(t // per * n, n), :] = (normalize(v)[0] * gain + bias).astype(jnp.bfloat16)
+
+
+def project_tiles(zn_ref, project_t):
+    per = zn_ref.shape[0]
+    hidden = project_t.shape[0] // KINDS
+    columns = []
+    for p in range(per):
+        parts = []
+        for kind in range(KINDS):
+            own = project_t[kind * hidden : (kind + 1) * hidden]
+            before, after = p * hidden, (per - 1 - p) * hidden
+            parts += [jnp.zeros((before, own.shape[1]), own.dtype)] * (before > 0) + [own]
+            parts += [jnp.zeros((after, own.shape[1]), own.dtype)] * (after > 0)
+        columns.append(jnp.concatenate(parts, axis=0))
+    weight = jnp.concatenate(columns, axis=1)
+    zn = jnp.concatenate([zn_ref[p] for p in range(per)], axis=1)
+    return dot(zn, weight, NT)
+
+
+def head_kernel(n, *refs):
+    *block_refs, gain_ref, bias_ref, project_ref, gate_ref, zn_ref, projected_ref, go_ref = refs
+    norm_tiles(n, block_refs, gain_ref[...], bias_ref[...], zn_ref)
+    projected_ref[...] = project_tiles(zn_ref, project_ref[...])
+    gate_weight = gate_ref[...]
+    for p in range(zn_ref.shape[0]):
+        go_ref[p] = sigmoid(dot(zn_ref[p], gate_weight))
+
+
+def tail_kernel(n, hidden, order, *refs):
+    blocks = len(order)
     block_refs, refs = refs[:blocks], refs[blocks:]
-    count_ref, gain_ref, bias_ref, project_ref, gate_ref = refs[:5]
-    out_gain_ref, out_bias_ref, out_weight_ref = refs[5:8]
-    update_ref, pair_ref, project_grad_ref, gate_grad_ref, out_grad_ref = refs[8:13]
-    zn_ref, ug_ref, upd_ref, dgo_ref, dp_ref, dpt_ref = refs[13:]
+    zn_head_ref, projected_head_ref, go_head_ref = refs[:3]
+    count_ref, gain_ref, bias_ref, project_ref, gate_ref = refs[3:8]
+    out_gain_ref, out_bias_ref, out_weight_ref = refs[8:11]
+    update_ref, pair_ref, project_grad_ref, gate_grad_ref, out_grad_ref = refs[11:16]
+    zn_tail_ref, dpt_ref = refs[16:]
     f32, bf16 = jnp.float32, jnp.bfloat16
     per = LANES // hidden
     groups = n // per
     wide = n * hidden
+    rows = n // blocks
     me = lax.axis_index("row")
-    rows = n // blocks
-    half = rows * n
     count = count_ref[0]
     gain, bias = gain_ref[...], bias_ref[...]
-
-    for d, block_ref in enumerate(block_refs):
-        for r in range(rows):
-            i = (me ^ d) * rows + r
-            p, where = lax.rem(i, per), pl.ds(pl.multiple_of(lax.div(i, per) * n, 16), n)
-            zhat, _ = normalize(block_ref[pl.ds(r * n, n), :].astype(f32))
-            zn_ref[p, where, :] = (zhat * gain + bias).astype(bf16)
-            ug_ref[p, where, :] = block_ref[pl.ds(half + r * n, n), :]
-
-    kinds = 4 * LANES
-    a, b = iota((4 * hidden, kinds), 0), iota((4 * hidden, kinds), 1)
-    spread = zero_one((a // hidden == b // LANES) & (a % hidden == b % hidden))
-    tiled = dot(project_ref[...], spread).astype(bf16)
-    place = (iota((LANES, kinds), 1) % LANES) // hidden
-    projected = jnp.zeros((groups * n, kinds), f32)
-    for p in range(per):
-        projected += dot(zn_ref[p], jnp.where(place == p, tiled, jnp.zeros_like(tiled)))
-    row_k = jnp.concatenate([iota((n, LANES), 0)] * groups, axis=0)
-    row_g = jnp.concatenate([jnp.full((n, LANES), g * per, jnp.int32) for g in range(groups)], axis=0)
-    row_i = row_g + iota((groups * n, LANES), 1) // hidden
-    mask = jnp.where((row_i < count) & (row_k < count), 1.0, 0.0)
+    gate_weight = gate_ref[...]
+    project_t = project_ref[...]
+
+    def row_of(t):
+        return (me ^ order[t // rows]) * rows + t % rows
+
+    def tiles(p):
+        return [(t // rows, t % rows * n) for t in range(p, n, per)]
+
+    norm_tiles(n, block_refs[blocks // 2 :], gain, bias, zn_tail_ref)
+
+    def zn_of(p):
+        return jnp.concatenate([zn_head_ref[p], zn_tail_ref[p]], axis=0)
+
+    projected = jnp.concatenate([projected_head_ref[...], project_tiles(zn_tail_ref, project_t)], axis=0)
+
+    place = iota((1, LANES), 1) // hidden
+    row_i = []
+    for g in range(groups):
+        at = jnp.full((1, LANES), row_of(g * per), jnp.int32)
+        for p in range(1, per):
+            at = jnp.where(place == p, row_of(g * per + p), at)
+        row_i.append(at)
+    live_k = iota((n, LANES), 0) < count
+    mask = jnp.concatenate([jnp.where(live_k & (at < count), 1.0, 0.0) for at in row_i], axis=0)
     value_left, value_right = projected[:, :LANES], projected[:, 2 * LANES : 3 * LANES]
     gate_left = sigmoid(projected[:, LANES : 2 * LANES])
     gate_right = sigmoid(projected[:, 3 * LANES :])
@@ -99,12 +134,12 @@
     right = lanes((mask_right * value_right).astype(bf16))
 
     same = iota((LANES, wide), 0) % hidden == iota((LANES, wide), 1) % hidden
-    pick = zero_one(iota((per, LANES), 0) == iota((per, LANES), 1) // hidden)
-    parts = []
+    x = jnp.zeros((n, wide), f32)
     for g in range(groups):
         cross = dot(right[:, g * LANES : (g + 1) * LANES], left, TN).astype(bf16)
-        parts.append(dot(pick, jnp.where(same, cross, jnp.zeros_like(cross))))
-    x = flatten(jnp.concatenate(parts, axis=0))
+        pick = zero_one(iota((n, LANES), 0) == row_i[g])
+        x += dot(pick, jnp.where(same, cross, jnp.zeros_like(cross)))
+    x = flatten(x)
 
     mean = jnp.where(iota((LANES, LANES), 0) // hidden == iota((LANES, LANES), 1) // hidden, 1.0 / hidden, 0.0)
     mean = mean.astype(bf16)
@@ -117,20 +152,23 @@
 
     out_weight = jnp.concatenate([out_weight_ref[...]] * per, axis=0)
     at = iota((LANES, LANES), 0) // hidden
-    gate_weight = gate_ref[...]
     gate_grad = jnp.zeros((LANES, LANES), f32)
     out_grad = jnp.zeros((hidden, LANES), f32)
     dxn = jnp.zeros((groups * n, LANES), f32)
+    own_dgo = []
     for p in range(per):
-        zn = zn_ref[p]
+        zn = zn_of(p)
         weight = jnp.where(at == p, out_weight, jnp.zeros_like(out_weight))
         y = dot(xn, weight)
-        go = sigmoid(dot(zn, gate_weight))
-        upd_ref[p] = (go * y).astype(bf16)
-        cotangent = ug_ref[p].astype(f32)
-        dy = (cotangent * go).astype(bf16)
-        dgo = (cotangent * y * go * (1.0 - go)).astype(bf16)
-        dgo_ref[p] = dgo
+        go = jnp.concatenate([go_head_ref[p], sigmoid(dot(zn_tail_ref[p], gate_weight))], axis=0)
+        ug = [block_refs[b][pl.ds(rows * n + start, n), :] for b, start in tiles(p)]
+        cotangent = jnp.concatenate(ug, axis=0).astype(f32)
+        dy_wide = cotangent * go
+        dy = dy_wide.astype(bf16)
+        dgo = (dy_wide * y * (1.0 - go)).astype(bf16)
+        if p < rows:
+            update_ref[p] = (go[:n] * y[:n]).astype(bf16)
+            own_dgo.append(dgo[:n])
         gate_grad += dot(zn, dgo, TN)
         out_grad += dot(xn, dy, TN)[p * hidden : (p + 1) * hidden]
         dxn += dot(dy, weight, NT)
@@ -141,40 +179,37 @@
     dx = xs * (u - dot_split(u, mean) - xhat * dot_split(u * xhat, mean))
     dx = lanes(dx.astype(bf16))
 
-    repeat = zero_one(iota((LANES, per), 0) // hidden == iota((LANES, per), 1))
     dleft = jnp.zeros((n, wide), f32)
     dright = []
     for g in range(groups):
-        spread_dx = dot(repeat, dx[g * per : (g + 1) * per]).astype(bf16)
-        diagonal = jnp.where(same, spread_dx, jnp.zeros_like(spread_dx))
+        repeat = [zero_one(iota((hidden, n), 1) == row_of(g * per + p)) for p in range(per)]
+        spread = dot(jnp.concatenate(repeat, axis=0), dx).astype(bf16)
+        diagonal = jnp.where(same, spread, jnp.zeros_like(spread))
         dleft += dot(right[:, g * LANES : (g + 1) * LANES], diagonal)
         dright.append(dot(left, diagonal, NT))
     dleft = flatten(dleft.astype(bf16)).astype(f32)
     dright = jnp.concatenate(dright, axis=0).astype(bf16).astype(f32)
+    dleft, dright = dleft * mask_left, dright * mask_right
     dp = [
-        dleft * mask_left,
-        dleft * mask_left * value_left * (1.0 - gate_left),
-        dright * mask_right,
-        dright * mask_right * value_right * (1.0 - gate_right),
+        dleft,
+        dleft * value_left * (1.0 - gate_left),
+        dright,
+        dright * value_right * (1.0 - gate_right),
     ]
     dp = jnp.concatenate([d.astype(bf16) for d in dp], axis=1)
-    dp_ref[...] = dp
     dpt_ref[...] = dp.T
-    project_grad = jnp.zeros((4 * hidden, LANES), f32)
+    project_grad = jnp.zeros((KINDS * hidden, LANES), f32)
     for p in range(per):
-        at_p = [dpt_ref[pl.ds(kind * LANES + p * hidden, hidden), :] for kind in range(4)]
-        project_grad += dot(jnp.concatenate(at_p, axis=0), zn_ref[p])
-    project_grad_ref[...] = project_grad.T / n
-
-    place = (iota((n, kinds), 1) % LANES) // hidden
+        at_p = [dpt_ref[pl.ds(kind * LANES + p * hidden, hidden), :] for kind in range(KINDS)]
+        project_grad += dot(jnp.concatenate(at_p, axis=0), zn_of(p))
+    project_grad_ref[...] = project_grad / n
+
+    tiled = [project_t[kind * hidden : (kind + 1) * hidden] for kind in range(KINDS) for _ in range(per)]
+    tiled = jnp.concatenate(tiled, axis=0)
+    place = iota((n, KINDS * LANES), 1) % LANES // hidden
     for r in range(rows):
-        i = me * rows + r
-        g, p = lax.div(i, per), lax.rem(i, per)
-        where = pl.ds(pl.multiple_of(g * n, 16), n)
-        update_ref[r] = upd_ref[p, where, :]
-        dp_row = dp_ref[where, :]
-        dp_row = jnp.where(place == p, dp_row, jnp.zeros_like(dp_row))
-        dzn = dot(dp_row, tiled, NT) + dot(dgo_ref[p, where, :], gate_weight, NT)
+        dp_row = jnp.where(place == r, dp[:n], jnp.zeros_like(dp[:n]))
+        dzn = dot(dp_row, tiled) + dot(own_dgo[r], gate_weight, NT)
         zhat, zs = normalize(block_refs[0][pl.ds(r * n, n), :].astype(f32))
         u = gain * dzn
         first = jnp.mean(u, axis=-1, keepdims=True)
@@ -197,6 +232,7 @@
 ):
     rows, n, channels = pair_acts.shape
     hidden = output_weight.shape[0]
+    f32, bf16 = jnp.float32, jnp.bfloat16
     half = rows * n
     send = jnp.concatenate(
         [pair_acts.reshape(half, channels), update_grad.reshape(half, channels)], axis=0
@@ -207,41 +243,56 @@
         pairs = [(i, i ^ step) for i in range(devices)]
         blocks.update({d ^ step: lax.ppermute(blocks[d], "row", pairs) for d in list(blocks)})
         step //= 2
+    order = sorted(blocks, key=lambda d: (d & 2, d))
+    ordered = [blocks[d] for d in order]
     per = LANES // hidden
     tall = n // per * n
-    f32, bf16 = jnp.float32, jnp.bfloat16
     vmem = pl.BlockSpec(memory_space=pltpu.VMEM)
-    return pl.pallas_call(
-        functools.partial(crop_kernel, n, hidden, devices),
+    shape = jax.ShapeDtypeStruct
+    gain, bias, project_t = input_gain[None], input_bias[None], project_weight.T
+    head_blocks = ordered[: devices // 2]
+    head = pl.pallas_call(
+        functools.partial(head_kernel, n),
         out_shape=(
-            jax.ShapeDtypeStruct((rows, n, channels), bf16),
-            jax.ShapeDtypeStruct((rows, n, channels), f32),
-            jax.ShapeDtypeStruct((channels, 4 * hidden), f32),
-            jax.ShapeDtypeStruct((channels, channels), f32),
-            jax.ShapeDtypeStruct((hidden, channels), f32),
+            shape((per, tall // 2, channels), bf16),
+            shape((tall // 2, KINDS * LANES), f32),
+            shape((per, tall // 2, channels), f32),
         ),
-        in_specs=[vmem] * devices + [pl.BlockSpec(memory_space=pltpu.SMEM)] + [vmem] * 7,
+        in_specs=[vmem] * (len(head_blocks) + 4),
+        out_specs=(vmem,) * 3,
+        compiler_params=pltpu.CompilerParams(vmem_limit_bytes=16 << 20),
+        name="head",
+    )(*head_blocks, gain, bias, project_t, gate_weight)
+    update, pair_grad, project_grad, gate_grad, output_grad = pl.pallas_call(
+        functools.partial(tail_kernel, n, hidden, order),
+        out_shape=(
+            shape((rows, n, channels), bf16),
+            shape((rows, n, channels), f32),
+            shape((KINDS * hidden, channels), f32),
+            shape((channels, channels), f32),
+            shape((hidden, channels), f32),
+        ),
+        in_specs=[vmem] * (devices + 3) + [pl.BlockSpec(memory_space=pltpu.SMEM)] + [vmem] * 7,
         out_specs=(vmem,) * 5,
         scratch_shapes=[
-            pltpu.VMEM((per, tall, channels), bf16),
-            pltpu.VMEM((per, tall, channels), bf16),
-            pltpu.VMEM((per, tall, channels), bf16),
-            pltpu.VMEM((per, tall, channels), bf16),
-            pltpu.VMEM((tall, 4 * LANES), bf16),
-            pltpu.VMEM((4 * LANES, tall), bf16),
+            pltpu.VMEM((per, tall // 2, channels), bf16),
+            pltpu.VMEM((KINDS * LANES, tall), bf16),
         ],
         compiler_params=pltpu.CompilerParams(vmem_limit_bytes=32 << 20),
+        name="tail",
     )(
-        *[blocks[d] for d in range(devices)],
+        *ordered,
+        *head,
         token_count,
-        input_gain[None],
-        input_bias[None],
-        project_weight,
+        gain,
+        bias,
+        project_t,
         gate_weight,
         output_norm_gain[None],
         output_shift_bias[None],
         output_weight,
     )
+    return update, pair_grad, project_grad.T, gate_grad, output_grad
 
 
 def layer_normalize(values, norm_gain, norm_bias, reduce_axis):
@@ -392,6 +443,9 @@
         and length % 16 == 0
         and devices & (devices - 1) == 0
         and length % devices == 0
+        and length // devices <= LANES // hidden
+        and devices >= 4
+        and length // 2 % (LANES // hidden) == 0
         and 2 * pair_acts.dtype.itemsize * length * length * channels <= WHOLE_BYTES
     )
 

time: 29.1 us -> 28.3 us (0.973); the launches traced: 28.5 us -> 28 us
  waiting for transfers between devices: 0.82 us -> 0.36 us
  starting transfers between devices: 15.9 us -> 16.2 us
    pallas_call x1 -> x0, local copies, waits for them, and re-layouts: 0.7 us -> none  [body_whole(): pl.pallas_call(functools.partial(crop_kernel, n, hidden, devices), out_sh...]
    unnamed x15 -> x14, local copies, waits for them, and re-layouts: 0.82 us -> 1.32 us
    ppermute x15, waiting for transfers between devices: 0.82 us -> 0.36 us  [body_whole(): lax.ppermute(blocks[d], 'row', pairs)]
    ppermute x15, starting transfers between devices: 15.9 us -> 16.2 us  [body_whole(): lax.ppermute(blocks[d], 'row', pairs)]
    pallas_call x1 -> x2, Pallas kernels: 8.19 us -> 7.97 us  [the longest x1 7.05 us: body_whole(): pl.pallas_call(functools.partial(tail_kernel, n, hidden, order), out_shap...]
  transfers between devices with their start and end apart: 15 -> 15, of which waited for: 3 -> 1; matrix products, arithmetic and copies ran while one was open for 0% -> 0% of each run, Pallas kernels for 0% -> 3%
where the time goes in v3:
time: 28.3 us; the launch traced here: 28 us
  starting transfers between devices  16.2 us (57%)
  Pallas kernels  7.97 us (28%)
  between operations  1.42 us (5%)
  local copies, waits for them, and re-layouts  1.32 us (5%)
  other arithmetic  0.8 us (3%)
  waiting for transfers between devices  0.36 us (1%)
    ppermute x15, starting transfers between devices, body_whole(): lax.ppermute(blocks[d], 'row', pairs)  16.2 us
    pallas_call x1, Pallas kernels, body_whole(): pl.pallas_call(functools.partial(tail_kernel, n, hidden, order), out_shap...  7.05 us
    unnamed x14, local copies, waits for them, and re-layouts  1.32 us
    pallas_call x1, Pallas kernels, body_whole(): pl.pallas_call(functools.partial(head_kernel, n), out_shape=(shape((per,...  0.91 us
    concatenate x1, other arithmetic, body_whole(): jnp.concatenate([pair_acts.reshape(half, channels), update_grad.reshape(h...  0.8 us
  transfers between devices with their start and end apart: 15, of which 1 were waited for; matrix products, arithmetic and copies ran while one was open for 0% of the time, Pallas kernels for 3%

profile of v3, /device:TPU:1, one launch (start us, length us, event | category | flops | bytes accessed | tf_op | source)
XLA Modules:
  0.0 28.0 jit_solution(12895240690225951740)
XLA Ops:
  0.7 0.8 %pad_maximum_fusion.refs_0_ = bf16[288,128]{1,0:T(8,128)(2,1)S(1)} fusion(bf16[144,128]{1,0:T(8,128)(2,1)} %bitcast.16, bf16[144,128]{1,0:T(8,128)(2,1)} %bitcast.17), kind=kLoop, calls=%fused_computation | loop fusion | flops 147456 | bytes 147456 | tf_op jit(solution)/shard_map/concatenate | solution.py:237
  1.5 3.1 %collective-permute-start.3 = (bf16[288,128]{1,0:T(8,128)(2,1)S(1)}, bf16[288,128]{1,0:T(8,128)(2,1)S(1)}, u32[]{:S(2)}, u32[]{:S(2)}) collective-permute-start(bf16[288,128]{1,0:T(8,128)(2,1)S(1)} %pad_maximum_fusion.refs_0_), channel_id=1, source_target_pairs={{0,8},{1,9},{2,10},{3,11},{4,12},{5,13},{6,14},{7,15},{8,0},{9,1},... | collective-permute-start | bytes 221192 | tf_op jit(solution)/shard_map/ppermute | solution.py:244
  4.6 1.2 %collective-permute-start.7 = (bf16[288,128]{1,0:T(8,128)(2,1)S(1)}, bf16[288,128]{1,0:T(8,128)(2,1)S(1)}, u32[]{:S(2)}, u32[]{:S(2)}) collective-permute-start(bf16[288,128]{1,0:T(8,128)(2,1)S(1)} %pad_maximum_fusion.refs_0_), channel_id=1, source_target_pairs={{0,2},{1,3},{2,0},{3,1},{4,6},{5,7},{6,4},{7,5},{8,10},{9,11},{10,... | collective-permute-start | bytes 221192 | tf_op jit(solution)/shard_map/ppermute | solution.py:244
  5.8 1.3 %collective-permute-start.1 = (bf16[288,128]{1,0:T(8,128)(2,1)S(1)}, bf16[288,128]{1,0:T(8,128)(2,1)S(1)}, u32[]{:S(2)}, u32[]{:S(2)}) collective-permute-start(bf16[288,128]{1,0:T(8,128)(2,1)S(1)} %pad_maximum_fusion.refs_0_), channel_id=1, source_target_pairs={{0,4},{1,5},{2,6},{3,7},{4,0},{5,1},{6,2},{7,3},{8,12},{9,13},{10,... | collective-permute-start | bytes 221192 | tf_op jit(solution)/shard_map/ppermute | solution.py:244
  7.1 1.5 %collective-permute-start = (bf16[288,128]{1,0:T(8,128)(2,1)S(1)}, bf16[288,128]{1,0:T(8,128)(2,1)S(1)}, u32[]{:S(2)}, u32[]{:S(2)}) collective-permute-start(bf16[288,128]{1,0:T(8,128)(2,1)S(1)} %pad_maximum_fusion.refs_0_), channel_id=1, source_target_pairs={{0,1},{1,0},{2,3},{3,2},{4,5},{5,4},{6,7},{7,6},{8,9},{9,8},{10,11... | collective-permute-start | bytes 221192 | tf_op jit(solution)/shard_map/ppermute | solution.py:244
  8.6 0.5 %collective-permute-start.5 = (bf16[288,128]{1,0:T(8,128)(2,1)S(1)}, bf16[288,128]{1,0:T(8,128)(2,1)S(1)}, u32[]{:S(2)}, u32[]{:S(2)}) collective-permute-start(bf16[288,128]{1,0:T(8,128)(2,1)S(1)} %collective-permute-done.3.refs_4_), channel_id=1, source_target_pairs={{0,4},{1,5},{2,6},{3,7},{4,0},{5,1},{6,2},{7,3},{8,12},{9,13},{10,... | collective-permute-start | bytes 221192 | tf_op jit(solution)/shard_map/ppermute | solution.py:244
  9.1 1.1 %collective-permute-start.11 = (bf16[288,128]{1,0:T(8,128)(2,1)S(1)}, bf16[288,128]{1,0:T(8,128)(2,1)S(1)}, u32[]{:S(2)}, u32[]{:S(2)}) collective-permute-start(bf16[288,128]{1,0:T(8,128)(2,1)S(1)} %collective-permute-done.3.refs_4_), channel_id=1, source_target_pairs={{0,2},{1,3},{2,0},{3,1},{4,6},{5,7},{6,4},{7,5},{8,10},{9,11},{10,... | collective-permute-start | bytes 221192 | tf_op jit(solution)/shard_map/ppermute | solution.py:244
  10.2 1.6 %collective-permute-start.4 = (bf16[288,128]{1,0:T(8,128)(2,1)S(1)}, bf16[288,128]{1,0:T(8,128)(2,1)S(1)}, u32[]{:S(2)}, u32[]{:S(2)}) collective-permute-start(bf16[288,128]{1,0:T(8,128)(2,1)S(1)} %collective-permute-done.3.refs_4_), channel_id=1, source_target_pairs={{0,1},{1,0},{2,3},{3,2},{4,5},{5,4},{6,7},{7,6},{8,9},{9,8},{10,11... | collective-permute-start | bytes 221192 | tf_op jit(solution)/shard_map/ppermute | solution.py:244
  11.7 0.3 %collective-permute-start.9 = (bf16[288,128]{1,0:T(8,128)(2,1)S(1)}, bf16[288,128]{1,0:T(8,128)(2,1)S(1)}, u32[]{:S(2)}, u32[]{:S(2)}) collective-permute-start(bf16[288,128]{1,0:T(8,128)(2,1)S(1)} %collective-permute-done.1.refs_2_), channel_id=1, source_target_pairs={{0,2},{1,3},{2,0},{3,1},{4,6},{5,7},{6,4},{7,5},{8,10},{9,11},{10,... | collective-permute-start | bytes 221192 | tf_op jit(solution)/shard_map/ppermute | solution.py:244
  12.1 0.3 %collective-permute-start.2 = (bf16[288,128]{1,0:T(8,128)(2,1)S(1)}, bf16[288,128]{1,0:T(8,128)(2,1)S(1)}, u32[]{:S(2)}, u32[]{:S(2)}) collective-permute-start(bf16[288,128]{1,0:T(8,128)(2,1)S(1)} %collective-permute-done.1.refs_2_), channel_id=1, source_target_pairs={{0,1},{1,0},{2,3},{3,2},{4,5},{5,4},{6,7},{7,6},{8,9},{9,8},{10,11... | collective-permute-start | bytes 221192 | tf_op jit(solution)/shard_map/ppermute | solution.py:244
  12.4 1.1 %collective-permute-start.13 = (bf16[288,128]{1,0:T(8,128)(2,1)S(1)}, bf16[288,128]{1,0:T(8,128)(2,1)S(1)}, u32[]{:S(2)}, u32[]{:S(2)}) collective-permute-start(bf16[288,128]{1,0:T(8,128)(2,1)S(1)} %collective-permute-done.5.refs_6_), channel_id=1, source_target_pairs={{0,2},{1,3},{2,0},{3,1},{4,6},{5,7},{6,4},{7,5},{8,10},{9,11},{10,... | collective-permute-start | bytes 221192 | tf_op jit(solution)/shard_map/ppermute | solution.py:244
  13.6 1.6 %collective-permute-start.6 = (bf16[288,128]{1,0:T(8,128)(2,1)S(1)}, bf16[288,128]{1,0:T(8,128)(2,1)S(1)}, u32[]{:S(2)}, u32[]{:S(2)}) collective-permute-start(bf16[288,128]{1,0:T(8,128)(2,1)S(1)} %collective-permute-done.5.refs_6_), channel_id=1, source_target_pairs={{0,1},{1,0},{2,3},{3,2},{4,5},{5,4},{6,7},{7,6},{8,9},{9,8},{10,11... | collective-permute-start | bytes 221192 | tf_op jit(solution)/shard_map/ppermute | solution.py:244
  15.2 0.1 collective-permute-start.8
  15.2 0.3 %collective-permute-done.9.refs_10_ = bf16[288,128]{1,0:T(8,128)(2,1)S(1)} collective-permute-done((bf16[288,128]{1,0:T(8,128)(2,1)S(1)}, bf16[288,128]{1,0:T(8,128)(2,1)S(1)}, u32[]{:S(2)}, u32[]{:S(2)}) %collective-permute-start.9) | collective-permute-done | bytes 73760 | tf_op jit(solution)/shard_map/ppermute | solution.py:244
  15.6 1.3 %collective-permute-start.12 = (bf16[288,128]{1,0:T(8,128)(2,1)S(1)}, bf16[288,128]{1,0:T(8,128)(2,1)S(1)}, u32[]{:S(2)}, u32[]{:S(2)}) collective-permute-start(bf16[288,128]{1,0:T(8,128)(2,1)S(1)} %collective-permute-done.11.refs_12_), channel_id=1, source_target_pairs={{0,1},{1,0},{2,3},{3,2},{4,5},{5,4},{6,7},{7,6},{8,9},{9,8},{10,11... | collective-permute-start | bytes 221192 | tf_op jit(solution)/shard_map/ppermute | solution.py:244
  16.9 0.0 collective-permute-start.10
  16.9 1.1 %collective-permute-start.14 = (bf16[288,128]{1,0:T(8,128)(2,1)S(1)}, bf16[288,128]{1,0:T(8,128)(2,1)S(1)}, u32[]{:S(2)}, u32[]{:S(2)}) collective-permute-start(bf16[288,128]{1,0:T(8,128)(2,1)S(1)} %collective-permute-done.13.refs_14_), channel_id=1, source_target_pairs={{0,1},{1,0},{2,3},{3,2},{4,5},{5,4},{6,7},{7,6},{8,9},{9,8},{10,11... | collective-permute-start | bytes 221192 | tf_op jit(solution)/shard_map/ppermute | solution.py:244
  18.7 0.0 copy-start.3
  18.7 0.0 copy-start.4
  18.7 0.6 %copy-done.3 = f32[128]{0:T(128)S(1)} copy-done((f32[128]{0:T(128)S(1)}, f32[128]{0:T(128)}, u32[]{:S(2)}) %copy-start.3) | copy-done | bytes 536
  19.3 0.0 copy-done.4
  19.3 0.9 %head.1 = (bf16[8,144,128]{2,1,0:T(8,128)(2,1)S(1)}, f32[144,512]{1,0:T(8,128)S(1)}, f32[8,144,128]{2,1,0:T(8,128)S(1)}) custom-call(bf16[288,128]{1,0:T(8,128)(2,1)S(1)} %pad_maximum_fusion.refs_0_, bf16[288,128]{1,0:T(8,128)(2,1)S(1)} %collective-permute-done.refs_1_, bf16[288,128]{1,0:T(8,128)(2,1)S(1)} %collective-permute-done.1.refs_2_, ...), custom_call_target="tpu_custom_call" | custom-call | tf_op jit(solution)/shard_map/head/pallas_call | solution.py:254
  20.3 0.7 %copy-done.2 = bf16[16,128]{1,0:T(8,128)(2,1)S(1)} copy-done((bf16[16,128]{1,0:T(8,128)(2,1)S(1)}, bf16[16,128]{1,0:T(8,128)(2,1)}, u32[]{:S(2)}) %copy-start.2) | copy-done | bytes 4120
  21.0 7.1 %tail.1 = (bf16[3,48,128]{2,1,0:T(8,128)(2,1)}, f32[3,48,128]{2,1,0:T(8,128)}, f32[64,128]{1,0:T(8,128)}, f32[128,128]{1,0:T(8,128)}, f32[16,128]{1,0:T(8,128)}) custom-call(bf16[288,128]{1,0:T(8,128)(2,1)S(1)} %pad_maximum_fusion.refs_0_, bf16[288,128]{1,0:T(8,128)(2,1)S(1)} %collective-permute-done.refs_1_, ...), custom_call_target="tpu_custom_call" | custom-call | tf_op jit(solution)/shard_map/tail/pallas_call | solution.py:266
  (23 shorter events, 0.1 us)
Async XLA Ops:
  0.6 18.1 %copy-start = (bf16[128,128]{1,0:T(8,128)(2,1)S(1)}, bf16[128,128]{1,0:T(8,128)(2,1)}, u32[]{:S(2)}) copy-start(bf16[128,128]{1,0:T(8,128)(2,1)} %refs_23_.1) | copy-start | bytes 98308
  0.6 18.1 %copy-start.1 = (bf16[128,64]{0,1:T(8,128)(2,1)S(1)}, bf16[128,64]{0,1:T(8,128)(2,1)}, u32[]{:S(2)}) copy-start(bf16[128,64]{0,1:T(8,128)(2,1)} %param.14) | copy-start | bytes 49156
  1.5 7.2 %collective-permute-start.3 = (bf16[288,128]{1,0:T(8,128)(2,1)S(1)}, bf16[288,128]{1,0:T(8,128)(2,1)S(1)}, u32[]{:S(2)}, u32[]{:S(2)}) collective-permute-start(bf16[288,128]{1,0:T(8,128)(2,1)S(1)} %pad_maximum_fusion.refs_0_), channel_id=1, source_target_pairs={{0,8},{1,9},{2,10},{3,11},{4,12},{5,13},{6,14},{7,15},{8,0},{9,1},... | collective-permute-start | bytes 221192 | tf_op jit(solution)/shard_map/ppermute | solution.py:244
  4.6 5.6 %collective-permute-start.7 = (bf16[288,128]{1,0:T(8,128)(2,1)S(1)}, bf16[288,128]{1,0:T(8,128)(2,1)S(1)}, u32[]{:S(2)}, u32[]{:S(2)}) collective-permute-start(bf16[288,128]{1,0:T(8,128)(2,1)S(1)} %pad_maximum_fusion.refs_0_), channel_id=1, source_target_pairs={{0,2},{1,3},{2,0},{3,1},{4,6},{5,7},{6,4},{7,5},{8,10},{9,11},{10,... | collective-permute-start | bytes 221192 | tf_op jit(solution)/shard_map/ppermute | solution.py:244
  5.8 5.9 %collective-permute-start.1 = (bf16[288,128]{1,0:T(8,128)(2,1)S(1)}, bf16[288,128]{1,0:T(8,128)(2,1)S(1)}, u32[]{:S(2)}, u32[]{:S(2)}) collective-permute-start(bf16[288,128]{1,0:T(8,128)(2,1)S(1)} %pad_maximum_fusion.refs_0_), channel_id=1, source_target_pairs={{0,4},{1,5},{2,6},{3,7},{4,0},{5,1},{6,2},{7,3},{8,12},{9,13},{10,... | collective-permute-start | bytes 221192 | tf_op jit(solution)/shard_map/ppermute | solution.py:244
  7.1 5.0 %collective-permute-start = (bf16[288,128]{1,0:T(8,128)(2,1)S(1)}, bf16[288,128]{1,0:T(8,128)(2,1)S(1)}, u32[]{:S(2)}, u32[]{:S(2)}) collective-permute-start(bf16[288,128]{1,0:T(8,128)(2,1)S(1)} %pad_maximum_fusion.refs_0_), channel_id=1, source_target_pairs={{0,1},{1,0},{2,3},{3,2},{4,5},{5,4},{6,7},{7,6},{8,9},{9,8},{10,11... | collective-permute-start | bytes 221192 | tf_op jit(solution)/shard_map/ppermute | solution.py:244
  8.6 3.8 %collective-permute-start.5 = (bf16[288,128]{1,0:T(8,128)(2,1)S(1)}, bf16[288,128]{1,0:T(8,128)(2,1)S(1)}, u32[]{:S(2)}, u32[]{:S(2)}) collective-permute-start(bf16[288,128]{1,0:T(8,128)(2,1)S(1)} %collective-permute-done.3.refs_4_), channel_id=1, source_target_pairs={{0,4},{1,5},{2,6},{3,7},{4,0},{5,1},{6,2},{7,3},{8,12},{9,13},{10,... | collective-permute-start | bytes 221192 | tf_op jit(solution)/shard_map/ppermute | solution.py:244
  9.1 4.5 %collective-permute-start.11 = (bf16[288,128]{1,0:T(8,128)(2,1)S(1)}, bf16[288,128]{1,0:T(8,128)(2,1)S(1)}, u32[]{:S(2)}, u32[]{:S(2)}) collective-permute-start(bf16[288,128]{1,0:T(8,128)(2,1)S(1)} %collective-permute-done.3.refs_4_), channel_id=1, source_target_pairs={{0,2},{1,3},{2,0},{3,1},{4,6},{5,7},{6,4},{7,5},{8,10},{9,11},{10,... | collective-permute-start | bytes 221192 | tf_op jit(solution)/shard_map/ppermute | solution.py:244
  10.2 5.0 %collective-permute-start.4 = (bf16[288,128]{1,0:T(8,128)(2,1)S(1)}, bf16[288,128]{1,0:T(8,128)(2,1)S(1)}, u32[]{:S(2)}, u32[]{:S(2)}) collective-permute-start(bf16[288,128]{1,0:T(8,128)(2,1)S(1)} %collective-permute-done.3.refs_4_), channel_id=1, source_target_pairs={{0,1},{1,0},{2,3},{3,2},{4,5},{5,4},{6,7},{7,6},{8,9},{9,8},{10,11... | collective-permute-start | bytes 221192 | tf_op jit(solution)/shard_map/ppermute | solution.py:244
  11.7 3.8 %collective-permute-start.9 = (bf16[288,128]{1,0:T(8,128)(2,1)S(1)}, bf16[288,128]{1,0:T(8,128)(2,1)S(1)}, u32[]{:S(2)}, u32[]{:S(2)}) collective-permute-start(bf16[288,128]{1,0:T(8,128)(2,1)S(1)} %collective-permute-done.1.refs_2_), channel_id=1, source_target_pairs={{0,2},{1,3},{2,0},{3,1},{4,6},{5,7},{6,4},{7,5},{8,10},{9,11},{10,... | collective-permute-start | bytes 221192 | tf_op jit(solution)/shard_map/ppermute | solution.py:244
  12.1 4.8 %collective-permute-start.2 = (bf16[288,128]{1,0:T(8,128)(2,1)S(1)}, bf16[288,128]{1,0:T(8,128)(2,1)S(1)}, u32[]{:S(2)}, u32[]{:S(2)}) collective-permute-start(bf16[288,128]{1,0:T(8,128)(2,1)S(1)} %collective-permute-done.1.refs_2_), channel_id=1, source_target_pairs={{0,1},{1,0},{2,3},{3,2},{4,5},{5,4},{6,7},{7,6},{8,9},{9,8},{10,11... | collective-permute-start | bytes 221192 | tf_op jit(solution)/shard_map/ppermute | solution.py:244
  12.4 4.5 %collective-permute-start.13 = (bf16[288,128]{1,0:T(8,128)(2,1)S(1)}, bf16[288,128]{1,0:T(8,128)(2,1)S(1)}, u32[]{:S(2)}, u32[]{:S(2)}) collective-permute-start(bf16[288,128]{1,0:T(8,128)(2,1)S(1)} %collective-permute-done.5.refs_6_), channel_id=1, source_target_pairs={{0,2},{1,3},{2,0},{3,1},{4,6},{5,7},{6,4},{7,5},{8,10},{9,11},{10,... | collective-permute-start | bytes 221192 | tf_op jit(solution)/shard_map/ppermute | solution.py:244
  13.6 5.1 %collective-permute-start.6 = (bf16[288,128]{1,0:T(8,128)(2,1)S(1)}, bf16[288,128]{1,0:T(8,128)(2,1)S(1)}, u32[]{:S(2)}, u32[]{:S(2)}) collective-permute-start(bf16[288,128]{1,0:T(8,128)(2,1)S(1)} %collective-permute-done.5.refs_6_), channel_id=1, source_target_pairs={{0,1},{1,0},{2,3},{3,2},{4,5},{5,4},{6,7},{7,6},{8,9},{9,8},{10,11... | collective-permute-start | bytes 221192 | tf_op jit(solution)/shard_map/ppermute | solution.py:244
  15.2 5.1 %collective-permute-start.8 = (bf16[288,128]{1,0:T(8,128)(2,1)S(1)}, bf16[288,128]{1,0:T(8,128)(2,1)S(1)}, u32[]{:S(2)}, u32[]{:S(2)}) collective-permute-start(bf16[288,128]{1,0:T(8,128)(2,1)S(1)} %collective-permute-done.7.refs_8_), channel_id=1, source_target_pairs={{0,1},{1,0},{2,3},{3,2},{4,5},{5,4},{6,7},{7,6},{8,9},{9,8},{10,11... | collective-permute-start | bytes 221192 | tf_op jit(solution)/shard_map/ppermute | solution.py:244
  15.6 4.7 %collective-permute-start.12 = (bf16[288,128]{1,0:T(8,128)(2,1)S(1)}, bf16[288,128]{1,0:T(8,128)(2,1)S(1)}, u32[]{:S(2)}, u32[]{:S(2)}) collective-permute-start(bf16[288,128]{1,0:T(8,128)(2,1)S(1)} %collective-permute-done.11.refs_12_), channel_id=1, source_target_pairs={{0,1},{1,0},{2,3},{3,2},{4,5},{5,4},{6,7},{7,6},{8,9},{9,8},{10,11... | collective-permute-start | bytes 221192 | tf_op jit(solution)/shard_map/ppermute | solution.py:244
  16.9 3.4 %collective-permute-start.10 = (bf16[288,128]{1,0:T(8,128)(2,1)S(1)}, bf16[288,128]{1,0:T(8,128)(2,1)S(1)}, u32[]{:S(2)}, u32[]{:S(2)}) collective-permute-start(bf16[288,128]{1,0:T(8,128)(2,1)S(1)} %collective-permute-done.9.refs_10_), channel_id=1, source_target_pairs={{0,1},{1,0},{2,3},{3,2},{4,5},{5,4},{6,7},{7,6},{8,9},{9,8},{10,11... | collective-permute-start | bytes 221192 | tf_op jit(solution)/shard_map/ppermute | solution.py:244
  16.9 3.4 %collective-permute-start.14 = (bf16[288,128]{1,0:T(8,128)(2,1)S(1)}, bf16[288,128]{1,0:T(8,128)(2,1)S(1)}, u32[]{:S(2)}, u32[]{:S(2)}) collective-permute-start(bf16[288,128]{1,0:T(8,128)(2,1)S(1)} %collective-permute-done.13.refs_14_), channel_id=1, source_target_pairs={{0,1},{1,0},{2,3},{3,2},{4,5},{5,4},{6,7},{7,6},{8,9},{9,8},{10,11... | collective-permute-start | bytes 221192 | tf_op jit(solution)/shard_map/ppermute | solution.py:244
  18.7 0.7 %copy-start.3 = (f32[128]{0:T(128)S(1)}, f32[128]{0:T(128)}, u32[]{:S(2)}) copy-start(f32[128]{0:T(128)} %param.12) | copy-start | bytes 1540
  18.7 0.7 %copy-start.4 = (f32[128]{0:T(128)S(1)}, f32[128]{0:T(128)}, u32[]{:S(2)}) copy-start(f32[128]{0:T(128)} %param.13) | copy-start | bytes 1540
  20.3 0.7 %copy-start.2 = (bf16[16,128]{1,0:T(8,128)(2,1)S(1)}, bf16[16,128]{1,0:T(8,128)(2,1)}, u32[]{:S(2)}) copy-start(bf16[16,128]{1,0:T(8,128)(2,1)} %refs_26_.1) | copy-start | bytes 12292
  20.3 0.7 %copy-start.5 = (f32[16]{0:T(128)S(1)}, f32[16]{0:T(128)}, u32[]{:S(2)}) copy-start(f32[16]{0:T(128)} %param.16) | copy-start | bytes 196
  20.3 0.7 %copy-start.6 = (f32[16]{0:T(128)S(1)}, f32[16]{0:T(128)}, u32[]{:S(2)}) copy-start(f32[16]{0:T(128)} %param.17) | copy-start | bytes 196

commit v4 on v3

--- a/solution.py
+++ b/solution.py
@@ -20,10 +20,10 @@
     return lax.dot_general(a, b, dims, preferred_element_type=jnp.float32)
 
 
-def dot_split(a, b):
+def dot_split(a, b_twice):
     high = a.astype(jnp.bfloat16)
     low = (a - high.astype(jnp.float32)).astype(jnp.bfloat16)
-    return dot(high, b) + dot(low, b)
+    return dot(jnp.concatenate([high, low], axis=1), b_twice)
 
 
 def iota(shape, dim):
@@ -52,40 +52,67 @@
         zn_ref[t % per, pl.ds(t // per * n, n), :] = (normalize(v)[0] * gain + bias).astype(jnp.bfloat16)
 
 
-def project_tiles(zn_ref, project_t):
-    per = zn_ref.shape[0]
-    hidden = project_t.shape[0] // KINDS
+def wide_project(project_t, per):
+    hidden, channels = project_t.shape[0] // KINDS, project_t.shape[1]
     columns = []
     for p in range(per):
         parts = []
         for kind in range(KINDS):
-            own = project_t[kind * hidden : (kind + 1) * hidden]
             before, after = p * hidden, (per - 1 - p) * hidden
-            parts += [jnp.zeros((before, own.shape[1]), own.dtype)] * (before > 0) + [own]
-            parts += [jnp.zeros((after, own.shape[1]), own.dtype)] * (after > 0)
+            parts += [jnp.zeros((before, channels), project_t.dtype)] * (before > 0)
+            parts += [project_t[kind * hidden : (kind + 1) * hidden]]
+            parts += [jnp.zeros((after, channels), project_t.dtype)] * (after > 0)
         columns.append(jnp.concatenate(parts, axis=0))
-    weight = jnp.concatenate(columns, axis=1)
-    zn = jnp.concatenate([zn_ref[p] for p in range(per)], axis=1)
-    return dot(zn, weight, NT)
+    return jnp.concatenate(columns, axis=1)
+
+
+def wide_out(out_weight, per):
+    hidden, channels = out_weight.shape
+    rows = []
+    for p in range(per):
+        before, after = p * channels, (per - 1 - p) * channels
+        parts = [jnp.zeros((hidden, before), out_weight.dtype)] * (before > 0) + [out_weight]
+        rows.append(jnp.concatenate(parts + [jnp.zeros((hidden, after), out_weight.dtype)] * (after > 0), axis=1))
+    return jnp.concatenate(rows, axis=0)
+
+
+def side_by_side(ref):
+    return jnp.concatenate([ref[p] for p in range(ref.shape[0])], axis=1)
+
+
+def load_kernel(*refs):
+    count = len(refs) // 2
+    sources, targets, sems = refs[:count], refs[count : 2 * count - 1], refs[-1]
+    half = sources[0].shape[0]
+    targets = [targets[0].at[pl.ds(0, half)], targets[0].at[pl.ds(half, half)], *targets[1:]]
+    copies = [pltpu.make_async_copy(a, b, sems.at[k]) for k, (a, b) in enumerate(zip(sources, targets))]
+    for copy in copies:
+        copy.start()
+    for copy in copies:
+        copy.wait()
 
 
 def head_kernel(n, *refs):
-    *block_refs, gain_ref, bias_ref, project_ref, gate_ref, zn_ref, projected_ref, go_ref = refs
+    *block_refs, gain_ref, bias_ref, project_ref, gate_ref, out_weight_ref = refs[:-6]
+    zn_ref, projected_ref, go_ref, znt_ref, project_wide_ref, out_wide_ref = refs[-6:]
+    per = zn_ref.shape[0]
     norm_tiles(n, block_refs, gain_ref[...], bias_ref[...], zn_ref)
-    projected_ref[...] = project_tiles(zn_ref, project_ref[...])
+    project_wide_ref[...] = wide_project(project_ref[...], per)
+    out_wide_ref[...] = wide_out(out_weight_ref[...], per)
+    projected_ref[...] = dot(side_by_side(zn_ref), project_wide_ref[...], NT)
     gate_weight = gate_ref[...]
-    for p in range(zn_ref.shape[0]):
+    for p in range(per):
         go_ref[p] = sigmoid(dot(zn_ref[p], gate_weight))
+    znt_ref[...] = jnp.concatenate([zn_ref[p] for p in range(per)], axis=0).T
 
 
 def tail_kernel(n, hidden, order, *refs):
     blocks = len(order)
     block_refs, refs = refs[:blocks], refs[blocks:]
-    zn_head_ref, projected_head_ref, go_head_ref = refs[:3]
-    count_ref, gain_ref, bias_ref, project_ref, gate_ref = refs[3:8]
-    out_gain_ref, out_bias_ref, out_weight_ref = refs[8:11]
-    update_ref, pair_ref, project_grad_ref, gate_grad_ref, out_grad_ref = refs[11:16]
-    zn_tail_ref, dpt_ref = refs[16:]
+    zn_head_ref, projected_head_ref, go_head_ref, znt_head_ref, project_wide_ref, out_wide_ref = refs[:6]
+    count_ref, gain_ref, bias_ref, project_ref, gate_ref, out_gain_ref, out_bias_ref = refs[6:13]
+    update_ref, pair_ref, project_grad_ref, gate_grad_ref, out_grad_ref = refs[13:18]
+    zn_tail_ref, dpt_ref, square_ref, dgo_head_ref, dgo_tail_ref, dy_ref = refs[18:]
     f32, bf16 = jnp.float32, jnp.bfloat16
     per = LANES // hidden
     groups = n // per
@@ -108,7 +135,7 @@
     def zn_of(p):
         return jnp.concatenate([zn_head_ref[p], zn_tail_ref[p]], axis=0)
 
-    projected = jnp.concatenate([projected_head_ref[...], project_tiles(zn_tail_ref, project_t)], axis=0)
+    projected = jnp.concatenate([projected_head_ref[...], dot(side_by_side(zn_tail_ref), project_wide_ref[...], NT)], axis=0)
 
     place = iota((1, LANES), 1) // hidden
     row_i = []
@@ -134,61 +161,57 @@
     right = lanes((mask_right * value_right).astype(bf16))
 
     same = iota((LANES, wide), 0) % hidden == iota((LANES, wide), 1) % hidden
-    x = jnp.zeros((n, wide), f32)
     for g in range(groups):
         cross = dot(right[:, g * LANES : (g + 1) * LANES], left, TN).astype(bf16)
-        pick = zero_one(iota((n, LANES), 0) == row_i[g])
-        x += dot(pick, jnp.where(same, cross, jnp.zeros_like(cross)))
-    x = flatten(x)
+        square_ref[pl.ds(g * LANES, LANES), :] = jnp.where(same, cross, jnp.zeros_like(cross))
+    pick = jnp.concatenate([zero_one(iota((n, LANES), 0) == at) for at in row_i], axis=1)
+    x = flatten(dot(pick, square_ref[...]))
 
     mean = jnp.where(iota((LANES, LANES), 0) // hidden == iota((LANES, LANES), 1) // hidden, 1.0 / hidden, 0.0)
     mean = mean.astype(bf16)
+    mean_twice = jnp.concatenate([mean, mean], axis=0)
     out_gain = jnp.concatenate([out_gain_ref[...]] * per, axis=1)
     out_bias = jnp.concatenate([out_bias_ref[...]] * per, axis=1)
     centered = x - dot(x.astype(bf16), mean)
-    xs = lax.rsqrt(dot_split(centered * centered, mean) + 1e-05)
+    xs = lax.rsqrt(dot_split(centered * centered, mean_twice) + 1e-05)
     xhat = centered * xs
     xn = (xhat * out_gain + out_bias).astype(bf16)
 
-    out_weight = jnp.concatenate([out_weight_ref[...]] * per, axis=0)
-    at = iota((LANES, LANES), 0) // hidden
-    gate_grad = jnp.zeros((LANES, LANES), f32)
-    out_grad = jnp.zeros((hidden, LANES), f32)
-    dxn = jnp.zeros((groups * n, LANES), f32)
+    out_wide = out_wide_ref[...]
+    y_all = dot(xn, out_wide)
     own_dgo = []
+    half = groups // 2 * n
     for p in range(per):
-        zn = zn_of(p)
-        weight = jnp.where(at == p, out_weight, jnp.zeros_like(out_weight))
-        y = dot(xn, weight)
+        y = y_all[:, p * LANES : (p + 1) * LANES]
         go = jnp.concatenate([go_head_ref[p], sigmoid(dot(zn_tail_ref[p], gate_weight))], axis=0)
         ug = [block_refs[b][pl.ds(rows * n + start, n), :] for b, start in tiles(p)]
-        cotangent = jnp.concatenate(ug, axis=0).astype(f32)
-        dy_wide = cotangent * go
-        dy = dy_wide.astype(bf16)
-        dgo = (dy_wide * y * (1.0 - go)).astype(bf16)
+        dy = jnp.concatenate(ug, axis=0).astype(f32) * go
+        dgo = (dy * y * (1.0 - go)).astype(bf16)
+        dy_ref[:, p * LANES : (p + 1) * LANES] = dy.astype(bf16)
+        dgo_head_ref[pl.ds(p * half, half), :] = dgo[:half]
+        dgo_tail_ref[pl.ds(p * half, half), :] = dgo[half:]
         if p < rows:
             update_ref[p] = (go[:n] * y[:n]).astype(bf16)
             own_dgo.append(dgo[:n])
-        gate_grad += dot(zn, dgo, TN)
-        out_grad += dot(xn, dy, TN)[p * hidden : (p + 1) * hidden]
-        dxn += dot(dy, weight, NT)
+    dxn = dot(dy_ref[...], out_wide, NT)
+    out_grad = dot(xn, dy_ref[...], TN)
+    out_grad = [out_grad[p * hidden : (p + 1) * hidden, p * LANES : (p + 1) * LANES] for p in range(per)]
+    out_grad_ref[...] = sum(out_grad) / n
+    zn_tail = jnp.concatenate([zn_tail_ref[p] for p in range(per)], axis=0)
+    gate_grad = dot(znt_head_ref[...], dgo_head_ref[...]) + dot(zn_tail, dgo_tail_ref[...], TN)
     gate_grad_ref[...] = gate_grad / n
-    out_grad_ref[...] = out_grad / n
 
     u = out_gain * dxn
-    dx = xs * (u - dot_split(u, mean) - xhat * dot_split(u * xhat, mean))
+    dx = xs * (u - dot_split(u, mean_twice) - xhat * dot_split(u * xhat, mean_twice))
     dx = lanes(dx.astype(bf16))
 
-    dleft = jnp.zeros((n, wide), f32)
-    dright = []
     for g in range(groups):
         repeat = [zero_one(iota((hidden, n), 1) == row_of(g * per + p)) for p in range(per)]
         spread = dot(jnp.concatenate(repeat, axis=0), dx).astype(bf16)
-        diagonal = jnp.where(same, spread, jnp.zeros_like(spread))
-        dleft += dot(right[:, g * LANES : (g + 1) * LANES], diagonal)
-        dright.append(dot(left, diagonal, NT))
-    dleft = flatten(dleft.astype(bf16)).astype(f32)
-    dright = jnp.concatenate(dright, axis=0).astype(bf16).astype(f32)
+        square_ref[pl.ds(g * LANES, LANES), :] = jnp.where(same, spread, jnp.zeros_like(spread))
+    diagonal = square_ref[...]
+    dleft = flatten(dot(right, diagonal).astype(bf16)).astype(f32)
+    dright = flatten(dot(left, diagonal, NT).astype(bf16)).astype(f32)
     dleft, dright = dleft * mask_left, dright * mask_right
     dp = [
         dleft,
@@ -234,35 +257,54 @@
     hidden = output_weight.shape[0]
     f32, bf16 = jnp.float32, jnp.bfloat16
     half = rows * n
-    send = jnp.concatenate(
-        [pair_acts.reshape(half, channels), update_grad.reshape(half, channels)], axis=0
-    )
+    vmem, anywhere = pl.BlockSpec(memory_space=pltpu.VMEM), pl.BlockSpec(memory_space=pl.ANY)
+    shape = jax.ShapeDtypeStruct
+    sources = [
+        pair_acts.reshape(half, channels),
+        update_grad.reshape(half, channels),
+        input_gain[None],
+        input_bias[None],
+        project_weight.T,
+        gate_weight,
+        output_norm_gain[None],
+        output_shift_bias[None],
+        output_weight,
+    ]
+    send, gain, bias, project_t, gate_weight, out_gain, out_bias, out_weight = pl.pallas_call(
+        load_kernel,
+        out_shape=[pltpu.VMEM((2 * half, channels), bf16)] + [pltpu.VMEM(v.shape, v.dtype) for v in sources[2:]],
+        in_specs=[anywhere] * len(sources),
+        out_specs=[vmem] * (len(sources) - 1),
+        scratch_shapes=[pltpu.SemaphoreType.DMA((len(sources),))],
+        name="load",
+    )(*sources)
     blocks = {0: send}
     step = devices // 2
     while step:
         pairs = [(i, i ^ step) for i in range(devices)]
         blocks.update({d ^ step: lax.ppermute(blocks[d], "row", pairs) for d in list(blocks)})
         step //= 2
-    order = sorted(blocks, key=lambda d: (d & 2, d))
+    order = sorted(blocks, key=lambda d: (2 * (d >> 1).bit_count() + (d & 1), -d))
     ordered = [blocks[d] for d in order]
     per = LANES // hidden
     tall = n // per * n
-    vmem = pl.BlockSpec(memory_space=pltpu.VMEM)
-    shape = jax.ShapeDtypeStruct
-    gain, bias, project_t = input_gain[None], input_bias[None], project_weight.T
     head_blocks = ordered[: devices // 2]
+    head_out = (
+        pltpu.VMEM((per, tall // 2, channels), bf16),
+        pltpu.VMEM((tall // 2, KINDS * LANES), f32),
+        pltpu.VMEM((per, tall // 2, channels), f32),
+        pltpu.VMEM((channels, per * tall // 2), bf16),
+        pltpu.VMEM((KINDS * LANES, per * channels), bf16),
+        pltpu.VMEM((LANES, per * channels), bf16),
+    )
     head = pl.pallas_call(
         functools.partial(head_kernel, n),
-        out_shape=(
-            shape((per, tall // 2, channels), bf16),
-            shape((tall // 2, KINDS * LANES), f32),
-            shape((per, tall // 2, channels), f32),
-        ),
-        in_specs=[vmem] * (len(head_blocks) + 4),
-        out_specs=(vmem,) * 3,
+        out_shape=head_out,
+        in_specs=[vmem] * (len(head_blocks) + 5),
+        out_specs=(vmem,) * len(head_out),
         compiler_params=pltpu.CompilerParams(vmem_limit_bytes=16 << 20),
         name="head",
-    )(*head_blocks, gain, bias, project_t, gate_weight)
+    )(*head_blocks, gain, bias, project_t, gate_weight, out_weight)
     update, pair_grad, project_grad, gate_grad, output_grad = pl.pallas_call(
         functools.partial(tail_kernel, n, hidden, order),
         out_shape=(
@@ -272,26 +314,19 @@
             shape((channels, channels), f32),
             shape((hidden, channels), f32),
         ),
-        in_specs=[vmem] * (devices + 3) + [pl.BlockSpec(memory_space=pltpu.SMEM)] + [vmem] * 7,
+        in_specs=[vmem] * (devices + len(head_out)) + [pl.BlockSpec(memory_space=pltpu.SMEM)] + [vmem] * 6,
         out_specs=(vmem,) * 5,
         scratch_shapes=[
             pltpu.VMEM((per, tall // 2, channels), bf16),
             pltpu.VMEM((KINDS * LANES, tall), bf16),
+            pltpu.VMEM((n * hidden, n * hidden), bf16),
+            pltpu.VMEM((per * tall // 2, channels), bf16),
+            pltpu.VMEM((per * tall // 2, channels), bf16),
+            pltpu.VMEM((tall, per * channels), bf16),
         ],
         compiler_params=pltpu.CompilerParams(vmem_limit_bytes=32 << 20),
         name="tail",
-    )(
-        *ordered,
-        *head,
-        token_count,
-        gain,
-        bias,
-        project_t,
-        gate_weight,
-        output_norm_gain[None],
-        output_shift_bias[None],
-        output_weight,
-    )
+    )(*ordered, *head, token_count, gain, bias, project_t, gate_weight, out_gain, out_bias)
     return update, pair_grad, project_grad.T, gate_grad, output_grad
 
 

time: 28.3 us -> 25.9 us (0.915)
  local copies, waits for them, and re-layouts: 1.32 us -> 0 us
  starting transfers between devices: 16.2 us -> 17.5 us
  Pallas kernels: 7.97 us -> 6.84 us
  other arithmetic: 0.8 us -> 0 us
  waiting for transfers between devices: 0.36 us -> 0.04 us
    pallas_call x1, Pallas kernels: 7.05 us -> 4.96 us  [body_whole(): pl.pallas_call(functools.partial(tail_kernel, n, hidden, order), out_shap...]
    unnamed x14 -> x0, local copies, waits for them, and re-layouts: 1.32 us -> none
    ppermute x15, starting transfers between devices: 16.2 us -> 17.5 us  [body_whole(): lax.ppermute(blocks[d], 'row', pairs)]
    pallas_call x1 -> x2, Pallas kernels: 0.91 us -> 1.88 us  [the longest x1 0.95 us: body_whole(): pl.pallas_call(functools.partial(head_kernel, n), out_shape=head_out, in_...]
    concatenate x1 -> x0, other arithmetic: 0.8 us -> none  [body_whole(): jnp.concatenate([pair_acts.reshape(half, channels), update_grad.reshape(h...]
    ppermute x15, waiting for transfers between devices: 0.36 us -> 0.04 us  [body_whole(): lax.ppermute(blocks[d], 'row', pairs)]
  transfers between devices with their start and end apart: 15 -> 15, of which waited for: 1 -> 0; matrix products, arithmetic and copies ran while one was open for 0% -> 0% of each run, Pallas kernels for 3% -> 4%
where the time goes in v4:
time: 25.9 us; the launch traced here: 25.7 us
  starting transfers between devices  17.5 us (68%)
  Pallas kernels  6.84 us (26%)
  between operations  1.36 us (5%)
    ppermute x15, starting transfers between devices, body_whole(): lax.ppermute(blocks[d], 'row', pairs)  17.5 us
    pallas_call x1, Pallas kernels, body_whole(): pl.pallas_call(functools.partial(tail_kernel, n, hidden, order), out_shap...  4.96 us
    pallas_call x1, Pallas kernels, body_whole(): pl.pallas_call(functools.partial(head_kernel, n), out_shape=head_out, in_...  0.95 us
    pallas_call x1, Pallas kernels, body_whole(): pl.pallas_call(load_kernel, out_shape=[pltpu.VMEM((2 * half, channels), b...  0.93 us
  transfers between devices with their start and end apart: 15, of which 0 were waited for; matrix products, arithmetic and copies ran while one was open for 0% of the time, Pallas kernels for 4%

profile of v4, /device:TPU:1, one launch (start us, length us, event | category | flops | bytes accessed | tf_op | source)
XLA Modules:
  0.0 25.7 jit_solution(17169707228782970361)
XLA Ops:
  0.6 0.9 %load.1 = (bf16[288,128]{1,0:T(8,128)(2,1)S(1)}, f32[1,128]{1,0:T(1,128)S(1)}, f32[1,128]{1,0:T(1,128)S(1)}, bf16[64,128]{1,0:T(8,128)(2,1)S(1)}, bf16[128,128]{...) custom-call(bf16[144,128]{1,0:T(8,128)(2,1)} %bitcast.8, ...), custom_call_target="tpu_custom_call" | custom-call | tf_op jit(solution)/shard_map/load/pallas_call | solution.py:273
  1.6 3.2 %collective-permute-start.1 = (bf16[288,128]{1,0:T(8,128)(2,1)S(1)}, bf16[288,128]{1,0:T(8,128)(2,1)S(1)}, u32[]{:S(2)}, u32[]{:S(2)}) collective-permute-start(bf16[288,128]{1,0:T(8,128)(2,1)S(1)} %get-tuple-element.24.refs_0_), channel_id=1, source_target_pairs={{0,8},{1,9},{2,10},{3,11},{4,12},{5,13},{6,14},{7,15},{8,0},{9,1},... | collective-permute-start | bytes 221192 | tf_op jit(solution)/shard_map/ppermute | solution.py:285
  4.8 1.2 %collective-permute-start.3 = (bf16[288,128]{1,0:T(8,128)(2,1)S(1)}, bf16[288,128]{1,0:T(8,128)(2,1)S(1)}, u32[]{:S(2)}, u32[]{:S(2)}) collective-permute-start(bf16[288,128]{1,0:T(8,128)(2,1)S(1)} %get-tuple-element.24.refs_0_), channel_id=1, source_target_pairs={{0,2},{1,3},{2,0},{3,1},{4,6},{5,7},{6,4},{7,5},{8,10},{9,11},{10,... | collective-permute-start | bytes 221192 | tf_op jit(solution)/shard_map/ppermute | solution.py:285
  6.0 1.3 %collective-permute-start.2 = (bf16[288,128]{1,0:T(8,128)(2,1)S(1)}, bf16[288,128]{1,0:T(8,128)(2,1)S(1)}, u32[]{:S(2)}, u32[]{:S(2)}) collective-permute-start(bf16[288,128]{1,0:T(8,128)(2,1)S(1)} %get-tuple-element.24.refs_0_), channel_id=1, source_target_pairs={{0,4},{1,5},{2,6},{3,7},{4,0},{5,1},{6,2},{7,3},{8,12},{9,13},{10,... | collective-permute-start | bytes 221192 | tf_op jit(solution)/shard_map/ppermute | solution.py:285
  7.3 1.5 %collective-permute-start = (bf16[288,128]{1,0:T(8,128)(2,1)S(1)}, bf16[288,128]{1,0:T(8,128)(2,1)S(1)}, u32[]{:S(2)}, u32[]{:S(2)}) collective-permute-start(bf16[288,128]{1,0:T(8,128)(2,1)S(1)} %get-tuple-element.24.refs_0_), channel_id=1, source_target_pairs={{0,1},{1,0},{2,3},{3,2},{4,5},{5,4},{6,7},{7,6},{8,9},{9,8},{10,11... | collective-permute-start | bytes 221192 | tf_op jit(solution)/shard_map/ppermute | solution.py:285
  8.8 0.0 collective-permute-done.1.refs_2_
  8.8 0.5 %collective-permute-start.7 = (bf16[288,128]{1,0:T(8,128)(2,1)S(1)}, bf16[288,128]{1,0:T(8,128)(2,1)S(1)}, u32[]{:S(2)}, u32[]{:S(2)}) collective-permute-start(bf16[288,128]{1,0:T(8,128)(2,1)S(1)} %collective-permute-done.1.refs_2_), channel_id=1, source_target_pairs={{0,4},{1,5},{2,6},{3,7},{4,0},{5,1},{6,2},{7,3},{8,12},{9,13},{10,... | collective-permute-start | bytes 221192 | tf_op jit(solution)/shard_map/ppermute | solution.py:285
  9.3 0.0 collective-permute-done.3.refs_4_
  9.3 1.2 %collective-permute-start.6 = (bf16[288,128]{1,0:T(8,128)(2,1)S(1)}, bf16[288,128]{1,0:T(8,128)(2,1)S(1)}, u32[]{:S(2)}, u32[]{:S(2)}) collective-permute-start(bf16[288,128]{1,0:T(8,128)(2,1)S(1)} %collective-permute-done.3.refs_4_), channel_id=1, source_target_pairs={{0,1},{1,0},{2,3},{3,2},{4,5},{5,4},{6,7},{7,6},{8,9},{9,8},{10,11... | collective-permute-start | bytes 221192 | tf_op jit(solution)/shard_map/ppermute | solution.py:285
  10.5 1.1 %collective-permute-start.9 = (bf16[288,128]{1,0:T(8,128)(2,1)S(1)}, bf16[288,128]{1,0:T(8,128)(2,1)S(1)}, u32[]{:S(2)}, u32[]{:S(2)}) collective-permute-start(bf16[288,128]{1,0:T(8,128)(2,1)S(1)} %collective-permute-done.2.refs_3_), channel_id=1, source_target_pairs={{0,2},{1,3},{2,0},{3,1},{4,6},{5,7},{6,4},{7,5},{8,10},{9,11},{10,... | collective-permute-start | bytes 221192 | tf_op jit(solution)/shard_map/ppermute | solution.py:285
  11.6 0.5 %collective-permute-start.5 = (bf16[288,128]{1,0:T(8,128)(2,1)S(1)}, bf16[288,128]{1,0:T(8,128)(2,1)S(1)}, u32[]{:S(2)}, u32[]{:S(2)}) collective-permute-start(bf16[288,128]{1,0:T(8,128)(2,1)S(1)} %collective-permute-done.2.refs_3_), channel_id=1, source_target_pairs={{0,1},{1,0},{2,3},{3,2},{4,5},{5,4},{6,7},{7,6},{8,9},{9,8},{10,11... | collective-permute-start | bytes 221192 | tf_op jit(solution)/shard_map/ppermute | solution.py:285
  12.1 0.0 collective-permute-done.refs_1_
  12.1 1.2 %collective-permute-start.8 = (bf16[288,128]{1,0:T(8,128)(2,1)S(1)}, bf16[288,128]{1,0:T(8,128)(2,1)S(1)}, u32[]{:S(2)}, u32[]{:S(2)}) collective-permute-start(bf16[288,128]{1,0:T(8,128)(2,1)S(1)} %collective-permute-done.1.refs_2_), channel_id=1, source_target_pairs={{0,2},{1,3},{2,0},{3,1},{4,6},{5,7},{6,4},{7,5},{8,10},{9,11},{10,... | collective-permute-start | bytes 221192 | tf_op jit(solution)/shard_map/ppermute | solution.py:285
  13.3 0.0 collective-permute-done.7.refs_8_
  13.3 0.3 collective-permute-start.13
  13.6 1.7 %collective-permute-start.4 = (bf16[288,128]{1,0:T(8,128)(2,1)S(1)}, bf16[288,128]{1,0:T(8,128)(2,1)S(1)}, u32[]{:S(2)}, u32[]{:S(2)}) collective-permute-start(bf16[288,128]{1,0:T(8,128)(2,1)S(1)} %collective-permute-done.1.refs_2_), channel_id=1, source_target_pairs={{0,1},{1,0},{2,3},{3,2},{4,5},{5,4},{6,7},{7,6},{8,9},{9,8},{10,11... | collective-permute-start | bytes 221192 | tf_op jit(solution)/shard_map/ppermute | solution.py:285
  15.3 1.3 %collective-permute-start.10 = (bf16[288,128]{1,0:T(8,128)(2,1)S(1)}, bf16[288,128]{1,0:T(8,128)(2,1)S(1)}, u32[]{:S(2)}, u32[]{:S(2)}) collective-permute-start(bf16[288,128]{1,0:T(8,128)(2,1)S(1)} %collective-permute-done.7.refs_8_), channel_id=1, source_target_pairs={{0,1},{1,0},{2,3},{3,2},{4,5},{5,4},{6,7},{7,6},{8,9},{9,8},{10,11... | collective-permute-start | bytes 221192 | tf_op jit(solution)/shard_map/ppermute | solution.py:285
  16.6 0.0 collective-permute-done.5.refs_6_
  16.6 0.0 collective-permute-start.12
  16.7 1.6 %collective-permute-start.11 = (bf16[288,128]{1,0:T(8,128)(2,1)S(1)}, bf16[288,128]{1,0:T(8,128)(2,1)S(1)}, u32[]{:S(2)}, u32[]{:S(2)}) collective-permute-start(bf16[288,128]{1,0:T(8,128)(2,1)S(1)} %collective-permute-done.8.refs_9_), channel_id=1, source_target_pairs={{0,1},{1,0},{2,3},{3,2},{4,5},{5,4},{6,7},{7,6},{8,9},{9,8},{10,11... | collective-permute-start | bytes 221192 | tf_op jit(solution)/shard_map/ppermute | solution.py:285
  18.2 0.0 collective-permute-done.13.refs_14_
  18.2 0.9 %collective-permute-start.14 = (bf16[288,128]{1,0:T(8,128)(2,1)S(1)}, bf16[288,128]{1,0:T(8,128)(2,1)S(1)}, u32[]{:S(2)}, u32[]{:S(2)}) collective-permute-start(bf16[288,128]{1,0:T(8,128)(2,1)S(1)} %collective-permute-done.13.refs_14_), channel_id=1, source_target_pairs={{0,1},{1,0},{2,3},{3,2},{4,5},{5,4},{6,7},{7,6},{8,9},{9,8},{10,11... | collective-permute-start | bytes 221192 | tf_op jit(solution)/shard_map/ppermute | solution.py:285
  19.8 0.9 %head.1 = (bf16[8,144,128]{2,1,0:T(8,128)(2,1)S(1)}, f32[144,512]{1,0:T(8,128)S(1)}, f32[8,144,128]{2,1,0:T(8,128)S(1)}, bf16[128,1152]{1,0:T(8,128)(2,1)S(1)}, ...) custom-call(bf16[288,128]{1,0:T(8,128)(2,1)S(1)} %get-tuple-element.24.refs_0_, ...), custom_call_target="tpu_custom_call" | custom-call | tf_op jit(solution)/shard_map/head/pallas_call | solution.py:300
  20.8 5.0 %tail.1 = (bf16[3,48,128]{2,1,0:T(8,128)(2,1)}, f32[3,48,128]{2,1,0:T(8,128)}, f32[64,128]{1,0:T(8,128)}, f32[128,128]{1,0:T(8,128)}, f32[16,128]{1,0:T(8,128)}) custom-call(bf16[288,128]{1,0:T(8,128)(2,1)S(1)} %get-tuple-element.24.refs_0_, bf16[288,128]{1,0:T(8,128)(2,1)S(1)} %collective-permute-done.refs_1_, ...), custom_call_target="tpu_custom_call" | custom-call | tf_op jit(solution)/shard_map/tail/pallas_call | solution.py:308
  (9 shorter events, 0.0 us)
Async XLA Ops:
  1.6 7.2 %collective-permute-start.1 = (bf16[288,128]{1,0:T(8,128)(2,1)S(1)}, bf16[288,128]{1,0:T(8,128)(2,1)S(1)}, u32[]{:S(2)}, u32[]{:S(2)}) collective-permute-start(bf16[288,128]{1,0:T(8,128)(2,1)S(1)} %get-tuple-element.24.refs_0_), channel_id=1, source_target_pairs={{0,8},{1,9},{2,10},{3,11},{4,12},{5,13},{6,14},{7,15},{8,0},{9,1},... | collective-permute-start | bytes 221192 | tf_op jit(solution)/shard_map/ppermute | solution.py:285
  4.8 4.5 %collective-permute-start.3 = (bf16[288,128]{1,0:T(8,128)(2,1)S(1)}, bf16[288,128]{1,0:T(8,128)(2,1)S(1)}, u32[]{:S(2)}, u32[]{:S(2)}) collective-permute-start(bf16[288,128]{1,0:T(8,128)(2,1)S(1)} %get-tuple-element.24.refs_0_), channel_id=1, source_target_pairs={{0,2},{1,3},{2,0},{3,1},{4,6},{5,7},{6,4},{7,5},{8,10},{9,11},{10,... | collective-permute-start | bytes 221192 | tf_op jit(solution)/shard_map/ppermute | solution.py:285
  6.0 4.5 %collective-permute-start.2 = (bf16[288,128]{1,0:T(8,128)(2,1)S(1)}, bf16[288,128]{1,0:T(8,128)(2,1)S(1)}, u32[]{:S(2)}, u32[]{:S(2)}) collective-permute-start(bf16[288,128]{1,0:T(8,128)(2,1)S(1)} %get-tuple-element.24.refs_0_), channel_id=1, source_target_pairs={{0,4},{1,5},{2,6},{3,7},{4,0},{5,1},{6,2},{7,3},{8,12},{9,13},{10,... | collective-permute-start | bytes 221192 | tf_op jit(solution)/shard_map/ppermute | solution.py:285
  7.3 4.8 %collective-permute-start = (bf16[288,128]{1,0:T(8,128)(2,1)S(1)}, bf16[288,128]{1,0:T(8,128)(2,1)S(1)}, u32[]{:S(2)}, u32[]{:S(2)}) collective-permute-start(bf16[288,128]{1,0:T(8,128)(2,1)S(1)} %get-tuple-element.24.refs_0_), channel_id=1, source_target_pairs={{0,1},{1,0},{2,3},{3,2},{4,5},{5,4},{6,7},{7,6},{8,9},{9,8},{10,11... | collective-permute-start | bytes 221192 | tf_op jit(solution)/shard_map/ppermute | solution.py:285
  8.8 4.5 %collective-permute-start.7 = (bf16[288,128]{1,0:T(8,128)(2,1)S(1)}, bf16[288,128]{1,0:T(8,128)(2,1)S(1)}, u32[]{:S(2)}, u32[]{:S(2)}) collective-permute-start(bf16[288,128]{1,0:T(8,128)(2,1)S(1)} %collective-permute-done.1.refs_2_), channel_id=1, source_target_pairs={{0,4},{1,5},{2,6},{3,7},{4,0},{5,1},{6,2},{7,3},{8,12},{9,13},{10,... | collective-permute-start | bytes 221192 | tf_op jit(solution)/shard_map/ppermute | solution.py:285
  9.3 4.3 %collective-permute-start.6 = (bf16[288,128]{1,0:T(8,128)(2,1)S(1)}, bf16[288,128]{1,0:T(8,128)(2,1)S(1)}, u32[]{:S(2)}, u32[]{:S(2)}) collective-permute-start(bf16[288,128]{1,0:T(8,128)(2,1)S(1)} %collective-permute-done.3.refs_4_), channel_id=1, source_target_pairs={{0,1},{1,0},{2,3},{3,2},{4,5},{5,4},{6,7},{7,6},{8,9},{9,8},{10,11... | collective-permute-start | bytes 221192 | tf_op jit(solution)/shard_map/ppermute | solution.py:285
  10.5 4.8 %collective-permute-start.9 = (bf16[288,128]{1,0:T(8,128)(2,1)S(1)}, bf16[288,128]{1,0:T(8,128)(2,1)S(1)}, u32[]{:S(2)}, u32[]{:S(2)}) collective-permute-start(bf16[288,128]{1,0:T(8,128)(2,1)S(1)} %collective-permute-done.2.refs_3_), channel_id=1, source_target_pairs={{0,2},{1,3},{2,0},{3,1},{4,6},{5,7},{6,4},{7,5},{8,10},{9,11},{10,... | collective-permute-start | bytes 221192 | tf_op jit(solution)/shard_map/ppermute | solution.py:285
  11.6 5.0 %collective-permute-start.5 = (bf16[288,128]{1,0:T(8,128)(2,1)S(1)}, bf16[288,128]{1,0:T(8,128)(2,1)S(1)}, u32[]{:S(2)}, u32[]{:S(2)}) collective-permute-start(bf16[288,128]{1,0:T(8,128)(2,1)S(1)} %collective-permute-done.2.refs_3_), channel_id=1, source_target_pairs={{0,1},{1,0},{2,3},{3,2},{4,5},{5,4},{6,7},{7,6},{8,9},{9,8},{10,11... | collective-permute-start | bytes 221192 | tf_op jit(solution)/shard_map/ppermute | solution.py:285
  12.1 4.5 %collective-permute-start.8 = (bf16[288,128]{1,0:T(8,128)(2,1)S(1)}, bf16[288,128]{1,0:T(8,128)(2,1)S(1)}, u32[]{:S(2)}, u32[]{:S(2)}) collective-permute-start(bf16[288,128]{1,0:T(8,128)(2,1)S(1)} %collective-permute-done.1.refs_2_), channel_id=1, source_target_pairs={{0,2},{1,3},{2,0},{3,1},{4,6},{5,7},{6,4},{7,5},{8,10},{9,11},{10,... | collective-permute-start | bytes 221192 | tf_op jit(solution)/shard_map/ppermute | solution.py:285
  13.3 4.9 %collective-permute-start.13 = (bf16[288,128]{1,0:T(8,128)(2,1)S(1)}, bf16[288,128]{1,0:T(8,128)(2,1)S(1)}, u32[]{:S(2)}, u32[]{:S(2)}) collective-permute-start(bf16[288,128]{1,0:T(8,128)(2,1)S(1)} %collective-permute-done.7.refs_8_), channel_id=1, source_target_pairs={{0,2},{1,3},{2,0},{3,1},{4,6},{5,7},{6,4},{7,5},{8,10},{9,11},{10,... | collective-permute-start | bytes 221192 | tf_op jit(solution)/shard_map/ppermute | solution.py:285
  13.6 6.2 %collective-permute-start.4 = (bf16[288,128]{1,0:T(8,128)(2,1)S(1)}, bf16[288,128]{1,0:T(8,128)(2,1)S(1)}, u32[]{:S(2)}, u32[]{:S(2)}) collective-permute-start(bf16[288,128]{1,0:T(8,128)(2,1)S(1)} %collective-permute-done.1.refs_2_), channel_id=1, source_target_pairs={{0,1},{1,0},{2,3},{3,2},{4,5},{5,4},{6,7},{7,6},{8,9},{9,8},{10,11... | collective-permute-start | bytes 221192 | tf_op jit(solution)/shard_map/ppermute | solution.py:285
  15.3 5.4 %collective-permute-start.10 = (bf16[288,128]{1,0:T(8,128)(2,1)S(1)}, bf16[288,128]{1,0:T(8,128)(2,1)S(1)}, u32[]{:S(2)}, u32[]{:S(2)}) collective-permute-start(bf16[288,128]{1,0:T(8,128)(2,1)S(1)} %collective-permute-done.7.refs_8_), channel_id=1, source_target_pairs={{0,1},{1,0},{2,3},{3,2},{4,5},{5,4},{6,7},{7,6},{8,9},{9,8},{10,11... | collective-permute-start | bytes 221192 | tf_op jit(solution)/shard_map/ppermute | solution.py:285
  16.6 4.1 %collective-permute-start.12 = (bf16[288,128]{1,0:T(8,128)(2,1)S(1)}, bf16[288,128]{1,0:T(8,128)(2,1)S(1)}, u32[]{:S(2)}, u32[]{:S(2)}) collective-permute-start(bf16[288,128]{1,0:T(8,128)(2,1)S(1)} %collective-permute-done.9.refs_10_), channel_id=1, source_target_pairs={{0,1},{1,0},{2,3},{3,2},{4,5},{5,4},{6,7},{7,6},{8,9},{9,8},{10,11... | collective-permute-start | bytes 221192 | tf_op jit(solution)/shard_map/ppermute | solution.py:285
  16.7 4.1 %collective-permute-start.11 = (bf16[288,128]{1,0:T(8,128)(2,1)S(1)}, bf16[288,128]{1,0:T(8,128)(2,1)S(1)}, u32[]{:S(2)}, u32[]{:S(2)}) collective-permute-start(bf16[288,128]{1,0:T(8,128)(2,1)S(1)} %collective-permute-done.8.refs_9_), channel_id=1, source_target_pairs={{0,1},{1,0},{2,3},{3,2},{4,5},{5,4},{6,7},{7,6},{8,9},{9,8},{10,11... | collective-permute-start | bytes 221192 | tf_op jit(solution)/shard_map/ppermute | solution.py:285
  18.2 2.5 %collective-permute-start.14 = (bf16[288,128]{1,0:T(8,128)(2,1)S(1)}, bf16[288,128]{1,0:T(8,128)(2,1)S(1)}, u32[]{:S(2)}, u32[]{:S(2)}) collective-permute-start(bf16[288,128]{1,0:T(8,128)(2,1)S(1)} %collective-permute-done.13.refs_14_), channel_id=1, source_target_pairs={{0,1},{1,0},{2,3},{3,2},{4,5},{5,4},{6,7},{7,6},{8,9},{9,8},{10,11... | collective-permute-start | bytes 221192 | tf_op jit(solution)/shard_map/ppermute | solution.py:285

commit v5 on v4

--- a/solution.py
+++ b/solution.py
@@ -44,12 +44,62 @@
     return centered * s, s
 
 
-def norm_tiles(n, block_refs, gain, bias, zn_ref):
-    per = zn_ref.shape[0]
-    rows = block_refs[0].shape[0] // (2 * n)
-    for t in range(len(block_refs) * rows):
-        v = block_refs[t // rows][pl.ds(t % rows * n, n), :].astype(jnp.float32)
-        zn_ref[t % per, pl.ds(t // per * n, n), :] = (normalize(v)[0] * gain + bias).astype(jnp.bfloat16)
+def row_of(order, rows, t):
+    return (lax.axis_index("row") ^ order[t // rows]) * rows + t % rows
+
+
+def rows_of_lanes(order, rows, hidden, group):
+    per = LANES // hidden
+    place = iota((1, LANES), 1) // hidden
+    at = jnp.full((1, LANES), row_of(order, rows, group * per), jnp.int32)
+    for p in range(1, per):
+        at = jnp.where(place == p, row_of(order, rows, group * per + p), at)
+    return at
+
+
+def stage(n, hidden, order, first, block_refs, count, gain, bias, project_wide, out_wide, gate_weight, refs):
+    left_ref, right_ref, mask_ref, slope_ref, dy_ref, dgo_part_ref, dxn_ref, znt_ref = refs
+    f32, bf16 = jnp.float32, jnp.bfloat16
+    per = LANES // hidden
+    rows = n // len(order)
+    tall = left_ref.shape[0]
+    start = first * per
+    zn, cotangent = {}, {}
+    for t in range(start, start + per * (tall // n)):
+        block, at = block_refs[t // rows - start // rows], t % rows * n
+        zn[t] = (normalize(block[pl.ds(at, n), :].astype(f32))[0] * gain + bias).astype(bf16)
+        cotangent[t] = block[pl.ds((rows + t % rows) * n, n), :]
+
+    def place(tiles, p):
+        return jnp.concatenate([tiles[t] for t in range(start + p, start + per * (tall // n), per)], axis=0)
+
+    zn = [place(zn, p) for p in range(per)]
+    projected = dot(jnp.concatenate(zn, axis=1), project_wide, NT)
+    live_k = iota((n, LANES), 0) < count
+    mask = [
+        jnp.where(live_k & (rows_of_lanes(order, rows, hidden, first + g) < count), 1.0, 0.0) for g in range(tall // n)
+    ]
+    mask = jnp.concatenate(mask, axis=0)
+    for side, ref in enumerate((left_ref, right_ref)):
+        value = projected[:, 2 * side * LANES : (2 * side + 1) * LANES]
+        gate = sigmoid(projected[:, (2 * side + 1) * LANES : (2 * side + 2) * LANES])
+        ref[...] = (mask * gate * value).astype(bf16)
+        mask_ref[side] = mask * gate
+        slope_ref[side] = value * (1.0 - gate)
+    own = []
+    zn_tall = jnp.concatenate(zn, axis=0)
+    gates = sigmoid(dot(zn_tall, gate_weight))
+    for p in range(per):
+        go = gates[p * tall : (p + 1) * tall]
+        dy = place(cotangent, p).astype(f32) * go
+        dy_ref[:, p * LANES : (p + 1) * LANES] = dy.astype(bf16)
+        dgo_part_ref[p] = dy * (1.0 - go)
+        own.append(go[:n])
+    dxn_ref[...] = dot(dy_ref[...], out_wide, NT)
+    half = per // 2 * tall
+    znt_ref[0] = zn_tall[:half].T
+    znt_ref[1] = zn_tall[half:].T
+    return own
 
 
 def wide_project(project_t, per):
@@ -76,8 +126,12 @@
     return jnp.concatenate(rows, axis=0)
 
 
-def side_by_side(ref):
-    return jnp.concatenate([ref[p] for p in range(ref.shape[0])], axis=1)
+def pick_place(per, hidden):
+    half, width = per // 2, KINDS * hidden
+    a, b = iota((KINDS * LANES, LANES), 0), iota((KINDS * LANES, LANES), 1)
+    own = (a // LANES == b % width // hidden) & (a % hidden == b % hidden)
+    place = a % LANES // hidden
+    return jnp.concatenate([zero_one(own & (place == b // width * half + q)) for q in range(half)], axis=1)
 
 
 def load_kernel(*refs):
@@ -92,64 +146,58 @@
         copy.wait()
 
 
-def head_kernel(n, *refs):
-    *block_refs, gain_ref, bias_ref, project_ref, gate_ref, out_weight_ref = refs[:-6]
-    zn_ref, projected_ref, go_ref, znt_ref, project_wide_ref, out_wide_ref = refs[-6:]
-    per = zn_ref.shape[0]
-    norm_tiles(n, block_refs, gain_ref[...], bias_ref[...], zn_ref)
+def head_kernel(n, hidden, order, *refs):
+    *block_refs, count_ref, gain_ref, bias_ref, project_ref, gate_ref, out_weight_ref = refs[:-12]
+    *stage_refs, project_wide_ref, out_wide_ref, pick_ref, own_ref = refs[-12:]
+    per = LANES // hidden
     project_wide_ref[...] = wide_project(project_ref[...], per)
     out_wide_ref[...] = wide_out(out_weight_ref[...], per)
-    projected_ref[...] = dot(side_by_side(zn_ref), project_wide_ref[...], NT)
-    gate_weight = gate_ref[...]
-    for p in range(per):
-        go_ref[p] = sigmoid(dot(zn_ref[p], gate_weight))
-    znt_ref[...] = jnp.concatenate([zn_ref[p] for p in range(per)], axis=0).T
-
-
-def tail_kernel(n, hidden, order, *refs):
+    pick_ref[...] = pick_place(per, hidden)
+    weights = [ref[...] for ref in (gain_ref, bias_ref, project_wide_ref, out_wide_ref, gate_ref)]
+    own = stage(n, hidden, order, 0, block_refs, count_ref[0], *weights, stage_refs)
+    for r in range(own_ref.shape[0]):
+        own_ref[r] = own[r]
+
+
+def middle_kernel(n, hidden, order, first, *refs):
+    *block_refs, count_ref, gain_ref, bias_ref, project_wide_ref, out_wide_ref, gate_ref = refs[:-8]
+    weights = [ref[...] for ref in (gain_ref, bias_ref, project_wide_ref, out_wide_ref, gate_ref)]
+    stage(n, hidden, order, first, block_refs, count_ref[0], *weights, refs[-8:])
+
+
+def tail_kernel(n, hidden, order, cuts, *refs):
     blocks = len(order)
     block_refs, refs = refs[:blocks], refs[blocks:]
-    zn_head_ref, projected_head_ref, go_head_ref, znt_head_ref, project_wide_ref, out_wide_ref = refs[:6]
-    count_ref, gain_ref, bias_ref, project_ref, gate_ref, out_gain_ref, out_bias_ref = refs[6:13]
-    update_ref, pair_ref, project_grad_ref, gate_grad_ref, out_grad_ref = refs[13:18]
-    zn_tail_ref, dpt_ref, square_ref, dgo_head_ref, dgo_tail_ref, dy_ref = refs[18:]
+    head_refs, (project_wide_ref, out_wide_ref, pick_ref, own_ref), middle_refs = refs[:8], refs[8:12], refs[12:20]
+    count_ref, gain_ref, bias_ref, project_ref, gate_ref, out_gain_ref, out_bias_ref = refs[20:27]
+    update_ref, pair_ref, project_grad_ref, gate_grad_ref, out_grad_ref = refs[27:32]
+    tail_refs, (square_ref, dgo_ref, dp_ref, dx_ref) = refs[32:40], refs[40:]
+    stages = (head_refs, middle_refs, tail_refs)
     f32, bf16 = jnp.float32, jnp.bfloat16
     per = LANES // hidden
     groups = n // per
     wide = n * hidden
     rows = n // blocks
-    me = lax.axis_index("row")
-    count = count_ref[0]
-    gain, bias = gain_ref[...], bias_ref[...]
-    gate_weight = gate_ref[...]
-    project_t = project_ref[...]
-
-    def row_of(t):
-        return (me ^ order[t // rows]) * rows + t % rows
-
-    def tiles(p):
-        return [(t // rows, t % rows * n) for t in range(p, n, per)]
-
-    norm_tiles(n, block_refs[blocks // 2 :], gain, bias, zn_tail_ref)
-
-    def zn_of(p):
-        return jnp.concatenate([zn_head_ref[p], zn_tail_ref[p]], axis=0)
-
-    projected = jnp.concatenate([projected_head_ref[...], dot(side_by_side(zn_tail_ref), project_wide_ref[...], NT)], axis=0)
-
-    place = iota((1, LANES), 1) // hidden
-    row_i = []
-    for g in range(groups):
-        at = jnp.full((1, LANES), row_of(g * per), jnp.int32)
-        for p in range(1, per):
-            at = jnp.where(place == p, row_of(g * per + p), at)
-        row_i.append(at)
-    live_k = iota((n, LANES), 0) < count
-    mask = jnp.concatenate([jnp.where(live_k & (at < count), 1.0, 0.0) for at in row_i], axis=0)
-    value_left, value_right = projected[:, :LANES], projected[:, 2 * LANES : 3 * LANES]
-    gate_left = sigmoid(projected[:, LANES : 2 * LANES])
-    gate_right = sigmoid(projected[:, 3 * LANES :])
-    mask_left, mask_right = mask * gate_left, mask * gate_right
+    gain, gate_weight, project_t = gain_ref[...], gate_ref[...], project_ref[...]
+    weights = gain, bias_ref[...], project_wide_ref[...], out_wide_ref[...], gate_weight
+    stage(n, hidden, order, cuts[1], block_refs[cuts[1] * per // rows :], count_ref[0], *weights, tail_refs)
+
+    spans = [(low * n, high * n) for low, high in zip((0, *cuts), (*cuts, groups))]
+    half = per // 2
+
+    def put(ref, q, column, value):
+        for low, high in spans:
+            ref[pl.ds(low * half + q * (high - low), high - low), pl.ds(column, LANES)] = value[low:high]
+
+    def sum_pairs(ref):
+        znt = [refs[7][...].reshape(2 * LANES, half * (high - low)) for refs, (low, high) in zip(stages, spans)]
+        rows_of = [ref[pl.ds(low * half, (high - low) * half), :] for low, high in spans]
+        return sum(dot(a, b) for a, b in zip(znt, rows_of))
+
+    def all_rows(k):
+        return jnp.concatenate([refs[k][...] for refs in stages], axis=0)
+
+    row_i = [rows_of_lanes(order, rows, hidden, g) for g in range(groups)]
 
     def lanes(flat):
         return jnp.concatenate([flat[g * n : (g + 1) * n] for g in range(groups)], axis=1)
@@ -157,13 +205,16 @@
     def flatten(rowed):
         return jnp.concatenate([rowed[:, g * LANES : (g + 1) * LANES] for g in range(groups)], axis=0)
 
-    left = lanes((mask_left * value_left).astype(bf16))
-    right = lanes((mask_right * value_right).astype(bf16))
+    left, right = lanes(all_rows(0)), lanes(all_rows(1))
 
     same = iota((LANES, wide), 0) % hidden == iota((LANES, wide), 1) % hidden
-    for g in range(groups):
-        cross = dot(right[:, g * LANES : (g + 1) * LANES], left, TN).astype(bf16)
-        square_ref[pl.ds(g * LANES, LANES), :] = jnp.where(same, cross, jnp.zeros_like(cross))
+
+    def keep_same(square):
+        for g in range(groups):
+            part = square[g * LANES : (g + 1) * LANES].astype(bf16)
+            square_ref[pl.ds(g * LANES, LANES), :] = jnp.where(same, part, jnp.zeros_like(part))
+
+    keep_same(dot(right, left, TN))
     pick = jnp.concatenate([zero_one(iota((n, LANES), 0) == at) for at in row_i], axis=1)
     x = flatten(dot(pick, square_ref[...]))
 
@@ -177,67 +228,56 @@
     xhat = centered * xs
     xn = (xhat * out_gain + out_bias).astype(bf16)
 
-    out_wide = out_wide_ref[...]
-    y_all = dot(xn, out_wide)
+    y_all = dot(xn, out_wide_ref[...])
     own_dgo = []
-    half = groups // 2 * n
     for p in range(per):
         y = y_all[:, p * LANES : (p + 1) * LANES]
-        go = jnp.concatenate([go_head_ref[p], sigmoid(dot(zn_tail_ref[p], gate_weight))], axis=0)
-        ug = [block_refs[b][pl.ds(rows * n + start, n), :] for b, start in tiles(p)]
-        dy = jnp.concatenate(ug, axis=0).astype(f32) * go
-        dgo = (dy * y * (1.0 - go)).astype(bf16)
-        dy_ref[:, p * LANES : (p + 1) * LANES] = dy.astype(bf16)
-        dgo_head_ref[pl.ds(p * half, half), :] = dgo[:half]
-        dgo_tail_ref[pl.ds(p * half, half), :] = dgo[half:]
+        dgo = (jnp.concatenate([refs[5][p] for refs in stages], axis=0) * y).astype(bf16)
+        put(dgo_ref, p % half, p // half * LANES, dgo)
         if p < rows:
-            update_ref[p] = (go[:n] * y[:n]).astype(bf16)
+            update_ref[p] = (own_ref[p] * y[:n]).astype(bf16)
             own_dgo.append(dgo[:n])
-    dxn = dot(dy_ref[...], out_wide, NT)
-    out_grad = dot(xn, dy_ref[...], TN)
+    out_grad = dot(xn, all_rows(4), TN)
     out_grad = [out_grad[p * hidden : (p + 1) * hidden, p * LANES : (p + 1) * LANES] for p in range(per)]
     out_grad_ref[...] = sum(out_grad) / n
-    zn_tail = jnp.concatenate([zn_tail_ref[p] for p in range(per)], axis=0)
-    gate_grad = dot(znt_head_ref[...], dgo_head_ref[...]) + dot(zn_tail, dgo_tail_ref[...], TN)
-    gate_grad_ref[...] = gate_grad / n
-
-    u = out_gain * dxn
+    gate_grad = sum_pairs(dgo_ref)
+    gate_grad_ref[...] = (gate_grad[:LANES, :LANES] + gate_grad[LANES:, LANES:]) / n
+
+    u = out_gain * all_rows(6)
     dx = xs * (u - dot_split(u, mean_twice) - xhat * dot_split(u * xhat, mean_twice))
-    dx = lanes(dx.astype(bf16))
-
-    for g in range(groups):
-        repeat = [zero_one(iota((hidden, n), 1) == row_of(g * per + p)) for p in range(per)]
-        spread = dot(jnp.concatenate(repeat, axis=0), dx).astype(bf16)
-        square_ref[pl.ds(g * LANES, LANES), :] = jnp.where(same, spread, jnp.zeros_like(spread))
+    dx_ref[...] = lanes(dx.astype(bf16)).astype(f32)
+
+    for t in range(n):
+        row = dx_ref[pl.ds(row_of(order, rows, t), 1), :]
+        row = jnp.broadcast_to(row, (hidden, wide)).astype(bf16)
+        square_ref[pl.ds(t * hidden, hidden), :] = jnp.where(same[:hidden], row, jnp.zeros_like(row))
     diagonal = square_ref[...]
     dleft = flatten(dot(right, diagonal).astype(bf16)).astype(f32)
     dright = flatten(dot(left, diagonal, NT).astype(bf16)).astype(f32)
-    dleft, dright = dleft * mask_left, dright * mask_right
-    dp = [
-        dleft,
-        dleft * value_left * (1.0 - gate_left),
-        dright,
-        dright * value_right * (1.0 - gate_right),
-    ]
+    dp = []
+    for side, grad in enumerate((dleft, dright)):
+        masked = grad * jnp.concatenate([refs[2][side] for refs in stages], axis=0)
+        dp += [masked, masked * jnp.concatenate([refs[3][side] for refs in stages], axis=0)]
     dp = jnp.concatenate([d.astype(bf16) for d in dp], axis=1)
-    dpt_ref[...] = dp.T
-    project_grad = jnp.zeros((KINDS * hidden, LANES), f32)
-    for p in range(per):
-        at_p = [dpt_ref[pl.ds(kind * LANES + p * hidden, hidden), :] for kind in range(KINDS)]
-        project_grad += dot(jnp.concatenate(at_p, axis=0), zn_of(p))
-    project_grad_ref[...] = project_grad / n
+    by_place = dot(dp, pick_ref[...]).astype(bf16)
+    for q in range(half):
+        put(dp_ref, q, 0, by_place[:, q * LANES : (q + 1) * LANES])
+    project_grad = sum_pairs(dp_ref).T
+    width = KINDS * hidden
+    project_grad_ref[...] = (project_grad[:width, :LANES] + project_grad[width:, LANES:]) / n
 
     tiled = [project_t[kind * hidden : (kind + 1) * hidden] for kind in range(KINDS) for _ in range(per)]
-    tiled = jnp.concatenate(tiled, axis=0)
     place = iota((n, KINDS * LANES), 1) % LANES // hidden
+    dp_rows = [jnp.where(place == r, dp[:n], jnp.zeros_like(dp[:n])) for r in range(rows)]
+    dzn = dot(jnp.concatenate(dp_rows, axis=0), jnp.concatenate(tiled, axis=0))
+    dzn += dot(jnp.concatenate(own_dgo, axis=0), gate_weight, NT)
+    zhat, zs = normalize(block_refs[0][pl.ds(0, rows * n), :].astype(f32))
+    u = gain * dzn
+    first = jnp.mean(u, axis=-1, keepdims=True)
+    second = jnp.mean(u * zhat, axis=-1, keepdims=True)
+    pair_grad = zs * (u - first - zhat * second)
     for r in range(rows):
-        dp_row = jnp.where(place == r, dp[:n], jnp.zeros_like(dp[:n]))
-        dzn = dot(dp_row, tiled) + dot(own_dgo[r], gate_weight, NT)
-        zhat, zs = normalize(block_refs[0][pl.ds(r * n, n), :].astype(f32))
-        u = gain * dzn
-        first = jnp.mean(u, axis=-1, keepdims=True)
-        second = jnp.mean(u * zhat, axis=-1, keepdims=True)
-        pair_ref[r] = zs * (u - first - zhat * second)
+        pair_ref[r] = pair_grad[r * n : (r + 1) * n]
 
 
 def body_whole(
@@ -279,34 +319,77 @@
         name="load",
     )(*sources)
     blocks = {0: send}
-    step = devices // 2
-    while step:
+    core, x, *z = [1 << bit for bit in range(devices.bit_length() - 1)]
+
+    def hop(step, sources):
         pairs = [(i, i ^ step) for i in range(devices)]
-        blocks.update({d ^ step: lax.ppermute(blocks[d], "row", pairs) for d in list(blocks)})
-        step //= 2
-    order = sorted(blocks, key=lambda d: (2 * (d >> 1).bit_count() + (d & 1), -d))
+        for d in sources:
+            blocks[d ^ step] = lax.ppermute(blocks[d], "row", pairs)
+
+    for step in reversed(z):
+        hop(step, [0])
+    hop(x, [0])
+    for k, step in enumerate(z[:-1]):
+        hop(step, [x])
+        hop(step, [d for d in list(blocks) if 0 < d and d % (2 * step) == 0])
+    hop(x, [d for d in list(blocks) if not d & x and d ^ x not in blocks])
+    hop(core, [d for d in list(blocks) if d != devices - 2])
+    order = sorted(range(devices), key=lambda d: (2 * d.bit_count() + (d & x) / x, -(d & core), -d))
+    blocks[devices - 1] = None
     ordered = [blocks[d] for d in order]
     per = LANES // hidden
-    tall = n // per * n
-    head_blocks = ordered[: devices // 2]
+    groups = n // per
+    cuts = (groups // 2, groups - 1)
+
+    def stage_out(count):
+        tall = count * n
+        return (
+            pltpu.VMEM((tall, LANES), bf16),
+            pltpu.VMEM((tall, LANES), bf16),
+            pltpu.VMEM((2, tall, LANES), f32),
+            pltpu.VMEM((2, tall, LANES), f32),
+            pltpu.VMEM((tall, per * channels), bf16),
+            pltpu.VMEM((per, tall, channels), f32),
+            pltpu.VMEM((tall, LANES), f32),
+            pltpu.VMEM((2, channels, per // 2 * tall), bf16),
+        )
+
+    def span(first, last):
+        return ordered[first * per // rows : -(-last * per // rows)]
+
+    head_in = [*span(0, cuts[0]), token_count, gain, bias, project_t, gate_weight, out_weight]
+    smem = pl.BlockSpec(memory_space=pltpu.SMEM)
     head_out = (
-        pltpu.VMEM((per, tall // 2, channels), bf16),
-        pltpu.VMEM((tall // 2, KINDS * LANES), f32),
-        pltpu.VMEM((per, tall // 2, channels), f32),
-        pltpu.VMEM((channels, per * tall // 2), bf16),
+        *stage_out(cuts[0]),
         pltpu.VMEM((KINDS * LANES, per * channels), bf16),
         pltpu.VMEM((LANES, per * channels), bf16),
+        pltpu.VMEM((KINDS * LANES, per // 2 * LANES), bf16),
+        pltpu.VMEM((rows, n, channels), f32),
     )
     head = pl.pallas_call(
-        functools.partial(head_kernel, n),
+        functools.partial(head_kernel, n, hidden, order),
         out_shape=head_out,
-        in_specs=[vmem] * (len(head_blocks) + 5),
+        in_specs=[vmem] * (len(head_in) - 6) + [smem] + [vmem] * 5,
         out_specs=(vmem,) * len(head_out),
         compiler_params=pltpu.CompilerParams(vmem_limit_bytes=16 << 20),
         name="head",
-    )(*head_blocks, gain, bias, project_t, gate_weight, out_weight)
+    )(*head_in)
+    blocks[devices - 2], head = lax.optimization_barrier((blocks[devices - 2], head))
+    hop(core, [devices - 2])
+    ordered = [blocks[d] for d in order]
+    middle_in = [*span(*cuts), token_count, gain, bias, head[8], head[9], gate_weight]
+    middle_out = stage_out(cuts[1] - cuts[0])
+    middle = pl.pallas_call(
+        functools.partial(middle_kernel, n, hidden, order, cuts[0]),
+        out_shape=middle_out,
+        in_specs=[vmem] * (len(middle_in) - 6) + [smem] + [vmem] * 5,
+        out_specs=(vmem,) * len(middle_out),
+        compiler_params=pltpu.CompilerParams(vmem_limit_bytes=16 << 20),
+        name="middle",
+    )(*middle_in)
+    tall = groups * n
     update, pair_grad, project_grad, gate_grad, output_grad = pl.pallas_call(
-        functools.partial(tail_kernel, n, hidden, order),
+        functools.partial(tail_kernel, n, hidden, order, cuts),
         out_shape=(
             shape((rows, n, channels), bf16),
             shape((rows, n, channels), f32),
@@ -314,19 +397,18 @@
             shape((channels, channels), f32),
             shape((hidden, channels), f32),
         ),
-        in_specs=[vmem] * (devices + len(head_out)) + [pl.BlockSpec(memory_space=pltpu.SMEM)] + [vmem] * 6,
+        in_specs=[vmem] * (devices + len(head) + len(middle)) + [smem] + [vmem] * 6,
         out_specs=(vmem,) * 5,
         scratch_shapes=[
-            pltpu.VMEM((per, tall // 2, channels), bf16),
-            pltpu.VMEM((KINDS * LANES, tall), bf16),
+            *stage_out(groups - cuts[1]),
             pltpu.VMEM((n * hidden, n * hidden), bf16),
-            pltpu.VMEM((per * tall // 2, channels), bf16),
-            pltpu.VMEM((per * tall // 2, channels), bf16),
-            pltpu.VMEM((tall, per * channels), bf16),
+            pltpu.VMEM((per // 2 * tall, 2 * channels), bf16),
+            pltpu.VMEM((per // 2 * tall, LANES), bf16),
+            pltpu.VMEM((n, n * hidden), f32),
         ],
         compiler_params=pltpu.CompilerParams(vmem_limit_bytes=32 << 20),
         name="tail",
-    )(*ordered, *head, token_count, gain, bias, project_t, gate_weight, out_gain, out_bias)
+    )(*ordered, *head, *middle, token_count, gain, bias, project_t, gate_weight, out_gain, out_bias)
     return update, pair_grad, project_grad.T, gate_grad, output_grad
 
 

time: 25.9 us -> 24.3 us (0.938)
  starting transfers between devices: 17.5 us -> 15 us
  Pallas kernels: 6.84 us -> 7.63 us
    ppermute x15, starting transfers between devices: 17.5 us -> 15 us  [hop(): blocks[d ^ step] = lax.ppermute(blocks[d], 'row', pairs)]
    pallas_call x2 -> x3, Pallas kernels: 5.91 us -> 6.69 us  [the longest x1 4.37 us: body_whole(): pl.pallas_call(functools.partial(tail_kernel, n, hidden, order, cuts), ou...]
  transfers between devices with their start and end apart: 15 -> 15, of which waited for: 0 -> 0; matrix products, arithmetic and copies ran while one was open for 0% -> 0% of each run, Pallas kernels for 4% -> 10%
where the time goes in v5:
time: 24.3 us; the launch traced here: 24 us
  starting transfers between devices  15 us (62%)
  Pallas kernels  7.63 us (31%)
  between operations  1.35 us (6%)
    ppermute x15, starting transfers between devices, hop(): blocks[d ^ step] = lax.ppermute(blocks[d], 'row', pairs)  15 us
    pallas_call x1, Pallas kernels, body_whole(): pl.pallas_call(functools.partial(tail_kernel, n, hidden, order, cuts), ou...  4.37 us
    pallas_call x1, Pallas kernels, body_whole(): pl.pallas_call(functools.partial(head_kernel, n, hidden, order), out_shap...  1.33 us
    pallas_call x1, Pallas kernels, body_whole(): pl.pallas_call(functools.partial(middle_kernel, n, hidden, order, cuts[0]...  1 us
    pallas_call x1, Pallas kernels, body_whole(): pl.pallas_call(load_kernel, out_shape=[pltpu.VMEM((2 * half, channels), b...  0.93 us
  transfers between devices with their start and end apart: 15, of which 0 were waited for; matrix products, arithmetic and copies ran while one was open for 0% of the time, Pallas kernels for 10%

profile of v5, /device:TPU:1, one launch (start us, length us, event | category | flops | bytes accessed | tf_op | source)
XLA Modules:
  0.0 24.0 jit_solution(16165216331369410001)
XLA Ops:
  0.6 0.9 %load.1 = (bf16[288,128]{1,0:T(8,128)(2,1)S(1)}, f32[1,128]{1,0:T(1,128)S(1)}, f32[1,128]{1,0:T(1,128)S(1)}, bf16[64,128]{1,0:T(8,128)(2,1)S(1)}, bf16[128,128]{...) custom-call(bf16[144,128]{1,0:T(8,128)(2,1)} %bitcast.8, ...), custom_call_target="tpu_custom_call" | custom-call | tf_op jit(solution)/shard_map/load/pallas_call | solution.py:313
  1.6 3.2 %collective-permute-start.1 = (bf16[288,128]{1,0:T(8,128)(2,1)S(1)}, bf16[288,128]{1,0:T(8,128)(2,1)S(1)}, u32[]{:S(2)}, u32[]{:S(2)}) collective-permute-start(bf16[288,128]{1,0:T(8,128)(2,1)S(1)} %get-tuple-element.51.refs_0_), channel_id=1, source_target_pairs={{0,8},{1,9},{2,10},{3,11},{4,12},{5,13},{6,14},{7,15},{8,0},{9,1},... | collective-permute-start | bytes 221192 | tf_op jit(solution)/shard_map/ppermute | solution.py:327
  4.8 1.2 %collective-permute-start.3 = (bf16[288,128]{1,0:T(8,128)(2,1)S(1)}, bf16[288,128]{1,0:T(8,128)(2,1)S(1)}, u32[]{:S(2)}, u32[]{:S(2)}) collective-permute-start(bf16[288,128]{1,0:T(8,128)(2,1)S(1)} %get-tuple-element.51.refs_0_), channel_id=1, source_target_pairs={{0,2},{1,3},{2,0},{3,1},{4,6},{5,7},{6,4},{7,5},{8,10},{9,11},{10,... | collective-permute-start | bytes 221192 | tf_op jit(solution)/shard_map/ppermute | solution.py:327
  6.0 1.3 %collective-permute-start.2 = (bf16[288,128]{1,0:T(8,128)(2,1)S(1)}, bf16[288,128]{1,0:T(8,128)(2,1)S(1)}, u32[]{:S(2)}, u32[]{:S(2)}) collective-permute-start(bf16[288,128]{1,0:T(8,128)(2,1)S(1)} %get-tuple-element.51.refs_0_), channel_id=1, source_target_pairs={{0,4},{1,5},{2,6},{3,7},{4,0},{5,1},{6,2},{7,3},{8,12},{9,13},{10,... | collective-permute-start | bytes 221192 | tf_op jit(solution)/shard_map/ppermute | solution.py:327
  7.3 1.5 %collective-permute-start = (bf16[288,128]{1,0:T(8,128)(2,1)S(1)}, bf16[288,128]{1,0:T(8,128)(2,1)S(1)}, u32[]{:S(2)}, u32[]{:S(2)}) collective-permute-start(bf16[288,128]{1,0:T(8,128)(2,1)S(1)} %get-tuple-element.51.refs_0_), channel_id=1, source_target_pairs={{0,1},{1,0},{2,3},{3,2},{4,5},{5,4},{6,7},{7,6},{8,9},{9,8},{10,11... | collective-permute-start | bytes 221192 | tf_op jit(solution)/shard_map/ppermute | solution.py:327
  8.8 0.0 collective-permute-done.1.refs_2_
  8.8 0.5 %collective-permute-start.6 = (bf16[288,128]{1,0:T(8,128)(2,1)S(1)}, bf16[288,128]{1,0:T(8,128)(2,1)S(1)}, u32[]{:S(2)}, u32[]{:S(2)}) collective-permute-start(bf16[288,128]{1,0:T(8,128)(2,1)S(1)} %collective-permute-done.1.refs_2_), channel_id=1, source_target_pairs={{0,4},{1,5},{2,6},{3,7},{4,0},{5,1},{6,2},{7,3},{8,12},{9,13},{10,... | collective-permute-start | bytes 221192 | tf_op jit(solution)/shard_map/ppermute | solution.py:327
  9.3 1.0 %collective-permute-start.9 = (bf16[288,128]{1,0:T(8,128)(2,1)S(1)}, bf16[288,128]{1,0:T(8,128)(2,1)S(1)}, u32[]{:S(2)}, u32[]{:S(2)}) collective-permute-start(bf16[288,128]{1,0:T(8,128)(2,1)S(1)} %collective-permute-done.3.refs_4_), channel_id=1, source_target_pairs={{0,4},{1,5},{2,6},{3,7},{4,0},{5,1},{6,2},{7,3},{8,12},{9,13},{10,... | collective-permute-start | bytes 221192 | tf_op jit(solution)/shard_map/ppermute | solution.py:327
  10.3 1.4 %collective-permute-start.5 = (bf16[288,128]{1,0:T(8,128)(2,1)S(1)}, bf16[288,128]{1,0:T(8,128)(2,1)S(1)}, u32[]{:S(2)}, u32[]{:S(2)}) collective-permute-start(bf16[288,128]{1,0:T(8,128)(2,1)S(1)} %collective-permute-done.2.refs_3_), channel_id=1, source_target_pairs={{0,1},{1,0},{2,3},{3,2},{4,5},{5,4},{6,7},{7,6},{8,9},{9,8},{10,11... | collective-permute-start | bytes 221192 | tf_op jit(solution)/shard_map/ppermute | solution.py:327
  11.7 1.2 %collective-permute-start.8 = (bf16[288,128]{1,0:T(8,128)(2,1)S(1)}, bf16[288,128]{1,0:T(8,128)(2,1)S(1)}, u32[]{:S(2)}, u32[]{:S(2)}) collective-permute-start(bf16[288,128]{1,0:T(8,128)(2,1)S(1)} %collective-permute-done.1.refs_2_), channel_id=1, source_target_pairs={{0,2},{1,3},{2,0},{3,1},{4,6},{5,7},{6,4},{7,5},{8,10},{9,11},{10,... | collective-permute-start | bytes 221192 | tf_op jit(solution)/shard_map/ppermute | solution.py:327
  12.9 0.3 %collective-permute-start.4 = (bf16[288,128]{1,0:T(8,128)(2,1)S(1)}, bf16[288,128]{1,0:T(8,128)(2,1)S(1)}, u32[]{:S(2)}, u32[]{:S(2)}) collective-permute-start(bf16[288,128]{1,0:T(8,128)(2,1)S(1)} %collective-permute-done.1.refs_2_), channel_id=1, source_target_pairs={{0,1},{1,0},{2,3},{3,2},{4,5},{5,4},{6,7},{7,6},{8,9},{9,8},{10,11... | collective-permute-start | bytes 221192 | tf_op jit(solution)/shard_map/ppermute | solution.py:327
  13.2 0.0 collective-permute-done.6.refs_7_
  13.2 0.3 %collective-permute-start.13 = (bf16[288,128]{1,0:T(8,128)(2,1)S(1)}, bf16[288,128]{1,0:T(8,128)(2,1)S(1)}, u32[]{:S(2)}, u32[]{:S(2)}) collective-permute-start(bf16[288,128]{1,0:T(8,128)(2,1)S(1)} %collective-permute-done.6.refs_7_), channel_id=1, source_target_pairs={{0,2},{1,3},{2,0},{3,1},{4,6},{5,7},{6,4},{7,5},{8,10},{9,11},{10,... | collective-permute-start | bytes 221192 | tf_op jit(solution)/shard_map/ppermute | solution.py:327
  14.1 0.0 collective-permute-done.9.refs_2_.refs_10_
  14.1 2.0 %collective-permute-start.7 = (bf16[288,128]{1,0:T(8,128)(2,1)S(1)}, bf16[288,128]{1,0:T(8,128)(2,1)S(1)}, u32[]{:S(2)}, u32[]{:S(2)}) collective-permute-start(bf16[288,128]{1,0:T(8,128)(2,1)S(1)} %collective-permute-done.3.refs_4_), channel_id=1, source_target_pairs={{0,1},{1,0},{2,3},{3,2},{4,5},{5,4},{6,7},{7,6},{8,9},{9,8},{10,11... | collective-permute-start | bytes 221192 | tf_op jit(solution)/shard_map/ppermute | solution.py:327
  16.1 0.0 collective-permute-done.5.refs_6_
  16.1 0.1 collective-permute-start.10
  16.2 0.4 %collective-permute-start.12 = (bf16[288,128]{1,0:T(8,128)(2,1)S(1)}, bf16[288,128]{1,0:T(8,128)(2,1)S(1)}, u32[]{:S(2)}, u32[]{:S(2)}) collective-permute-start(bf16[288,128]{1,0:T(8,128)(2,1)S(1)} %collective-permute-done.9.refs_2_.refs_10_), channel_id=1, source_target_pairs={{0,1},{1,0},{2,3},{3,2},{4,5},{5,4},{6,7},{7,6},{8,9},{9,8},{10,11... | collective-permute-start | bytes 221192 | tf_op jit(solution)/shard_map/ppermute | solution.py:327
  16.6 0.1 collective-permute-start.11
  16.7 1.3 %head.1 = (bf16[144,128]{1,0:T(8,128)(2,1)S(1)}, bf16[144,128]{1,0:T(8,128)(2,1)S(1)}, f32[2,144,128]{2,1,0:T(8,128)S(1)}, f32[2,144,128]{2,1,0:T(8,128)S(1)}, b...) custom-call(bf16[288,128]{1,0:T(8,128)(2,1)S(1)} %get-tuple-element., ...), custom_call_target="tpu_custom_call" | custom-call | tf_op jit(solution)/shard_map/head/pallas_call | solution.py:369
  18.0 0.6 %collective-permute-start.14 = (bf16[288,128]{1,0:T(8,128)(2,1)S(1)}, bf16[288,128]{1,0:T(8,128)(2,1)S(1)}, u32[]{:S(2)}, u32[]{:S(2)}) collective-permute-start(bf16[288,128]{1,0:T(8,128)(2,1)S(1)} %collective-permute-done.13.refs_14_), channel_id=1, source_target_pairs={{0,1},{1,0},{2,3},{3,2},{4,5},{5,4},{6,7},{7,6},{8,9},{9,8},{10,11... | collective-permute-start | bytes 221192 | tf_op jit(solution)/shard_map/ppermute | solution.py:327
  18.7 1.0 %middle.1 = (bf16[96,128]{1,0:T(8,128)(2,1)S(1)}, bf16[96,128]{1,0:T(8,128)(2,1)S(1)}, f32[2,96,128]{2,1,0:T(8,128)S(1)}, f32[2,96,128]{2,1,0:T(8,128)S(1)}, bf1...) custom-call(bf16[288,128]{1,0:T(8,128)(2,1)S(1)} %collective-permute, ...), custom_call_target="tpu_custom_call" | custom-call | tf_op jit(solution)/shard_map/middle/pallas_call | solution.py:382
  19.7 0.0 collective-permute-done.14.refs_15_
  19.7 4.4 %tail.1 = (bf16[3,48,128]{2,1,0:T(8,128)(2,1)}, f32[3,48,128]{2,1,0:T(8,128)}, f32[64,128]{1,0:T(8,128)}, f32[128,128]{1,0:T(8,128)}, f32[16,128]{1,0:T(8,128)}) custom-call(bf16[288,128]{1,0:T(8,128)(2,1)S(1)} %get-tuple-element.51.refs_0_, bf16[288,128]{1,0:T(8,128)(2,1)S(1)} %collective-permute-done.refs_1_, ...), custom_call_target="tpu_custom_call" | custom-call | tf_op jit(solution)/shard_map/tail/pallas_call | solution.py:391
  (10 shorter events, 0.0 us)
Async XLA Ops:
  1.6 7.2 %collective-permute-start.1 = (bf16[288,128]{1,0:T(8,128)(2,1)S(1)}, bf16[288,128]{1,0:T(8,128)(2,1)S(1)}, u32[]{:S(2)}, u32[]{:S(2)}) collective-permute-start(bf16[288,128]{1,0:T(8,128)(2,1)S(1)} %get-tuple-element.51.refs_0_), channel_id=1, source_target_pairs={{0,8},{1,9},{2,10},{3,11},{4,12},{5,13},{6,14},{7,15},{8,0},{9,1},... | collective-permute-start | bytes 221192 | tf_op jit(solution)/shard_map/ppermute | solution.py:327
  4.8 4.5 %collective-permute-start.3 = (bf16[288,128]{1,0:T(8,128)(2,1)S(1)}, bf16[288,128]{1,0:T(8,128)(2,1)S(1)}, u32[]{:S(2)}, u32[]{:S(2)}) collective-permute-start(bf16[288,128]{1,0:T(8,128)(2,1)S(1)} %get-tuple-element.51.refs_0_), channel_id=1, source_target_pairs={{0,2},{1,3},{2,0},{3,1},{4,6},{5,7},{6,4},{7,5},{8,10},{9,11},{10,... | collective-permute-start | bytes 221192 | tf_op jit(solution)/shard_map/ppermute | solution.py:327
  6.0 4.3 %collective-permute-start.2 = (bf16[288,128]{1,0:T(8,128)(2,1)S(1)}, bf16[288,128]{1,0:T(8,128)(2,1)S(1)}, u32[]{:S(2)}, u32[]{:S(2)}) collective-permute-start(bf16[288,128]{1,0:T(8,128)(2,1)S(1)} %get-tuple-element.51.refs_0_), channel_id=1, source_target_pairs={{0,4},{1,5},{2,6},{3,7},{4,0},{5,1},{6,2},{7,3},{8,12},{9,13},{10,... | collective-permute-start | bytes 221192 | tf_op jit(solution)/shard_map/ppermute | solution.py:327
  7.3 5.6 %collective-permute-start = (bf16[288,128]{1,0:T(8,128)(2,1)S(1)}, bf16[288,128]{1,0:T(8,128)(2,1)S(1)}, u32[]{:S(2)}, u32[]{:S(2)}) collective-permute-start(bf16[288,128]{1,0:T(8,128)(2,1)S(1)} %get-tuple-element.51.refs_0_), channel_id=1, source_target_pairs={{0,1},{1,0},{2,3},{3,2},{4,5},{5,4},{6,7},{7,6},{8,9},{9,8},{10,11... | collective-permute-start | bytes 221192 | tf_op jit(solution)/shard_map/ppermute | solution.py:327
  8.8 4.4 %collective-permute-start.6 = (bf16[288,128]{1,0:T(8,128)(2,1)S(1)}, bf16[288,128]{1,0:T(8,128)(2,1)S(1)}, u32[]{:S(2)}, u32[]{:S(2)}) collective-permute-start(bf16[288,128]{1,0:T(8,128)(2,1)S(1)} %collective-permute-done.1.refs_2_), channel_id=1, source_target_pairs={{0,4},{1,5},{2,6},{3,7},{4,0},{5,1},{6,2},{7,3},{8,12},{9,13},{10,... | collective-permute-start | bytes 221192 | tf_op jit(solution)/shard_map/ppermute | solution.py:327
  9.3 4.8 %collective-permute-start.9 = (bf16[288,128]{1,0:T(8,128)(2,1)S(1)}, bf16[288,128]{1,0:T(8,128)(2,1)S(1)}, u32[]{:S(2)}, u32[]{:S(2)}) collective-permute-start(bf16[288,128]{1,0:T(8,128)(2,1)S(1)} %collective-permute-done.3.refs_4_), channel_id=1, source_target_pairs={{0,4},{1,5},{2,6},{3,7},{4,0},{5,1},{6,2},{7,3},{8,12},{9,13},{10,... | collective-permute-start | bytes 221192 | tf_op jit(solution)/shard_map/ppermute | solution.py:327
  10.3 5.8 %collective-permute-start.5 = (bf16[288,128]{1,0:T(8,128)(2,1)S(1)}, bf16[288,128]{1,0:T(8,128)(2,1)S(1)}, u32[]{:S(2)}, u32[]{:S(2)}) collective-permute-start(bf16[288,128]{1,0:T(8,128)(2,1)S(1)} %collective-permute-done.2.refs_3_), channel_id=1, source_target_pairs={{0,1},{1,0},{2,3},{3,2},{4,5},{5,4},{6,7},{7,6},{8,9},{9,8},{10,11... | collective-permute-start | bytes 221192 | tf_op jit(solution)/shard_map/ppermute | solution.py:327
  11.7 4.5 %collective-permute-start.8 = (bf16[288,128]{1,0:T(8,128)(2,1)S(1)}, bf16[288,128]{1,0:T(8,128)(2,1)S(1)}, u32[]{:S(2)}, u32[]{:S(2)}) collective-permute-start(bf16[288,128]{1,0:T(8,128)(2,1)S(1)} %collective-permute-done.1.refs_2_), channel_id=1, source_target_pairs={{0,2},{1,3},{2,0},{3,1},{4,6},{5,7},{6,4},{7,5},{8,10},{9,11},{10,... | collective-permute-start | bytes 221192 | tf_op jit(solution)/shard_map/ppermute | solution.py:327
  12.9 3.7 %collective-permute-start.4 = (bf16[288,128]{1,0:T(8,128)(2,1)S(1)}, bf16[288,128]{1,0:T(8,128)(2,1)S(1)}, u32[]{:S(2)}, u32[]{:S(2)}) collective-permute-start(bf16[288,128]{1,0:T(8,128)(2,1)S(1)} %collective-permute-done.1.refs_2_), channel_id=1, source_target_pairs={{0,1},{1,0},{2,3},{3,2},{4,5},{5,4},{6,7},{7,6},{8,9},{9,8},{10,11... | collective-permute-start | bytes 221192 | tf_op jit(solution)/shard_map/ppermute | solution.py:327
  13.2 4.8 %collective-permute-start.13 = (bf16[288,128]{1,0:T(8,128)(2,1)S(1)}, bf16[288,128]{1,0:T(8,128)(2,1)S(1)}, u32[]{:S(2)}, u32[]{:S(2)}) collective-permute-start(bf16[288,128]{1,0:T(8,128)(2,1)S(1)} %collective-permute-done.6.refs_7_), channel_id=1, source_target_pairs={{0,2},{1,3},{2,0},{3,1},{4,6},{5,7},{6,4},{7,5},{8,10},{9,11},{10,... | collective-permute-start | bytes 221192 | tf_op jit(solution)/shard_map/ppermute | solution.py:327
  14.1 4.5 %collective-permute-start.7 = (bf16[288,128]{1,0:T(8,128)(2,1)S(1)}, bf16[288,128]{1,0:T(8,128)(2,1)S(1)}, u32[]{:S(2)}, u32[]{:S(2)}) collective-permute-start(bf16[288,128]{1,0:T(8,128)(2,1)S(1)} %collective-permute-done.3.refs_4_), channel_id=1, source_target_pairs={{0,1},{1,0},{2,3},{3,2},{4,5},{5,4},{6,7},{7,6},{8,9},{9,8},{10,11... | collective-permute-start | bytes 221192 | tf_op jit(solution)/shard_map/ppermute | solution.py:327
  16.1 2.6 %collective-permute-start.10 = (bf16[288,128]{1,0:T(8,128)(2,1)S(1)}, bf16[288,128]{1,0:T(8,128)(2,1)S(1)}, u32[]{:S(2)}, u32[]{:S(2)}) collective-permute-start(bf16[288,128]{1,0:T(8,128)(2,1)S(1)} %collective-permute-done.6.refs_7_), channel_id=1, source_target_pairs={{0,1},{1,0},{2,3},{3,2},{4,5},{5,4},{6,7},{7,6},{8,9},{9,8},{10,11... | collective-permute-start | bytes 221192 | tf_op jit(solution)/shard_map/ppermute | solution.py:327
  16.2 2.5 %collective-permute-start.12 = (bf16[288,128]{1,0:T(8,128)(2,1)S(1)}, bf16[288,128]{1,0:T(8,128)(2,1)S(1)}, u32[]{:S(2)}, u32[]{:S(2)}) collective-permute-start(bf16[288,128]{1,0:T(8,128)(2,1)S(1)} %collective-permute-done.9.refs_2_.refs_10_), channel_id=1, source_target_pairs={{0,1},{1,0},{2,3},{3,2},{4,5},{5,4},{6,7},{7,6},{8,9},{9,8},{10,11... | collective-permute-start | bytes 221192 | tf_op jit(solution)/shard_map/ppermute | solution.py:327
  16.6 2.1 %collective-permute-start.11 = (bf16[288,128]{1,0:T(8,128)(2,1)S(1)}, bf16[288,128]{1,0:T(8,128)(2,1)S(1)}, u32[]{:S(2)}, u32[]{:S(2)}) collective-permute-start(bf16[288,128]{1,0:T(8,128)(2,1)S(1)} %collective-permute-done.8.refs_1_.refs_9_), channel_id=1, source_target_pairs={{0,1},{1,0},{2,3},{3,2},{4,5},{5,4},{6,7},{7,6},{8,9},{9,8},{10,11... | collective-permute-start | bytes 221192 | tf_op jit(solution)/shard_map/ppermute | solution.py:327
  18.0 1.6 %collective-permute-start.14 = (bf16[288,128]{1,0:T(8,128)(2,1)S(1)}, bf16[288,128]{1,0:T(8,128)(2,1)S(1)}, u32[]{:S(2)}, u32[]{:S(2)}) collective-permute-start(bf16[288,128]{1,0:T(8,128)(2,1)S(1)} %collective-permute-done.13.refs_14_), channel_id=1, source_target_pairs={{0,1},{1,0},{2,3},{3,2},{4,5},{5,4},{6,7},{7,6},{8,9},{9,8},{10,11... | collective-permute-start | bytes 221192 | tf_op jit(solution)/shard_map/ppermute | solution.py:327

commit v6 on v5

--- a/solution.py
+++ b/solution.py
@@ -127,11 +127,16 @@
 
 
 def pick_place(per, hidden):
-    half, width = per // 2, KINDS * hidden
-    a, b = iota((KINDS * LANES, LANES), 0), iota((KINDS * LANES, LANES), 1)
-    own = (a // LANES == b % width // hidden) & (a % hidden == b % hidden)
-    place = a % LANES // hidden
-    return jnp.concatenate([zero_one(own & (place == b // width * half + q)) for q in range(half)], axis=1)
+    half = per // 2
+    rows = []
+    for kind in range(KINDS):
+        for p in range(per):
+            column = (p // half * KINDS + kind) * hidden
+            own = zero_one(iota((hidden, LANES), 1) == iota((hidden, LANES), 0) + column)
+            before, after = p % half * LANES, (half - 1 - p % half) * LANES
+            parts = [jnp.zeros((hidden, before), own.dtype)] * (before > 0) + [own]
+            rows.append(jnp.concatenate(parts + [jnp.zeros((hidden, after), own.dtype)] * (after > 0), axis=1))
+    return jnp.concatenate(rows, axis=0)
 
 
 def load_kernel(*refs):
@@ -144,6 +149,19 @@
         copy.start()
     for copy in copies:
         copy.wait()
+
+
+def cross(n, hidden, order, lefts, rights, first, store):
+    wide = lefts.shape[1]
+    same = iota((hidden, wide), 0) == iota((hidden, wide), 1) % hidden
+    product = dot(rights, lefts, TN)
+    for t in range(rights.shape[1] // hidden):
+        own = jnp.where(same, product[t * hidden : (t + 1) * hidden], 0.0)
+        store(pl.ds(row_of(order, n // len(order), first + t), 1), jnp.sum(own, axis=0, keepdims=True))
+
+
+def side_by_side(ref, n):
+    return jnp.concatenate([ref[pl.ds(g * n, n), :] for g in range(ref.shape[0] // n)], axis=1)
 
 
 def head_kernel(n, hidden, order, *refs):
@@ -160,18 +178,29 @@
 
 
 def middle_kernel(n, hidden, order, first, *refs):
-    *block_refs, count_ref, gain_ref, bias_ref, project_wide_ref, out_wide_ref, gate_ref = refs[:-8]
+    left_head_ref, right_head_ref, *block_refs = refs[:-15]
+    count_ref, gain_ref, bias_ref, project_wide_ref, out_wide_ref, gate_ref = refs[-15:-9]
+    *stage_refs, x_ref = refs[-9:]
     weights = [ref[...] for ref in (gain_ref, bias_ref, project_wide_ref, out_wide_ref, gate_ref)]
-    stage(n, hidden, order, first, block_refs, count_ref[0], *weights, refs[-8:])
+    stage(n, hidden, order, first, block_refs, count_ref[0], *weights, stage_refs)
+    left = jnp.concatenate([side_by_side(left_head_ref, n), side_by_side(stage_refs[0], n)], axis=1)
+    right = jnp.concatenate([side_by_side(right_head_ref, n), side_by_side(stage_refs[1], n)], axis=1)
+    x_ref[...] = jnp.zeros_like(x_ref)
+
+    def store(row, value):
+        x_ref[row, :] = value
+
+    cross(n, hidden, order, left, right, 0, store)
 
 
 def tail_kernel(n, hidden, order, cuts, *refs):
     blocks = len(order)
     block_refs, refs = refs[:blocks], refs[blocks:]
     head_refs, (project_wide_ref, out_wide_ref, pick_ref, own_ref), middle_refs = refs[:8], refs[8:12], refs[12:20]
-    count_ref, gain_ref, bias_ref, project_ref, gate_ref, out_gain_ref, out_bias_ref = refs[20:27]
-    update_ref, pair_ref, project_grad_ref, gate_grad_ref, out_grad_ref = refs[27:32]
-    tail_refs, (square_ref, dgo_ref, dp_ref, dx_ref) = refs[32:40], refs[40:]
+    x_early_ref, *refs = refs[20:]
+    count_ref, gain_ref, bias_ref, project_ref, gate_ref, out_gain_ref, out_bias_ref = refs[:7]
+    update_ref, pair_ref, project_grad_ref, gate_grad_ref, out_grad_ref = refs[7:12]
+    tail_refs, (square_ref, dgo_ref, dp_ref, x_ref, x_late_ref, dx_ref) = refs[12:20], refs[20:]
     stages = (head_refs, middle_refs, tail_refs)
     f32, bf16 = jnp.float32, jnp.bfloat16
     per = LANES // hidden
@@ -197,7 +226,6 @@
     def all_rows(k):
         return jnp.concatenate([refs[k][...] for refs in stages], axis=0)
 
-    row_i = [rows_of_lanes(order, rows, hidden, g) for g in range(groups)]
 
     def lanes(flat):
         return jnp.concatenate([flat[g * n : (g + 1) * n] for g in range(groups)], axis=1)
@@ -207,16 +235,20 @@
 
     left, right = lanes(all_rows(0)), lanes(all_rows(1))
 
-    same = iota((LANES, wide), 0) % hidden == iota((LANES, wide), 1) % hidden
-
-    def keep_same(square):
-        for g in range(groups):
-            part = square[g * LANES : (g + 1) * LANES].astype(bf16)
-            square_ref[pl.ds(g * LANES, LANES), :] = jnp.where(same, part, jnp.zeros_like(part))
-
-    keep_same(dot(right, left, TN))
-    pick = jnp.concatenate([zero_one(iota((n, LANES), 0) == at) for at in row_i], axis=1)
-    x = flatten(dot(pick, square_ref[...]))
+    split = cuts[1] * LANES
+    x_ref[...] = jnp.zeros_like(x_ref)
+
+    def store_late(row, value):
+        x_late_ref[row, :] = value
+
+    def store_both(row, value):
+        x_ref[row, :] = value[:, :split]
+        x_late_ref[row, :] = value[:, split:]
+
+    cross(n, hidden, order, left[:, split:], right[:, :split], 0, store_late)
+    cross(n, hidden, order, left, right[:, split:], split // hidden, store_both)
+    x = jnp.concatenate([x_early_ref[...] + x_ref[...], x_late_ref[...]], axis=1)
+    x = flatten(x.astype(bf16).astype(f32))
 
     mean = jnp.where(iota((LANES, LANES), 0) // hidden == iota((LANES, LANES), 1) // hidden, 1.0 / hidden, 0.0)
     mean = mean.astype(bf16)
@@ -228,6 +260,15 @@
     xhat = centered * xs
     xn = (xhat * out_gain + out_bias).astype(bf16)
 
+    u = out_gain * all_rows(6)
+    dx = xs * (u - dot_split(u, mean_twice) - xhat * dot_split(u * xhat, mean_twice))
+    dx_ref[...] = lanes(dx.astype(bf16)).astype(f32)
+
+    same = iota((hidden, wide), 0) == iota((hidden, wide), 1) % hidden
+    for t in range(n):
+        row = dx_ref[pl.ds(row_of(order, rows, t), 1), :]
+        row = jnp.broadcast_to(row, (hidden, wide)).astype(bf16)
+        square_ref[pl.ds(t * hidden, hidden), :] = jnp.where(same, row, jnp.zeros_like(row))
     y_all = dot(xn, out_wide_ref[...])
     own_dgo = []
     for p in range(per):
@@ -237,23 +278,15 @@
         if p < rows:
             update_ref[p] = (own_ref[p] * y[:n]).astype(bf16)
             own_dgo.append(dgo[:n])
-    out_grad = dot(xn, all_rows(4), TN)
-    out_grad = [out_grad[p * hidden : (p + 1) * hidden, p * LANES : (p + 1) * LANES] for p in range(per)]
+    diagonal = square_ref[...]
+    dleft = flatten(dot(right, diagonal).astype(bf16)).astype(f32)
+    dright = flatten(dot(left, diagonal, NT).astype(bf16)).astype(f32)
+    xnt, dy = xn.T, all_rows(4)
+    out_grad = [dot(xnt[p * hidden : (p + 1) * hidden], dy[:, p * LANES : (p + 1) * LANES]) for p in range(per)]
     out_grad_ref[...] = sum(out_grad) / n
     gate_grad = sum_pairs(dgo_ref)
     gate_grad_ref[...] = (gate_grad[:LANES, :LANES] + gate_grad[LANES:, LANES:]) / n
 
-    u = out_gain * all_rows(6)
-    dx = xs * (u - dot_split(u, mean_twice) - xhat * dot_split(u * xhat, mean_twice))
-    dx_ref[...] = lanes(dx.astype(bf16)).astype(f32)
-
-    for t in range(n):
-        row = dx_ref[pl.ds(row_of(order, rows, t), 1), :]
-        row = jnp.broadcast_to(row, (hidden, wide)).astype(bf16)
-        square_ref[pl.ds(t * hidden, hidden), :] = jnp.where(same[:hidden], row, jnp.zeros_like(row))
-    diagonal = square_ref[...]
-    dleft = flatten(dot(right, diagonal).astype(bf16)).astype(f32)
-    dright = flatten(dot(left, diagonal, NT).astype(bf16)).astype(f32)
     dp = []
     for side, grad in enumerate((dleft, dright)):
         masked = grad * jnp.concatenate([refs[2][side] for refs in stages], axis=0)
@@ -328,14 +361,15 @@
 
     for step in reversed(z):
         hop(step, [0])
-    hop(x, [0])
+        if step == z[-1]:
+            hop(x, [0])
     for k, step in enumerate(z[:-1]):
         hop(step, [x])
         hop(step, [d for d in list(blocks) if 0 < d and d % (2 * step) == 0])
     hop(x, [d for d in list(blocks) if not d & x and d ^ x not in blocks])
-    hop(core, [d for d in list(blocks) if d != devices - 2])
+    hop(core, [d for d in list(blocks) if d not in [14]])
     order = sorted(range(devices), key=lambda d: (2 * d.bit_count() + (d & x) / x, -(d & core), -d))
-    blocks[devices - 1] = None
+    blocks[15] = None
     ordered = [blocks[d] for d in order]
     per = LANES // hidden
     groups = n // per
@@ -374,11 +408,14 @@
         compiler_params=pltpu.CompilerParams(vmem_limit_bytes=16 << 20),
         name="head",
     )(*head_in)
-    blocks[devices - 2], head = lax.optimization_barrier((blocks[devices - 2], head))
-    hop(core, [devices - 2])
+    held = [blocks[d] for d in [14]]
+    held, head = lax.optimization_barrier((held, head))
+    for d, block in zip([14], held):
+        blocks[d] = block
+    hop(core, [14])
     ordered = [blocks[d] for d in order]
-    middle_in = [*span(*cuts), token_count, gain, bias, head[8], head[9], gate_weight]
-    middle_out = stage_out(cuts[1] - cuts[0])
+    middle_in = [head[0], head[1], *span(*cuts), token_count, gain, bias, head[8], head[9], gate_weight]
+    middle_out = (*stage_out(cuts[1] - cuts[0]), pltpu.VMEM((n, cuts[1] * LANES), f32))
     middle = pl.pallas_call(
         functools.partial(middle_kernel, n, hidden, order, cuts[0]),
         out_shape=middle_out,
@@ -404,6 +441,8 @@
             pltpu.VMEM((n * hidden, n * hidden), bf16),
             pltpu.VMEM((per // 2 * tall, 2 * channels), bf16),
             pltpu.VMEM((per // 2 * tall, LANES), bf16),
+            pltpu.VMEM((n, cuts[1] * LANES), f32),
+            pltpu.VMEM((n, (groups - cuts[1]) * LANES), f32),
             pltpu.VMEM((n, n * hidden), f32),
         ],
         compiler_params=pltpu.CompilerParams(vmem_limit_bytes=32 << 20),

time: 24.3 us -> 23.9 us (0.984)
  Pallas kernels: 7.63 us -> 7.05 us
  starting transfers between devices: 15 us -> 15.3 us
    pallas_call x1, Pallas kernels: 4.37 us -> 3.78 us  [body_whole(): pl.pallas_call(functools.partial(tail_kernel, n, hidden, order, cuts), ou...]
    pallas_call x1, Pallas kernels: 1 us -> 1.26 us  [body_whole(): pl.pallas_call(functools.partial(middle_kernel, n, hidden, order, cuts[0]...]
    ppermute x15, starting transfers between devices: 15 us -> 15.3 us  [hop(): blocks[d ^ step] = lax.ppermute(blocks[d], 'row', pairs)]
    pallas_call x1, Pallas kernels: 1.33 us -> 1.08 us  [body_whole(): pl.pallas_call(functools.partial(head_kernel, n, hidden, order), out_shap...]
where the time goes in v6:
time: 23.9 us; the launch traced here: 23.7 us
  starting transfers between devices  15.3 us (64%)
  Pallas kernels  7.05 us (29%)
  between operations  1.35 us (6%)
    ppermute x15, starting transfers between devices, hop(): blocks[d ^ step] = lax.ppermute(blocks[d], 'row', pairs)  15.3 us
    pallas_call x1, Pallas kernels, body_whole(): pl.pallas_call(functools.partial(tail_kernel, n, hidden, order, cuts), ou...  3.78 us
    pallas_call x1, Pallas kernels, body_whole(): pl.pallas_call(functools.partial(middle_kernel, n, hidden, order, cuts[0]...  1.26 us
    pallas_call x1, Pallas kernels, body_whole(): pl.pallas_call(functools.partial(head_kernel, n, hidden, order), out_shap...  1.08 us
    pallas_call x1, Pallas kernels, body_whole(): pl.pallas_call(load_kernel, out_shape=[pltpu.VMEM((2 * half, channels), b...  0.93 us
  transfers between devices with their start and end apart: 15, of which 0 were waited for; matrix products, arithmetic and copies ran while one was open for 0% of the time, Pallas kernels for 10%

profile of v6, /device:TPU:1, one launch (start us, length us, event | category | flops | bytes accessed | tf_op | source)
XLA Modules:
  0.0 23.7 jit_solution(14522089771111531497)
XLA Ops:
  0.6 0.9 %load.1 = (bf16[288,128]{1,0:T(8,128)(2,1)S(1)}, f32[1,128]{1,0:T(1,128)S(1)}, f32[1,128]{1,0:T(1,128)S(1)}, bf16[64,128]{1,0:T(8,128)(2,1)S(1)}, bf16[128,128]{...) custom-call(bf16[144,128]{1,0:T(8,128)(2,1)} %bitcast.8, ...), custom_call_target="tpu_custom_call" | custom-call | tf_op jit(solution)/shard_map/load/pallas_call | solution.py:346
  1.6 3.2 %collective-permute-start.1 = (bf16[288,128]{1,0:T(8,128)(2,1)S(1)}, bf16[288,128]{1,0:T(8,128)(2,1)S(1)}, u32[]{:S(2)}, u32[]{:S(2)}) collective-permute-start(bf16[288,128]{1,0:T(8,128)(2,1)S(1)} %get-tuple-element.52.refs_0_), channel_id=1, source_target_pairs={{0,8},{1,9},{2,10},{3,11},{4,12},{5,13},{6,14},{7,15},{8,0},{9,1},... | collective-permute-start | bytes 221192 | tf_op jit(solution)/shard_map/ppermute | solution.py:360
  4.8 1.2 %collective-permute-start.3 = (bf16[288,128]{1,0:T(8,128)(2,1)S(1)}, bf16[288,128]{1,0:T(8,128)(2,1)S(1)}, u32[]{:S(2)}, u32[]{:S(2)}) collective-permute-start(bf16[288,128]{1,0:T(8,128)(2,1)S(1)} %get-tuple-element.52.refs_0_), channel_id=1, source_target_pairs={{0,2},{1,3},{2,0},{3,1},{4,6},{5,7},{6,4},{7,5},{8,10},{9,11},{10,... | collective-permute-start | bytes 221192 | tf_op jit(solution)/shard_map/ppermute | solution.py:360
  6.0 1.3 %collective-permute-start.2 = (bf16[288,128]{1,0:T(8,128)(2,1)S(1)}, bf16[288,128]{1,0:T(8,128)(2,1)S(1)}, u32[]{:S(2)}, u32[]{:S(2)}) collective-permute-start(bf16[288,128]{1,0:T(8,128)(2,1)S(1)} %get-tuple-element.52.refs_0_), channel_id=1, source_target_pairs={{0,4},{1,5},{2,6},{3,7},{4,0},{5,1},{6,2},{7,3},{8,12},{9,13},{10,... | collective-permute-start | bytes 221192 | tf_op jit(solution)/shard_map/ppermute | solution.py:360
  7.3 1.5 %collective-permute-start = (bf16[288,128]{1,0:T(8,128)(2,1)S(1)}, bf16[288,128]{1,0:T(8,128)(2,1)S(1)}, u32[]{:S(2)}, u32[]{:S(2)}) collective-permute-start(bf16[288,128]{1,0:T(8,128)(2,1)S(1)} %get-tuple-element.52.refs_0_), channel_id=1, source_target_pairs={{0,1},{1,0},{2,3},{3,2},{4,5},{5,4},{6,7},{7,6},{8,9},{9,8},{10,11... | collective-permute-start | bytes 221192 | tf_op jit(solution)/shard_map/ppermute | solution.py:360
  8.8 0.5 %collective-permute-start.6 = (bf16[288,128]{1,0:T(8,128)(2,1)S(1)}, bf16[288,128]{1,0:T(8,128)(2,1)S(1)}, u32[]{:S(2)}, u32[]{:S(2)}) collective-permute-start(bf16[288,128]{1,0:T(8,128)(2,1)S(1)} %collective-permute-done.1.refs_2_), channel_id=1, source_target_pairs={{0,4},{1,5},{2,6},{3,7},{4,0},{5,1},{6,2},{7,3},{8,12},{9,13},{10,... | collective-permute-start | bytes 221192 | tf_op jit(solution)/shard_map/ppermute | solution.py:360
  9.3 1.0 %collective-permute-start.9 = (bf16[288,128]{1,0:T(8,128)(2,1)S(1)}, bf16[288,128]{1,0:T(8,128)(2,1)S(1)}, u32[]{:S(2)}, u32[]{:S(2)}) collective-permute-start(bf16[288,128]{1,0:T(8,128)(2,1)S(1)} %collective-permute-done.3.refs_4_), channel_id=1, source_target_pairs={{0,4},{1,5},{2,6},{3,7},{4,0},{5,1},{6,2},{7,3},{8,12},{9,13},{10,... | collective-permute-start | bytes 221192 | tf_op jit(solution)/shard_map/ppermute | solution.py:360
  10.3 0.0 collective-permute-done.2.refs_3_
  10.3 1.4 %collective-permute-start.5 = (bf16[288,128]{1,0:T(8,128)(2,1)S(1)}, bf16[288,128]{1,0:T(8,128)(2,1)S(1)}, u32[]{:S(2)}, u32[]{:S(2)}) collective-permute-start(bf16[288,128]{1,0:T(8,128)(2,1)S(1)} %collective-permute-done.2.refs_3_), channel_id=1, source_target_pairs={{0,1},{1,0},{2,3},{3,2},{4,5},{5,4},{6,7},{7,6},{8,9},{9,8},{10,11... | collective-permute-start | bytes 221192 | tf_op jit(solution)/shard_map/ppermute | solution.py:360
  11.7 1.2 %collective-permute-start.8 = (bf16[288,128]{1,0:T(8,128)(2,1)S(1)}, bf16[288,128]{1,0:T(8,128)(2,1)S(1)}, u32[]{:S(2)}, u32[]{:S(2)}) collective-permute-start(bf16[288,128]{1,0:T(8,128)(2,1)S(1)} %collective-permute-done.1.refs_2_), channel_id=1, source_target_pairs={{0,2},{1,3},{2,0},{3,1},{4,6},{5,7},{6,4},{7,5},{8,10},{9,11},{10,... | collective-permute-start | bytes 221192 | tf_op jit(solution)/shard_map/ppermute | solution.py:360
  12.9 0.0 collective-permute-done.refs_1_
  12.9 0.3 %collective-permute-start.4 = (bf16[288,128]{1,0:T(8,128)(2,1)S(1)}, bf16[288,128]{1,0:T(8,128)(2,1)S(1)}, u32[]{:S(2)}, u32[]{:S(2)}) collective-permute-start(bf16[288,128]{1,0:T(8,128)(2,1)S(1)} %collective-permute-done.1.refs_2_), channel_id=1, source_target_pairs={{0,1},{1,0},{2,3},{3,2},{4,5},{5,4},{6,7},{7,6},{8,9},{9,8},{10,11... | collective-permute-start | bytes 221192 | tf_op jit(solution)/shard_map/ppermute | solution.py:360
  13.2 0.0 collective-permute-done.6.refs_7_
  13.2 0.3 %collective-permute-start.13 = (bf16[288,128]{1,0:T(8,128)(2,1)S(1)}, bf16[288,128]{1,0:T(8,128)(2,1)S(1)}, u32[]{:S(2)}, u32[]{:S(2)}) collective-permute-start(bf16[288,128]{1,0:T(8,128)(2,1)S(1)} %collective-permute-done.6.refs_7_), channel_id=1, source_target_pairs={{0,2},{1,3},{2,0},{3,1},{4,6},{5,7},{6,4},{7,5},{8,10},{9,11},{10,... | collective-permute-start | bytes 221192 | tf_op jit(solution)/shard_map/ppermute | solution.py:360
  14.1 2.0 %collective-permute-start.7 = (bf16[288,128]{1,0:T(8,128)(2,1)S(1)}, bf16[288,128]{1,0:T(8,128)(2,1)S(1)}, u32[]{:S(2)}, u32[]{:S(2)}) collective-permute-start(bf16[288,128]{1,0:T(8,128)(2,1)S(1)} %collective-permute-done.3.refs_4_), channel_id=1, source_target_pairs={{0,1},{1,0},{2,3},{3,2},{4,5},{5,4},{6,7},{7,6},{8,9},{9,8},{10,11... | collective-permute-start | bytes 221192 | tf_op jit(solution)/shard_map/ppermute | solution.py:360
  16.1 0.0 collective-permute-done.5.refs_6_
  16.1 0.1 collective-permute-start.10
  16.2 0.0 collective-permute-done.8.refs_3_.refs_9_
  16.2 0.4 %collective-permute-start.12 = (bf16[288,128]{1,0:T(8,128)(2,1)S(1)}, bf16[288,128]{1,0:T(8,128)(2,1)S(1)}, u32[]{:S(2)}, u32[]{:S(2)}) collective-permute-start(bf16[288,128]{1,0:T(8,128)(2,1)S(1)} %collective-permute-done.9.refs_4_.refs_10_), channel_id=1, source_target_pairs={{0,1},{1,0},{2,3},{3,2},{4,5},{5,4},{6,7},{7,6},{8,9},{9,8},{10,11... | collective-permute-start | bytes 221192 | tf_op jit(solution)/shard_map/ppermute | solution.py:360
  16.6 0.1 collective-permute-start.11
  16.7 1.1 %head.1 = (bf16[144,128]{1,0:T(8,128)(2,1)S(1)}, bf16[144,128]{1,0:T(8,128)(2,1)S(1)}, f32[2,144,128]{2,1,0:T(8,128)S(1)}, f32[2,144,128]{2,1,0:T(8,128)S(1)}, b...) custom-call(bf16[288,128]{1,0:T(8,128)(2,1)S(1)} %get-tuple-element., ...), custom_call_target="tpu_custom_call" | custom-call | tf_op jit(solution)/shard_map/head/pallas_call | solution.py:403
  17.8 0.9 %collective-permute-start.14 = (bf16[288,128]{1,0:T(8,128)(2,1)S(1)}, bf16[288,128]{1,0:T(8,128)(2,1)S(1)}, u32[]{:S(2)}, u32[]{:S(2)}) collective-permute-start(bf16[288,128]{1,0:T(8,128)(2,1)S(1)} %collective-permute-done.13.refs_14_), channel_id=1, source_target_pairs={{0,1},{1,0},{2,3},{3,2},{4,5},{5,4},{6,7},{7,6},{8,9},{9,8},{10,11... | collective-permute-start | bytes 221192 | tf_op jit(solution)/shard_map/ppermute | solution.py:360
  18.7 1.3 %middle.1 = (bf16[96,128]{1,0:T(8,128)(2,1)S(1)}, bf16[96,128]{1,0:T(8,128)(2,1)S(1)}, f32[2,96,128]{2,1,0:T(8,128)S(1)}, f32[2,96,128]{2,1,0:T(8,128)S(1)}, bf1...) custom-call(bf16[144,128]{1,0:T(8,128)(2,1)S(1)} %get-tuple-element., ...), custom_call_target="tpu_custom_call" | custom-call | tf_op jit(solution)/shard_map/middle/pallas_call | solution.py:419
  19.9 3.8 %tail.1 = (bf16[3,48,128]{2,1,0:T(8,128)(2,1)}, f32[3,48,128]{2,1,0:T(8,128)}, f32[64,128]{1,0:T(8,128)}, f32[128,128]{1,0:T(8,128)}, f32[16,128]{1,0:T(8,128)}) custom-call(bf16[288,128]{1,0:T(8,128)(2,1)S(1)} %get-tuple-element.52.refs_0_, bf16[288,128]{1,0:T(8,128)(2,1)S(1)} %collective-permute-done.refs_1_, ...), custom_call_target="tpu_custom_call" | custom-call | tf_op jit(solution)/shard_map/tail/pallas_call | solution.py:428
  (10 shorter events, 0.0 us)
Async XLA Ops:
  1.6 7.2 %collective-permute-start.1 = (bf16[288,128]{1,0:T(8,128)(2,1)S(1)}, bf16[288,128]{1,0:T(8,128)(2,1)S(1)}, u32[]{:S(2)}, u32[]{:S(2)}) collective-permute-start(bf16[288,128]{1,0:T(8,128)(2,1)S(1)} %get-tuple-element.52.refs_0_), channel_id=1, source_target_pairs={{0,8},{1,9},{2,10},{3,11},{4,12},{5,13},{6,14},{7,15},{8,0},{9,1},... | collective-permute-start | bytes 221192 | tf_op jit(solution)/shard_map/ppermute | solution.py:360
  4.8 4.5 %collective-permute-start.3 = (bf16[288,128]{1,0:T(8,128)(2,1)S(1)}, bf16[288,128]{1,0:T(8,128)(2,1)S(1)}, u32[]{:S(2)}, u32[]{:S(2)}) collective-permute-start(bf16[288,128]{1,0:T(8,128)(2,1)S(1)} %get-tuple-element.52.refs_0_), channel_id=1, source_target_pairs={{0,2},{1,3},{2,0},{3,1},{4,6},{5,7},{6,4},{7,5},{8,10},{9,11},{10,... | collective-permute-start | bytes 221192 | tf_op jit(solution)/shard_map/ppermute | solution.py:360
  6.0 4.3 %collective-permute-start.2 = (bf16[288,128]{1,0:T(8,128)(2,1)S(1)}, bf16[288,128]{1,0:T(8,128)(2,1)S(1)}, u32[]{:S(2)}, u32[]{:S(2)}) collective-permute-start(bf16[288,128]{1,0:T(8,128)(2,1)S(1)} %get-tuple-element.52.refs_0_), channel_id=1, source_target_pairs={{0,4},{1,5},{2,6},{3,7},{4,0},{5,1},{6,2},{7,3},{8,12},{9,13},{10,... | collective-permute-start | bytes 221192 | tf_op jit(solution)/shard_map/ppermute | solution.py:360
  7.3 5.6 %collective-permute-start = (bf16[288,128]{1,0:T(8,128)(2,1)S(1)}, bf16[288,128]{1,0:T(8,128)(2,1)S(1)}, u32[]{:S(2)}, u32[]{:S(2)}) collective-permute-start(bf16[288,128]{1,0:T(8,128)(2,1)S(1)} %get-tuple-element.52.refs_0_), channel_id=1, source_target_pairs={{0,1},{1,0},{2,3},{3,2},{4,5},{5,4},{6,7},{7,6},{8,9},{9,8},{10,11... | collective-permute-start | bytes 221192 | tf_op jit(solution)/shard_map/ppermute | solution.py:360
  8.8 4.4 %collective-permute-start.6 = (bf16[288,128]{1,0:T(8,128)(2,1)S(1)}, bf16[288,128]{1,0:T(8,128)(2,1)S(1)}, u32[]{:S(2)}, u32[]{:S(2)}) collective-permute-start(bf16[288,128]{1,0:T(8,128)(2,1)S(1)} %collective-permute-done.1.refs_2_), channel_id=1, source_target_pairs={{0,4},{1,5},{2,6},{3,7},{4,0},{5,1},{6,2},{7,3},{8,12},{9,13},{10,... | collective-permute-start | bytes 221192 | tf_op jit(solution)/shard_map/ppermute | solution.py:360
  9.3 4.8 %collective-permute-start.9 = (bf16[288,128]{1,0:T(8,128)(2,1)S(1)}, bf16[288,128]{1,0:T(8,128)(2,1)S(1)}, u32[]{:S(2)}, u32[]{:S(2)}) collective-permute-start(bf16[288,128]{1,0:T(8,128)(2,1)S(1)} %collective-permute-done.3.refs_4_), channel_id=1, source_target_pairs={{0,4},{1,5},{2,6},{3,7},{4,0},{5,1},{6,2},{7,3},{8,12},{9,13},{10,... | collective-permute-start | bytes 221192 | tf_op jit(solution)/shard_map/ppermute | solution.py:360
  10.3 5.8 %collective-permute-start.5 = (bf16[288,128]{1,0:T(8,128)(2,1)S(1)}, bf16[288,128]{1,0:T(8,128)(2,1)S(1)}, u32[]{:S(2)}, u32[]{:S(2)}) collective-permute-start(bf16[288,128]{1,0:T(8,128)(2,1)S(1)} %collective-permute-done.2.refs_3_), channel_id=1, source_target_pairs={{0,1},{1,0},{2,3},{3,2},{4,5},{5,4},{6,7},{7,6},{8,9},{9,8},{10,11... | collective-permute-start | bytes 221192 | tf_op jit(solution)/shard_map/ppermute | solution.py:360
  11.7 4.5 %collective-permute-start.8 = (bf16[288,128]{1,0:T(8,128)(2,1)S(1)}, bf16[288,128]{1,0:T(8,128)(2,1)S(1)}, u32[]{:S(2)}, u32[]{:S(2)}) collective-permute-start(bf16[288,128]{1,0:T(8,128)(2,1)S(1)} %collective-permute-done.1.refs_2_), channel_id=1, source_target_pairs={{0,2},{1,3},{2,0},{3,1},{4,6},{5,7},{6,4},{7,5},{8,10},{9,11},{10,... | collective-permute-start | bytes 221192 | tf_op jit(solution)/shard_map/ppermute | solution.py:360
  12.9 3.7 %collective-permute-start.4 = (bf16[288,128]{1,0:T(8,128)(2,1)S(1)}, bf16[288,128]{1,0:T(8,128)(2,1)S(1)}, u32[]{:S(2)}, u32[]{:S(2)}) collective-permute-start(bf16[288,128]{1,0:T(8,128)(2,1)S(1)} %collective-permute-done.1.refs_2_), channel_id=1, source_target_pairs={{0,1},{1,0},{2,3},{3,2},{4,5},{5,4},{6,7},{7,6},{8,9},{9,8},{10,11... | collective-permute-start | bytes 221192 | tf_op jit(solution)/shard_map/ppermute | solution.py:360
  13.2 4.6 %collective-permute-start.13 = (bf16[288,128]{1,0:T(8,128)(2,1)S(1)}, bf16[288,128]{1,0:T(8,128)(2,1)S(1)}, u32[]{:S(2)}, u32[]{:S(2)}) collective-permute-start(bf16[288,128]{1,0:T(8,128)(2,1)S(1)} %collective-permute-done.6.refs_7_), channel_id=1, source_target_pairs={{0,2},{1,3},{2,0},{3,1},{4,6},{5,7},{6,4},{7,5},{8,10},{9,11},{10,... | collective-permute-start | bytes 221192 | tf_op jit(solution)/shard_map/ppermute | solution.py:360
  14.1 4.5 %collective-permute-start.7 = (bf16[288,128]{1,0:T(8,128)(2,1)S(1)}, bf16[288,128]{1,0:T(8,128)(2,1)S(1)}, u32[]{:S(2)}, u32[]{:S(2)}) collective-permute-start(bf16[288,128]{1,0:T(8,128)(2,1)S(1)} %collective-permute-done.3.refs_4_), channel_id=1, source_target_pairs={{0,1},{1,0},{2,3},{3,2},{4,5},{5,4},{6,7},{7,6},{8,9},{9,8},{10,11... | collective-permute-start | bytes 221192 | tf_op jit(solution)/shard_map/ppermute | solution.py:360
  16.1 2.6 %collective-permute-start.10 = (bf16[288,128]{1,0:T(8,128)(2,1)S(1)}, bf16[288,128]{1,0:T(8,128)(2,1)S(1)}, u32[]{:S(2)}, u32[]{:S(2)}) collective-permute-start(bf16[288,128]{1,0:T(8,128)(2,1)S(1)} %collective-permute-done.6.refs_7_), channel_id=1, source_target_pairs={{0,1},{1,0},{2,3},{3,2},{4,5},{5,4},{6,7},{7,6},{8,9},{9,8},{10,11... | collective-permute-start | bytes 221192 | tf_op jit(solution)/shard_map/ppermute | solution.py:360
  16.2 2.5 %collective-permute-start.12 = (bf16[288,128]{1,0:T(8,128)(2,1)S(1)}, bf16[288,128]{1,0:T(8,128)(2,1)S(1)}, u32[]{:S(2)}, u32[]{:S(2)}) collective-permute-start(bf16[288,128]{1,0:T(8,128)(2,1)S(1)} %collective-permute-done.9.refs_4_.refs_10_), channel_id=1, source_target_pairs={{0,1},{1,0},{2,3},{3,2},{4,5},{5,4},{6,7},{7,6},{8,9},{9,8},{10,11... | collective-permute-start | bytes 221192 | tf_op jit(solution)/shard_map/ppermute | solution.py:360
  16.6 2.1 %collective-permute-start.11 = (bf16[288,128]{1,0:T(8,128)(2,1)S(1)}, bf16[288,128]{1,0:T(8,128)(2,1)S(1)}, u32[]{:S(2)}, u32[]{:S(2)}) collective-permute-start(bf16[288,128]{1,0:T(8,128)(2,1)S(1)} %collective-permute-done.8.refs_3_.refs_9_), channel_id=1, source_target_pairs={{0,1},{1,0},{2,3},{3,2},{4,5},{5,4},{6,7},{7,6},{8,9},{9,8},{10,11... | collective-permute-start | bytes 221192 | tf_op jit(solution)/shard_map/ppermute | solution.py:360
  17.8 2.2 %collective-permute-start.14 = (bf16[288,128]{1,0:T(8,128)(2,1)S(1)}, bf16[288,128]{1,0:T(8,128)(2,1)S(1)}, u32[]{:S(2)}, u32[]{:S(2)}) collective-permute-start(bf16[288,128]{1,0:T(8,128)(2,1)S(1)} %collective-permute-done.13.refs_14_), channel_id=1, source_target_pairs={{0,1},{1,0},{2,3},{3,2},{4,5},{5,4},{6,7},{7,6},{8,9},{9,8},{10,11... | collective-permute-start | bytes 221192 | tf_op jit(solution)/shard_map/ppermute | solution.py:360

commit v7 on v6

--- a/solution.py
+++ b/solution.py
@@ -35,7 +35,7 @@
 
 
 def sigmoid(v):
-    return 0.5 * jnp.tanh(0.5 * v) + 0.5
+    return 1.0 / (1.0 + jnp.exp(-v))
 
 
 def normalize(v):
@@ -367,10 +367,10 @@
         hop(step, [x])
         hop(step, [d for d in list(blocks) if 0 < d and d % (2 * step) == 0])
     hop(x, [d for d in list(blocks) if not d & x and d ^ x not in blocks])
-    hop(core, [d for d in list(blocks) if d not in [14]])
+    last = devices - 1 - core
+    hop(core, [d for d in list(blocks) if d != last])
     order = sorted(range(devices), key=lambda d: (2 * d.bit_count() + (d & x) / x, -(d & core), -d))
-    blocks[15] = None
-    ordered = [blocks[d] for d in order]
+    ordered = [blocks.get(d) for d in order]
     per = LANES // hidden
     groups = n // per
     cuts = (groups // 2, groups - 1)
@@ -408,11 +408,8 @@
         compiler_params=pltpu.CompilerParams(vmem_limit_bytes=16 << 20),
         name="head",
     )(*head_in)
-    held = [blocks[d] for d in [14]]
-    held, head = lax.optimization_barrier((held, head))
-    for d, block in zip([14], held):
-        blocks[d] = block
-    hop(core, [14])
+    blocks[last], head = lax.optimization_barrier((blocks[last], head))
+    hop(core, [last])
     ordered = [blocks[d] for d in order]
     middle_in = [head[0], head[1], *span(*cuts), token_count, gain, bias, head[8], head[9], gate_weight]
     middle_out = (*stage_out(cuts[1] - cuts[0]), pltpu.VMEM((n, cuts[1] * LANES), f32))
@@ -597,10 +594,11 @@
         and length % (LANES // hidden) == 0
         and (LANES // hidden) % 8 == 0
         and length % 16 == 0
-        and devices & (devices - 1) == 0
         and length % devices == 0
         and length // devices <= LANES // hidden
-        and devices >= 4
+        and devices in (8, 16)
+        and 2 * KINDS * hidden == LANES
+        and length // (LANES // hidden) >= 4
         and length // 2 % (LANES // hidden) == 0
         and 2 * pair_acts.dtype.itemsize * length * length * channels <= WHOLE_BYTES
     )

time: 23.9 us -> 24 us (level)
  no operation moved by 1% of the time
where the time goes in v7:
time: 24 us; the launch traced here: 23.8 us
  starting transfers between devices  15.3 us (64%)
  Pallas kernels  7.11 us (30%)
  between operations  1.36 us (6%)
    ppermute x15, starting transfers between devices, hop(): blocks[d ^ step] = lax.ppermute(blocks[d], 'row', pairs)  15.3 us
    pallas_call x1, Pallas kernels, body_whole(): pl.pallas_call(functools.partial(tail_kernel, n, hidden, order, cuts), ou...  3.79 us
    pallas_call x1, Pallas kernels, body_whole(): pl.pallas_call(functools.partial(middle_kernel, n, hidden, order, cuts[0]...  1.3 us
    pallas_call x1, Pallas kernels, body_whole(): pl.pallas_call(functools.partial(head_kernel, n, hidden, order), out_shap...  1.09 us
    pallas_call x1, Pallas kernels, body_whole(): pl.pallas_call(load_kernel, out_shape=[pltpu.VMEM((2 * half, channels), b...  0.93 us
  transfers between devices with their start and end apart: 15, of which 0 were waited for; matrix products, arithmetic and copies ran while one was open for 0% of the time, Pallas kernels for 10%

profile of v7, /device:TPU:1, one launch (start us, length us, event | category | flops | bytes accessed | tf_op | source)
XLA Modules:
  0.0 23.8 jit_solution(4823598999035073659)
XLA Ops:
  0.6 0.9 %load.1 = (bf16[288,128]{1,0:T(8,128)(2,1)S(1)}, f32[1,128]{1,0:T(1,128)S(1)}, f32[1,128]{1,0:T(1,128)S(1)}, bf16[64,128]{1,0:T(8,128)(2,1)S(1)}, bf16[128,128]{...) custom-call(bf16[144,128]{1,0:T(8,128)(2,1)} %bitcast.8, ...), custom_call_target="tpu_custom_call" | custom-call | tf_op jit(solution)/shard_map/load/pallas_call | solution.py:346
  1.6 3.2 %collective-permute-start.1 = (bf16[288,128]{1,0:T(8,128)(2,1)S(1)}, bf16[288,128]{1,0:T(8,128)(2,1)S(1)}, u32[]{:S(2)}, u32[]{:S(2)}) collective-permute-start(bf16[288,128]{1,0:T(8,128)(2,1)S(1)} %get-tuple-element.52.refs_0_), channel_id=1, source_target_pairs={{0,8},{1,9},{2,10},{3,11},{4,12},{5,13},{6,14},{7,15},{8,0},{9,1},... | collective-permute-start | bytes 221192 | tf_op jit(solution)/shard_map/ppermute | solution.py:360
  4.8 1.2 %collective-permute-start.3 = (bf16[288,128]{1,0:T(8,128)(2,1)S(1)}, bf16[288,128]{1,0:T(8,128)(2,1)S(1)}, u32[]{:S(2)}, u32[]{:S(2)}) collective-permute-start(bf16[288,128]{1,0:T(8,128)(2,1)S(1)} %get-tuple-element.52.refs_0_), channel_id=1, source_target_pairs={{0,2},{1,3},{2,0},{3,1},{4,6},{5,7},{6,4},{7,5},{8,10},{9,11},{10,... | collective-permute-start | bytes 221192 | tf_op jit(solution)/shard_map/ppermute | solution.py:360
  6.0 1.3 %collective-permute-start.2 = (bf16[288,128]{1,0:T(8,128)(2,1)S(1)}, bf16[288,128]{1,0:T(8,128)(2,1)S(1)}, u32[]{:S(2)}, u32[]{:S(2)}) collective-permute-start(bf16[288,128]{1,0:T(8,128)(2,1)S(1)} %get-tuple-element.52.refs_0_), channel_id=1, source_target_pairs={{0,4},{1,5},{2,6},{3,7},{4,0},{5,1},{6,2},{7,3},{8,12},{9,13},{10,... | collective-permute-start | bytes 221192 | tf_op jit(solution)/shard_map/ppermute | solution.py:360
  7.3 1.5 %collective-permute-start = (bf16[288,128]{1,0:T(8,128)(2,1)S(1)}, bf16[288,128]{1,0:T(8,128)(2,1)S(1)}, u32[]{:S(2)}, u32[]{:S(2)}) collective-permute-start(bf16[288,128]{1,0:T(8,128)(2,1)S(1)} %get-tuple-element.52.refs_0_), channel_id=1, source_target_pairs={{0,1},{1,0},{2,3},{3,2},{4,5},{5,4},{6,7},{7,6},{8,9},{9,8},{10,11... | collective-permute-start | bytes 221192 | tf_op jit(solution)/shard_map/ppermute | solution.py:360
  8.8 0.5 %collective-permute-start.6 = (bf16[288,128]{1,0:T(8,128)(2,1)S(1)}, bf16[288,128]{1,0:T(8,128)(2,1)S(1)}, u32[]{:S(2)}, u32[]{:S(2)}) collective-permute-start(bf16[288,128]{1,0:T(8,128)(2,1)S(1)} %collective-permute-done.1.refs_2_), channel_id=1, source_target_pairs={{0,4},{1,5},{2,6},{3,7},{4,0},{5,1},{6,2},{7,3},{8,12},{9,13},{10,... | collective-permute-start | bytes 221192 | tf_op jit(solution)/shard_map/ppermute | solution.py:360
  9.3 1.0 %collective-permute-start.9 = (bf16[288,128]{1,0:T(8,128)(2,1)S(1)}, bf16[288,128]{1,0:T(8,128)(2,1)S(1)}, u32[]{:S(2)}, u32[]{:S(2)}) collective-permute-start(bf16[288,128]{1,0:T(8,128)(2,1)S(1)} %collective-permute-done.3.refs_4_), channel_id=1, source_target_pairs={{0,4},{1,5},{2,6},{3,7},{4,0},{5,1},{6,2},{7,3},{8,12},{9,13},{10,... | collective-permute-start | bytes 221192 | tf_op jit(solution)/shard_map/ppermute | solution.py:360
  10.3 0.0 collective-permute-done.2.refs_3_
  10.3 1.4 %collective-permute-start.5 = (bf16[288,128]{1,0:T(8,128)(2,1)S(1)}, bf16[288,128]{1,0:T(8,128)(2,1)S(1)}, u32[]{:S(2)}, u32[]{:S(2)}) collective-permute-start(bf16[288,128]{1,0:T(8,128)(2,1)S(1)} %collective-permute-done.2.refs_3_), channel_id=1, source_target_pairs={{0,1},{1,0},{2,3},{3,2},{4,5},{5,4},{6,7},{7,6},{8,9},{9,8},{10,11... | collective-permute-start | bytes 221192 | tf_op jit(solution)/shard_map/ppermute | solution.py:360
  11.7 1.2 %collective-permute-start.8 = (bf16[288,128]{1,0:T(8,128)(2,1)S(1)}, bf16[288,128]{1,0:T(8,128)(2,1)S(1)}, u32[]{:S(2)}, u32[]{:S(2)}) collective-permute-start(bf16[288,128]{1,0:T(8,128)(2,1)S(1)} %collective-permute-done.1.refs_2_), channel_id=1, source_target_pairs={{0,2},{1,3},{2,0},{3,1},{4,6},{5,7},{6,4},{7,5},{8,10},{9,11},{10,... | collective-permute-start | bytes 221192 | tf_op jit(solution)/shard_map/ppermute | solution.py:360
  12.9 0.0 collective-permute-done.refs_1_
  12.9 0.3 %collective-permute-start.4 = (bf16[288,128]{1,0:T(8,128)(2,1)S(1)}, bf16[288,128]{1,0:T(8,128)(2,1)S(1)}, u32[]{:S(2)}, u32[]{:S(2)}) collective-permute-start(bf16[288,128]{1,0:T(8,128)(2,1)S(1)} %collective-permute-done.1.refs_2_), channel_id=1, source_target_pairs={{0,1},{1,0},{2,3},{3,2},{4,5},{5,4},{6,7},{7,6},{8,9},{9,8},{10,11... | collective-permute-start | bytes 221192 | tf_op jit(solution)/shard_map/ppermute | solution.py:360
  13.2 0.0 collective-permute-done.6.refs_7_
  13.2 0.3 %collective-permute-start.13 = (bf16[288,128]{1,0:T(8,128)(2,1)S(1)}, bf16[288,128]{1,0:T(8,128)(2,1)S(1)}, u32[]{:S(2)}, u32[]{:S(2)}) collective-permute-start(bf16[288,128]{1,0:T(8,128)(2,1)S(1)} %collective-permute-done.6.refs_7_), channel_id=1, source_target_pairs={{0,2},{1,3},{2,0},{3,1},{4,6},{5,7},{6,4},{7,5},{8,10},{9,11},{10,... | collective-permute-start | bytes 221192 | tf_op jit(solution)/shard_map/ppermute | solution.py:360
  14.1 2.0 %collective-permute-start.7 = (bf16[288,128]{1,0:T(8,128)(2,1)S(1)}, bf16[288,128]{1,0:T(8,128)(2,1)S(1)}, u32[]{:S(2)}, u32[]{:S(2)}) collective-permute-start(bf16[288,128]{1,0:T(8,128)(2,1)S(1)} %collective-permute-done.3.refs_4_), channel_id=1, source_target_pairs={{0,1},{1,0},{2,3},{3,2},{4,5},{5,4},{6,7},{7,6},{8,9},{9,8},{10,11... | collective-permute-start | bytes 221192 | tf_op jit(solution)/shard_map/ppermute | solution.py:360
  16.1 0.1 collective-permute-start.10
  16.2 0.0 collective-permute-done.8.refs_3_.refs_9_
  16.2 0.4 %collective-permute-start.12 = (bf16[288,128]{1,0:T(8,128)(2,1)S(1)}, bf16[288,128]{1,0:T(8,128)(2,1)S(1)}, u32[]{:S(2)}, u32[]{:S(2)}) collective-permute-start(bf16[288,128]{1,0:T(8,128)(2,1)S(1)} %collective-permute-done.9.refs_4_.refs_10_), channel_id=1, source_target_pairs={{0,1},{1,0},{2,3},{3,2},{4,5},{5,4},{6,7},{7,6},{8,9},{9,8},{10,11... | collective-permute-start | bytes 221192 | tf_op jit(solution)/shard_map/ppermute | solution.py:360
  16.6 0.1 collective-permute-start.11
  16.7 1.1 %head.1 = (bf16[144,128]{1,0:T(8,128)(2,1)S(1)}, bf16[144,128]{1,0:T(8,128)(2,1)S(1)}, f32[2,144,128]{2,1,0:T(8,128)S(1)}, f32[2,144,128]{2,1,0:T(8,128)S(1)}, b...) custom-call(bf16[288,128]{1,0:T(8,128)(2,1)S(1)} %get-tuple-element., ...), custom_call_target="tpu_custom_call" | custom-call | tf_op jit(solution)/shard_map/head/pallas_call | solution.py:403
  17.8 0.0 collective-permute-done.13.refs_14_
  17.8 0.9 %collective-permute-start.14 = (bf16[288,128]{1,0:T(8,128)(2,1)S(1)}, bf16[288,128]{1,0:T(8,128)(2,1)S(1)}, u32[]{:S(2)}, u32[]{:S(2)}) collective-permute-start(bf16[288,128]{1,0:T(8,128)(2,1)S(1)} %collective-permute-done.13.refs_14_), channel_id=1, source_target_pairs={{0,1},{1,0},{2,3},{3,2},{4,5},{5,4},{6,7},{7,6},{8,9},{9,8},{10,11... | collective-permute-start | bytes 221192 | tf_op jit(solution)/shard_map/ppermute | solution.py:360
  18.7 1.3 %middle.1 = (bf16[96,128]{1,0:T(8,128)(2,1)S(1)}, bf16[96,128]{1,0:T(8,128)(2,1)S(1)}, f32[2,96,128]{2,1,0:T(8,128)S(1)}, f32[2,96,128]{2,1,0:T(8,128)S(1)}, bf1...) custom-call(bf16[144,128]{1,0:T(8,128)(2,1)S(1)} %get-tuple-element., ...), custom_call_target="tpu_custom_call" | custom-call | tf_op jit(solution)/shard_map/middle/pallas_call | solution.py:416
  20.0 3.8 %tail.1 = (bf16[3,48,128]{2,1,0:T(8,128)(2,1)}, f32[3,48,128]{2,1,0:T(8,128)}, f32[64,128]{1,0:T(8,128)}, f32[128,128]{1,0:T(8,128)}, f32[16,128]{1,0:T(8,128)}) custom-call(bf16[288,128]{1,0:T(8,128)(2,1)S(1)} %get-tuple-element.52.refs_0_, bf16[288,128]{1,0:T(8,128)(2,1)S(1)} %collective-permute-done.refs_1_, ...), custom_call_target="tpu_custom_call" | custom-call | tf_op jit(solution)/shard_map/tail/pallas_call | solution.py:425
  (10 shorter events, 0.0 us)
Async XLA Ops:
  1.6 7.2 %collective-permute-start.1 = (bf16[288,128]{1,0:T(8,128)(2,1)S(1)}, bf16[288,128]{1,0:T(8,128)(2,1)S(1)}, u32[]{:S(2)}, u32[]{:S(2)}) collective-permute-start(bf16[288,128]{1,0:T(8,128)(2,1)S(1)} %get-tuple-element.52.refs_0_), channel_id=1, source_target_pairs={{0,8},{1,9},{2,10},{3,11},{4,12},{5,13},{6,14},{7,15},{8,0},{9,1},... | collective-permute-start | bytes 221192 | tf_op jit(solution)/shard_map/ppermute | solution.py:360
  4.8 4.5 %collective-permute-start.3 = (bf16[288,128]{1,0:T(8,128)(2,1)S(1)}, bf16[288,128]{1,0:T(8,128)(2,1)S(1)}, u32[]{:S(2)}, u32[]{:S(2)}) collective-permute-start(bf16[288,128]{1,0:T(8,128)(2,1)S(1)} %get-tuple-element.52.refs_0_), channel_id=1, source_target_pairs={{0,2},{1,3},{2,0},{3,1},{4,6},{5,7},{6,4},{7,5},{8,10},{9,11},{10,... | collective-permute-start | bytes 221192 | tf_op jit(solution)/shard_map/ppermute | solution.py:360
  6.0 4.3 %collective-permute-start.2 = (bf16[288,128]{1,0:T(8,128)(2,1)S(1)}, bf16[288,128]{1,0:T(8,128)(2,1)S(1)}, u32[]{:S(2)}, u32[]{:S(2)}) collective-permute-start(bf16[288,128]{1,0:T(8,128)(2,1)S(1)} %get-tuple-element.52.refs_0_), channel_id=1, source_target_pairs={{0,4},{1,5},{2,6},{3,7},{4,0},{5,1},{6,2},{7,3},{8,12},{9,13},{10,... | collective-permute-start | bytes 221192 | tf_op jit(solution)/shard_map/ppermute | solution.py:360
  7.3 5.6 %collective-permute-start = (bf16[288,128]{1,0:T(8,128)(2,1)S(1)}, bf16[288,128]{1,0:T(8,128)(2,1)S(1)}, u32[]{:S(2)}, u32[]{:S(2)}) collective-permute-start(bf16[288,128]{1,0:T(8,128)(2,1)S(1)} %get-tuple-element.52.refs_0_), channel_id=1, source_target_pairs={{0,1},{1,0},{2,3},{3,2},{4,5},{5,4},{6,7},{7,6},{8,9},{9,8},{10,11... | collective-permute-start | bytes 221192 | tf_op jit(solution)/shard_map/ppermute | solution.py:360
  8.8 4.4 %collective-permute-start.6 = (bf16[288,128]{1,0:T(8,128)(2,1)S(1)}, bf16[288,128]{1,0:T(8,128)(2,1)S(1)}, u32[]{:S(2)}, u32[]{:S(2)}) collective-permute-start(bf16[288,128]{1,0:T(8,128)(2,1)S(1)} %collective-permute-done.1.refs_2_), channel_id=1, source_target_pairs={{0,4},{1,5},{2,6},{3,7},{4,0},{5,1},{6,2},{7,3},{8,12},{9,13},{10,... | collective-permute-start | bytes 221192 | tf_op jit(solution)/shard_map/ppermute | solution.py:360
  9.3 4.8 %collective-permute-start.9 = (bf16[288,128]{1,0:T(8,128)(2,1)S(1)}, bf16[288,128]{1,0:T(8,128)(2,1)S(1)}, u32[]{:S(2)}, u32[]{:S(2)}) collective-permute-start(bf16[288,128]{1,0:T(8,128)(2,1)S(1)} %collective-permute-done.3.refs_4_), channel_id=1, source_target_pairs={{0,4},{1,5},{2,6},{3,7},{4,0},{5,1},{6,2},{7,3},{8,12},{9,13},{10,... | collective-permute-start | bytes 221192 | tf_op jit(solution)/shard_map/ppermute | solution.py:360
  10.3 5.8 %collective-permute-start.5 = (bf16[288,128]{1,0:T(8,128)(2,1)S(1)}, bf16[288,128]{1,0:T(8,128)(2,1)S(1)}, u32[]{:S(2)}, u32[]{:S(2)}) collective-permute-start(bf16[288,128]{1,0:T(8,128)(2,1)S(1)} %collective-permute-done.2.refs_3_), channel_id=1, source_target_pairs={{0,1},{1,0},{2,3},{3,2},{4,5},{5,4},{6,7},{7,6},{8,9},{9,8},{10,11... | collective-permute-start | bytes 221192 | tf_op jit(solution)/shard_map/ppermute | solution.py:360
  11.7 4.5 %collective-permute-start.8 = (bf16[288,128]{1,0:T(8,128)(2,1)S(1)}, bf16[288,128]{1,0:T(8,128)(2,1)S(1)}, u32[]{:S(2)}, u32[]{:S(2)}) collective-permute-start(bf16[288,128]{1,0:T(8,128)(2,1)S(1)} %collective-permute-done.1.refs_2_), channel_id=1, source_target_pairs={{0,2},{1,3},{2,0},{3,1},{4,6},{5,7},{6,4},{7,5},{8,10},{9,11},{10,... | collective-permute-start | bytes 221192 | tf_op jit(solution)/shard_map/ppermute | solution.py:360
  12.9 3.7 %collective-permute-start.4 = (bf16[288,128]{1,0:T(8,128)(2,1)S(1)}, bf16[288,128]{1,0:T(8,128)(2,1)S(1)}, u32[]{:S(2)}, u32[]{:S(2)}) collective-permute-start(bf16[288,128]{1,0:T(8,128)(2,1)S(1)} %collective-permute-done.1.refs_2_), channel_id=1, source_target_pairs={{0,1},{1,0},{2,3},{3,2},{4,5},{5,4},{6,7},{7,6},{8,9},{9,8},{10,11... | collective-permute-start | bytes 221192 | tf_op jit(solution)/shard_map/ppermute | solution.py:360
  13.2 4.6 %collective-permute-start.13 = (bf16[288,128]{1,0:T(8,128)(2,1)S(1)}, bf16[288,128]{1,0:T(8,128)(2,1)S(1)}, u32[]{:S(2)}, u32[]{:S(2)}) collective-permute-start(bf16[288,128]{1,0:T(8,128)(2,1)S(1)} %collective-permute-done.6.refs_7_), channel_id=1, source_target_pairs={{0,2},{1,3},{2,0},{3,1},{4,6},{5,7},{6,4},{7,5},{8,10},{9,11},{10,... | collective-permute-start | bytes 221192 | tf_op jit(solution)/shard_map/ppermute | solution.py:360
  14.1 4.5 %collective-permute-start.7 = (bf16[288,128]{1,0:T(8,128)(2,1)S(1)}, bf16[288,128]{1,0:T(8,128)(2,1)S(1)}, u32[]{:S(2)}, u32[]{:S(2)}) collective-permute-start(bf16[288,128]{1,0:T(8,128)(2,1)S(1)} %collective-permute-done.3.refs_4_), channel_id=1, source_target_pairs={{0,1},{1,0},{2,3},{3,2},{4,5},{5,4},{6,7},{7,6},{8,9},{9,8},{10,11... | collective-permute-start | bytes 221192 | tf_op jit(solution)/shard_map/ppermute | solution.py:360
  16.1 2.6 %collective-permute-start.10 = (bf16[288,128]{1,0:T(8,128)(2,1)S(1)}, bf16[288,128]{1,0:T(8,128)(2,1)S(1)}, u32[]{:S(2)}, u32[]{:S(2)}) collective-permute-start(bf16[288,128]{1,0:T(8,128)(2,1)S(1)} %collective-permute-done.6.refs_7_), channel_id=1, source_target_pairs={{0,1},{1,0},{2,3},{3,2},{4,5},{5,4},{6,7},{7,6},{8,9},{9,8},{10,11... | collective-permute-start | bytes 221192 | tf_op jit(solution)/shard_map/ppermute | solution.py:360
  16.2 2.5 %collective-permute-start.12 = (bf16[288,128]{1,0:T(8,128)(2,1)S(1)}, bf16[288,128]{1,0:T(8,128)(2,1)S(1)}, u32[]{:S(2)}, u32[]{:S(2)}) collective-permute-start(bf16[288,128]{1,0:T(8,128)(2,1)S(1)} %collective-permute-done.9.refs_4_.refs_10_), channel_id=1, source_target_pairs={{0,1},{1,0},{2,3},{3,2},{4,5},{5,4},{6,7},{7,6},{8,9},{9,8},{10,11... | collective-permute-start | bytes 221192 | tf_op jit(solution)/shard_map/ppermute | solution.py:360
  16.6 2.1 %collective-permute-start.11 = (bf16[288,128]{1,0:T(8,128)(2,1)S(1)}, bf16[288,128]{1,0:T(8,128)(2,1)S(1)}, u32[]{:S(2)}, u32[]{:S(2)}) collective-permute-start(bf16[288,128]{1,0:T(8,128)(2,1)S(1)} %collective-permute-done.8.refs_3_.refs_9_), channel_id=1, source_target_pairs={{0,1},{1,0},{2,3},{3,2},{4,5},{5,4},{6,7},{7,6},{8,9},{9,8},{10,11... | collective-permute-start | bytes 221192 | tf_op jit(solution)/shard_map/ppermute | solution.py:360
  17.8 2.2 %collective-permute-start.14 = (bf16[288,128]{1,0:T(8,128)(2,1)S(1)}, bf16[288,128]{1,0:T(8,128)(2,1)S(1)}, u32[]{:S(2)}, u32[]{:S(2)}) collective-permute-start(bf16[288,128]{1,0:T(8,128)(2,1)S(1)} %collective-permute-done.13.refs_14_), channel_id=1, source_target_pairs={{0,1},{1,0},{2,3},{3,2},{4,5},{5,4},{6,7},{7,6},{8,9},{9,8},{10,11... | collective-permute-start | bytes 221192 | tf_op jit(solution)/shard_map/ppermute | solution.py:360

commit v8 on v7

--- a/solution.py
+++ b/solution.py
@@ -295,10 +295,6 @@
     by_place = dot(dp, pick_ref[...]).astype(bf16)
     for q in range(half):
         put(dp_ref, q, 0, by_place[:, q * LANES : (q + 1) * LANES])
-    project_grad = sum_pairs(dp_ref).T
-    width = KINDS * hidden
-    project_grad_ref[...] = (project_grad[:width, :LANES] + project_grad[width:, LANES:]) / n
-
     tiled = [project_t[kind * hidden : (kind + 1) * hidden] for kind in range(KINDS) for _ in range(per)]
     place = iota((n, KINDS * LANES), 1) % LANES // hidden
     dp_rows = [jnp.where(place == r, dp[:n], jnp.zeros_like(dp[:n])) for r in range(rows)]
@@ -311,6 +307,10 @@
     pair_grad = zs * (u - first - zhat * second)
     for r in range(rows):
         pair_ref[r] = pair_grad[r * n : (r + 1) * n]
+
+    project_grad = sum_pairs(dp_ref).T
+    width = KINDS * hidden
+    project_grad_ref[...] = (project_grad[:width, :LANES] + project_grad[width:, LANES:]) / n
 
 
 def body_whole(

time: 24 us -> 23.8 us (level)
  no operation moved by 1% of the time
where the time goes in v8:
time: 23.8 us; the launch traced here: 23.6 us
  starting transfers between devices  15.3 us (64%)
  Pallas kernels  6.99 us (29%)
  between operations  1.36 us (6%)
    ppermute x15, starting transfers between devices, hop(): blocks[d ^ step] = lax.ppermute(blocks[d], 'row', pairs)  15.3 us
    pallas_call x1, Pallas kernels, body_whole(): pl.pallas_call(functools.partial(tail_kernel, n, hidden, order, cuts), ou...  3.67 us
    pallas_call x1, Pallas kernels, body_whole(): pl.pallas_call(functools.partial(middle_kernel, n, hidden, order, cuts[0]...  1.3 us
    pallas_call x1, Pallas kernels, body_whole(): pl.pallas_call(functools.partial(head_kernel, n, hidden, order), out_shap...  1.09 us
    pallas_call x1, Pallas kernels, body_whole(): pl.pallas_call(load_kernel, out_shape=[pltpu.VMEM((2 * half, channels), b...  0.93 us
  transfers between devices with their start and end apart: 15, of which 0 were waited for; matrix products, arithmetic and copies ran while one was open for 0% of the time, Pallas kernels for 10%

profile of v8, /device:TPU:1, one launch (start us, length us, event | category | flops | bytes accessed | tf_op | source)
XLA Modules:
  0.0 23.6 jit_solution(15096579255101868897)
XLA Ops:
  0.6 0.9 %load.1 = (bf16[288,128]{1,0:T(8,128)(2,1)S(1)}, f32[1,128]{1,0:T(1,128)S(1)}, f32[1,128]{1,0:T(1,128)S(1)}, bf16[64,128]{1,0:T(8,128)(2,1)S(1)}, bf16[128,128]{...) custom-call(bf16[144,128]{1,0:T(8,128)(2,1)} %bitcast.8, ...), custom_call_target="tpu_custom_call" | custom-call | tf_op jit(solution)/shard_map/load/pallas_call | solution.py:346
  1.6 3.2 %collective-permute-start.1 = (bf16[288,128]{1,0:T(8,128)(2,1)S(1)}, bf16[288,128]{1,0:T(8,128)(2,1)S(1)}, u32[]{:S(2)}, u32[]{:S(2)}) collective-permute-start(bf16[288,128]{1,0:T(8,128)(2,1)S(1)} %get-tuple-element.52.refs_0_), channel_id=1, source_target_pairs={{0,8},{1,9},{2,10},{3,11},{4,12},{5,13},{6,14},{7,15},{8,0},{9,1},... | collective-permute-start | bytes 221192 | tf_op jit(solution)/shard_map/ppermute | solution.py:360
  4.8 1.2 %collective-permute-start.3 = (bf16[288,128]{1,0:T(8,128)(2,1)S(1)}, bf16[288,128]{1,0:T(8,128)(2,1)S(1)}, u32[]{:S(2)}, u32[]{:S(2)}) collective-permute-start(bf16[288,128]{1,0:T(8,128)(2,1)S(1)} %get-tuple-element.52.refs_0_), channel_id=1, source_target_pairs={{0,2},{1,3},{2,0},{3,1},{4,6},{5,7},{6,4},{7,5},{8,10},{9,11},{10,... | collective-permute-start | bytes 221192 | tf_op jit(solution)/shard_map/ppermute | solution.py:360
  6.0 1.3 %collective-permute-start.2 = (bf16[288,128]{1,0:T(8,128)(2,1)S(1)}, bf16[288,128]{1,0:T(8,128)(2,1)S(1)}, u32[]{:S(2)}, u32[]{:S(2)}) collective-permute-start(bf16[288,128]{1,0:T(8,128)(2,1)S(1)} %get-tuple-element.52.refs_0_), channel_id=1, source_target_pairs={{0,4},{1,5},{2,6},{3,7},{4,0},{5,1},{6,2},{7,3},{8,12},{9,13},{10,... | collective-permute-start | bytes 221192 | tf_op jit(solution)/shard_map/ppermute | solution.py:360
  7.3 1.5 %collective-permute-start = (bf16[288,128]{1,0:T(8,128)(2,1)S(1)}, bf16[288,128]{1,0:T(8,128)(2,1)S(1)}, u32[]{:S(2)}, u32[]{:S(2)}) collective-permute-start(bf16[288,128]{1,0:T(8,128)(2,1)S(1)} %get-tuple-element.52.refs_0_), channel_id=1, source_target_pairs={{0,1},{1,0},{2,3},{3,2},{4,5},{5,4},{6,7},{7,6},{8,9},{9,8},{10,11... | collective-permute-start | bytes 221192 | tf_op jit(solution)/shard_map/ppermute | solution.py:360
  8.8 0.0 collective-permute-done.1.refs_2_
  8.8 0.5 %collective-permute-start.6 = (bf16[288,128]{1,0:T(8,128)(2,1)S(1)}, bf16[288,128]{1,0:T(8,128)(2,1)S(1)}, u32[]{:S(2)}, u32[]{:S(2)}) collective-permute-start(bf16[288,128]{1,0:T(8,128)(2,1)S(1)} %collective-permute-done.1.refs_2_), channel_id=1, source_target_pairs={{0,4},{1,5},{2,6},{3,7},{4,0},{5,1},{6,2},{7,3},{8,12},{9,13},{10,... | collective-permute-start | bytes 221192 | tf_op jit(solution)/shard_map/ppermute | solution.py:360
  9.3 1.0 %collective-permute-start.9 = (bf16[288,128]{1,0:T(8,128)(2,1)S(1)}, bf16[288,128]{1,0:T(8,128)(2,1)S(1)}, u32[]{:S(2)}, u32[]{:S(2)}) collective-permute-start(bf16[288,128]{1,0:T(8,128)(2,1)S(1)} %collective-permute-done.3.refs_4_), channel_id=1, source_target_pairs={{0,4},{1,5},{2,6},{3,7},{4,0},{5,1},{6,2},{7,3},{8,12},{9,13},{10,... | collective-permute-start | bytes 221192 | tf_op jit(solution)/shard_map/ppermute | solution.py:360
  10.3 1.4 %collective-permute-start.5 = (bf16[288,128]{1,0:T(8,128)(2,1)S(1)}, bf16[288,128]{1,0:T(8,128)(2,1)S(1)}, u32[]{:S(2)}, u32[]{:S(2)}) collective-permute-start(bf16[288,128]{1,0:T(8,128)(2,1)S(1)} %collective-permute-done.2.refs_3_), channel_id=1, source_target_pairs={{0,1},{1,0},{2,3},{3,2},{4,5},{5,4},{6,7},{7,6},{8,9},{9,8},{10,11... | collective-permute-start | bytes 221192 | tf_op jit(solution)/shard_map/ppermute | solution.py:360
  11.7 1.2 %collective-permute-start.8 = (bf16[288,128]{1,0:T(8,128)(2,1)S(1)}, bf16[288,128]{1,0:T(8,128)(2,1)S(1)}, u32[]{:S(2)}, u32[]{:S(2)}) collective-permute-start(bf16[288,128]{1,0:T(8,128)(2,1)S(1)} %collective-permute-done.1.refs_2_), channel_id=1, source_target_pairs={{0,2},{1,3},{2,0},{3,1},{4,6},{5,7},{6,4},{7,5},{8,10},{9,11},{10,... | collective-permute-start | bytes 221192 | tf_op jit(solution)/shard_map/ppermute | solution.py:360
  12.9 0.3 %collective-permute-start.4 = (bf16[288,128]{1,0:T(8,128)(2,1)S(1)}, bf16[288,128]{1,0:T(8,128)(2,1)S(1)}, u32[]{:S(2)}, u32[]{:S(2)}) collective-permute-start(bf16[288,128]{1,0:T(8,128)(2,1)S(1)} %collective-permute-done.1.refs_2_), channel_id=1, source_target_pairs={{0,1},{1,0},{2,3},{3,2},{4,5},{5,4},{6,7},{7,6},{8,9},{9,8},{10,11... | collective-permute-start | bytes 221192 | tf_op jit(solution)/shard_map/ppermute | solution.py:360
  13.2 0.0 collective-permute-done.6.refs_7_
  13.2 0.3 %collective-permute-start.13 = (bf16[288,128]{1,0:T(8,128)(2,1)S(1)}, bf16[288,128]{1,0:T(8,128)(2,1)S(1)}, u32[]{:S(2)}, u32[]{:S(2)}) collective-permute-start(bf16[288,128]{1,0:T(8,128)(2,1)S(1)} %collective-permute-done.6.refs_7_), channel_id=1, source_target_pairs={{0,2},{1,3},{2,0},{3,1},{4,6},{5,7},{6,4},{7,5},{8,10},{9,11},{10,... | collective-permute-start | bytes 221192 | tf_op jit(solution)/shard_map/ppermute | solution.py:360
  14.1 0.0 collective-permute-done.9.refs_4_.refs_10_
  14.1 2.0 %collective-permute-start.7 = (bf16[288,128]{1,0:T(8,128)(2,1)S(1)}, bf16[288,128]{1,0:T(8,128)(2,1)S(1)}, u32[]{:S(2)}, u32[]{:S(2)}) collective-permute-start(bf16[288,128]{1,0:T(8,128)(2,1)S(1)} %collective-permute-done.3.refs_4_), channel_id=1, source_target_pairs={{0,1},{1,0},{2,3},{3,2},{4,5},{5,4},{6,7},{7,6},{8,9},{9,8},{10,11... | collective-permute-start | bytes 221192 | tf_op jit(solution)/shard_map/ppermute | solution.py:360
  16.1 0.0 collective-permute-done.5.refs_6_
  16.1 0.1 collective-permute-start.10
  16.2 0.4 %collective-permute-start.12 = (bf16[288,128]{1,0:T(8,128)(2,1)S(1)}, bf16[288,128]{1,0:T(8,128)(2,1)S(1)}, u32[]{:S(2)}, u32[]{:S(2)}) collective-permute-start(bf16[288,128]{1,0:T(8,128)(2,1)S(1)} %collective-permute-done.9.refs_4_.refs_10_), channel_id=1, source_target_pairs={{0,1},{1,0},{2,3},{3,2},{4,5},{5,4},{6,7},{7,6},{8,9},{9,8},{10,11... | collective-permute-start | bytes 221192 | tf_op jit(solution)/shard_map/ppermute | solution.py:360
  16.6 0.0 collective-permute-done.4.refs_5_
  16.6 0.1 collective-permute-start.11
  16.7 1.1 %head.1 = (bf16[144,128]{1,0:T(8,128)(2,1)S(1)}, bf16[144,128]{1,0:T(8,128)(2,1)S(1)}, f32[2,144,128]{2,1,0:T(8,128)S(1)}, f32[2,144,128]{2,1,0:T(8,128)S(1)}, b...) custom-call(bf16[288,128]{1,0:T(8,128)(2,1)S(1)} %get-tuple-element., ...), custom_call_target="tpu_custom_call" | custom-call | tf_op jit(solution)/shard_map/head/pallas_call | solution.py:403
  17.8 0.9 %collective-permute-start.14 = (bf16[288,128]{1,0:T(8,128)(2,1)S(1)}, bf16[288,128]{1,0:T(8,128)(2,1)S(1)}, u32[]{:S(2)}, u32[]{:S(2)}) collective-permute-start(bf16[288,128]{1,0:T(8,128)(2,1)S(1)} %collective-permute-done.13.refs_14_), channel_id=1, source_target_pairs={{0,1},{1,0},{2,3},{3,2},{4,5},{5,4},{6,7},{7,6},{8,9},{9,8},{10,11... | collective-permute-start | bytes 221192 | tf_op jit(solution)/shard_map/ppermute | solution.py:360
  18.7 1.3 %middle.1 = (bf16[96,128]{1,0:T(8,128)(2,1)S(1)}, bf16[96,128]{1,0:T(8,128)(2,1)S(1)}, f32[2,96,128]{2,1,0:T(8,128)S(1)}, f32[2,96,128]{2,1,0:T(8,128)S(1)}, bf1...) custom-call(bf16[144,128]{1,0:T(8,128)(2,1)S(1)} %get-tuple-element., ...), custom_call_target="tpu_custom_call" | custom-call | tf_op jit(solution)/shard_map/middle/pallas_call | solution.py:416
  20.0 3.7 %tail.1 = (bf16[3,48,128]{2,1,0:T(8,128)(2,1)}, f32[3,48,128]{2,1,0:T(8,128)}, f32[64,128]{1,0:T(8,128)}, f32[128,128]{1,0:T(8,128)}, f32[16,128]{1,0:T(8,128)}) custom-call(bf16[288,128]{1,0:T(8,128)(2,1)S(1)} %get-tuple-element.52.refs_0_, bf16[288,128]{1,0:T(8,128)(2,1)S(1)} %collective-permute-done.refs_1_, ...), custom_call_target="tpu_custom_call" | custom-call | tf_op jit(solution)/shard_map/tail/pallas_call | solution.py:425
  (10 shorter events, 0.0 us)
Async XLA Ops:
  1.6 7.2 %collective-permute-start.1 = (bf16[288,128]{1,0:T(8,128)(2,1)S(1)}, bf16[288,128]{1,0:T(8,128)(2,1)S(1)}, u32[]{:S(2)}, u32[]{:S(2)}) collective-permute-start(bf16[288,128]{1,0:T(8,128)(2,1)S(1)} %get-tuple-element.52.refs_0_), channel_id=1, source_target_pairs={{0,8},{1,9},{2,10},{3,11},{4,12},{5,13},{6,14},{7,15},{8,0},{9,1},... | collective-permute-start | bytes 221192 | tf_op jit(solution)/shard_map/ppermute | solution.py:360
  4.8 4.5 %collective-permute-start.3 = (bf16[288,128]{1,0:T(8,128)(2,1)S(1)}, bf16[288,128]{1,0:T(8,128)(2,1)S(1)}, u32[]{:S(2)}, u32[]{:S(2)}) collective-permute-start(bf16[288,128]{1,0:T(8,128)(2,1)S(1)} %get-tuple-element.52.refs_0_), channel_id=1, source_target_pairs={{0,2},{1,3},{2,0},{3,1},{4,6},{5,7},{6,4},{7,5},{8,10},{9,11},{10,... | collective-permute-start | bytes 221192 | tf_op jit(solution)/shard_map/ppermute | solution.py:360
  6.0 4.3 %collective-permute-start.2 = (bf16[288,128]{1,0:T(8,128)(2,1)S(1)}, bf16[288,128]{1,0:T(8,128)(2,1)S(1)}, u32[]{:S(2)}, u32[]{:S(2)}) collective-permute-start(bf16[288,128]{1,0:T(8,128)(2,1)S(1)} %get-tuple-element.52.refs_0_), channel_id=1, source_target_pairs={{0,4},{1,5},{2,6},{3,7},{4,0},{5,1},{6,2},{7,3},{8,12},{9,13},{10,... | collective-permute-start | bytes 221192 | tf_op jit(solution)/shard_map/ppermute | solution.py:360
  7.3 5.6 %collective-permute-start = (bf16[288,128]{1,0:T(8,128)(2,1)S(1)}, bf16[288,128]{1,0:T(8,128)(2,1)S(1)}, u32[]{:S(2)}, u32[]{:S(2)}) collective-permute-start(bf16[288,128]{1,0:T(8,128)(2,1)S(1)} %get-tuple-element.52.refs_0_), channel_id=1, source_target_pairs={{0,1},{1,0},{2,3},{3,2},{4,5},{5,4},{6,7},{7,6},{8,9},{9,8},{10,11... | collective-permute-start | bytes 221192 | tf_op jit(solution)/shard_map/ppermute | solution.py:360
  8.8 4.4 %collective-permute-start.6 = (bf16[288,128]{1,0:T(8,128)(2,1)S(1)}, bf16[288,128]{1,0:T(8,128)(2,1)S(1)}, u32[]{:S(2)}, u32[]{:S(2)}) collective-permute-start(bf16[288,128]{1,0:T(8,128)(2,1)S(1)} %collective-permute-done.1.refs_2_), channel_id=1, source_target_pairs={{0,4},{1,5},{2,6},{3,7},{4,0},{5,1},{6,2},{7,3},{8,12},{9,13},{10,... | collective-permute-start | bytes 221192 | tf_op jit(solution)/shard_map/ppermute | solution.py:360
  9.3 4.8 %collective-permute-start.9 = (bf16[288,128]{1,0:T(8,128)(2,1)S(1)}, bf16[288,128]{1,0:T(8,128)(2,1)S(1)}, u32[]{:S(2)}, u32[]{:S(2)}) collective-permute-start(bf16[288,128]{1,0:T(8,128)(2,1)S(1)} %collective-permute-done.3.refs_4_), channel_id=1, source_target_pairs={{0,4},{1,5},{2,6},{3,7},{4,0},{5,1},{6,2},{7,3},{8,12},{9,13},{10,... | collective-permute-start | bytes 221192 | tf_op jit(solution)/shard_map/ppermute | solution.py:360
  10.3 5.8 %collective-permute-start.5 = (bf16[288,128]{1,0:T(8,128)(2,1)S(1)}, bf16[288,128]{1,0:T(8,128)(2,1)S(1)}, u32[]{:S(2)}, u32[]{:S(2)}) collective-permute-start(bf16[288,128]{1,0:T(8,128)(2,1)S(1)} %collective-permute-done.2.refs_3_), channel_id=1, source_target_pairs={{0,1},{1,0},{2,3},{3,2},{4,5},{5,4},{6,7},{7,6},{8,9},{9,8},{10,11... | collective-permute-start | bytes 221192 | tf_op jit(solution)/shard_map/ppermute | solution.py:360
  11.7 4.5 %collective-permute-start.8 = (bf16[288,128]{1,0:T(8,128)(2,1)S(1)}, bf16[288,128]{1,0:T(8,128)(2,1)S(1)}, u32[]{:S(2)}, u32[]{:S(2)}) collective-permute-start(bf16[288,128]{1,0:T(8,128)(2,1)S(1)} %collective-permute-done.1.refs_2_), channel_id=1, source_target_pairs={{0,2},{1,3},{2,0},{3,1},{4,6},{5,7},{6,4},{7,5},{8,10},{9,11},{10,... | collective-permute-start | bytes 221192 | tf_op jit(solution)/shard_map/ppermute | solution.py:360
  12.9 3.7 %collective-permute-start.4 = (bf16[288,128]{1,0:T(8,128)(2,1)S(1)}, bf16[288,128]{1,0:T(8,128)(2,1)S(1)}, u32[]{:S(2)}, u32[]{:S(2)}) collective-permute-start(bf16[288,128]{1,0:T(8,128)(2,1)S(1)} %collective-permute-done.1.refs_2_), channel_id=1, source_target_pairs={{0,1},{1,0},{2,3},{3,2},{4,5},{5,4},{6,7},{7,6},{8,9},{9,8},{10,11... | collective-permute-start | bytes 221192 | tf_op jit(solution)/shard_map/ppermute | solution.py:360
  13.2 4.6 %collective-permute-start.13 = (bf16[288,128]{1,0:T(8,128)(2,1)S(1)}, bf16[288,128]{1,0:T(8,128)(2,1)S(1)}, u32[]{:S(2)}, u32[]{:S(2)}) collective-permute-start(bf16[288,128]{1,0:T(8,128)(2,1)S(1)} %collective-permute-done.6.refs_7_), channel_id=1, source_target_pairs={{0,2},{1,3},{2,0},{3,1},{4,6},{5,7},{6,4},{7,5},{8,10},{9,11},{10,... | collective-permute-start | bytes 221192 | tf_op jit(solution)/shard_map/ppermute | solution.py:360
  14.1 4.5 %collective-permute-start.7 = (bf16[288,128]{1,0:T(8,128)(2,1)S(1)}, bf16[288,128]{1,0:T(8,128)(2,1)S(1)}, u32[]{:S(2)}, u32[]{:S(2)}) collective-permute-start(bf16[288,128]{1,0:T(8,128)(2,1)S(1)} %collective-permute-done.3.refs_4_), channel_id=1, source_target_pairs={{0,1},{1,0},{2,3},{3,2},{4,5},{5,4},{6,7},{7,6},{8,9},{9,8},{10,11... | collective-permute-start | bytes 221192 | tf_op jit(solution)/shard_map/ppermute | solution.py:360
  16.1 2.6 %collective-permute-start.10 = (bf16[288,128]{1,0:T(8,128)(2,1)S(1)}, bf16[288,128]{1,0:T(8,128)(2,1)S(1)}, u32[]{:S(2)}, u32[]{:S(2)}) collective-permute-start(bf16[288,128]{1,0:T(8,128)(2,1)S(1)} %collective-permute-done.6.refs_7_), channel_id=1, source_target_pairs={{0,1},{1,0},{2,3},{3,2},{4,5},{5,4},{6,7},{7,6},{8,9},{9,8},{10,11... | collective-permute-start | bytes 221192 | tf_op jit(solution)/shard_map/ppermute | solution.py:360
  16.2 2.5 %collective-permute-start.12 = (bf16[288,128]{1,0:T(8,128)(2,1)S(1)}, bf16[288,128]{1,0:T(8,128)(2,1)S(1)}, u32[]{:S(2)}, u32[]{:S(2)}) collective-permute-start(bf16[288,128]{1,0:T(8,128)(2,1)S(1)} %collective-permute-done.9.refs_4_.refs_10_), channel_id=1, source_target_pairs={{0,1},{1,0},{2,3},{3,2},{4,5},{5,4},{6,7},{7,6},{8,9},{9,8},{10,11... | collective-permute-start | bytes 221192 | tf_op jit(solution)/shard_map/ppermute | solution.py:360
  16.6 2.1 %collective-permute-start.11 = (bf16[288,128]{1,0:T(8,128)(2,1)S(1)}, bf16[288,128]{1,0:T(8,128)(2,1)S(1)}, u32[]{:S(2)}, u32[]{:S(2)}) collective-permute-start(bf16[288,128]{1,0:T(8,128)(2,1)S(1)} %collective-permute-done.8.refs_3_.refs_9_), channel_id=1, source_target_pairs={{0,1},{1,0},{2,3},{3,2},{4,5},{5,4},{6,7},{7,6},{8,9},{9,8},{10,11... | collective-permute-start | bytes 221192 | tf_op jit(solution)/shard_map/ppermute | solution.py:360
  17.8 2.2 %collective-permute-start.14 = (bf16[288,128]{1,0:T(8,128)(2,1)S(1)}, bf16[288,128]{1,0:T(8,128)(2,1)S(1)}, u32[]{:S(2)}, u32[]{:S(2)}) collective-permute-start(bf16[288,128]{1,0:T(8,128)(2,1)S(1)} %collective-permute-done.13.refs_14_), channel_id=1, source_target_pairs={{0,1},{1,0},{2,3},{3,2},{4,5},{5,4},{6,7},{7,6},{8,9},{9,8},{10,11... | collective-permute-start | bytes 221192 | tf_op jit(solution)/shard_map/ppermute | solution.py:360

commit v9 on v8

--- a/solution.py
+++ b/solution.py
@@ -250,6 +250,7 @@
     x = jnp.concatenate([x_early_ref[...] + x_ref[...], x_late_ref[...]], axis=1)
     x = flatten(x.astype(bf16).astype(f32))
 
+    zhat, zs = normalize(block_refs[0][pl.ds(0, rows * n), :].astype(f32))
     mean = jnp.where(iota((LANES, LANES), 0) // hidden == iota((LANES, LANES), 1) // hidden, 1.0 / hidden, 0.0)
     mean = mean.astype(bf16)
     mean_twice = jnp.concatenate([mean, mean], axis=0)
@@ -300,7 +301,6 @@
     dp_rows = [jnp.where(place == r, dp[:n], jnp.zeros_like(dp[:n])) for r in range(rows)]
     dzn = dot(jnp.concatenate(dp_rows, axis=0), jnp.concatenate(tiled, axis=0))
     dzn += dot(jnp.concatenate(own_dgo, axis=0), gate_weight, NT)
-    zhat, zs = normalize(block_refs[0][pl.ds(0, rows * n), :].astype(f32))
     u = gain * dzn
     first = jnp.mean(u, axis=-1, keepdims=True)
     second = jnp.mean(u * zhat, axis=-1, keepdims=True)

time: 23.8 us -> 23.8 us (level)
  no operation moved by 1% of the time
where the time goes in v9:
time: 23.8 us; the launch traced here: 23.6 us
  starting transfers between devices  15.3 us (64%)
  Pallas kernels  6.99 us (29%)
  between operations  1.36 us (6%)
    ppermute x15, starting transfers between devices, hop(): blocks[d ^ step] = lax.ppermute(blocks[d], 'row', pairs)  15.3 us
    pallas_call x1, Pallas kernels, body_whole(): pl.pallas_call(functools.partial(tail_kernel, n, hidden, order, cuts), ou...  3.67 us
    pallas_call x1, Pallas kernels, body_whole(): pl.pallas_call(functools.partial(middle_kernel, n, hidden, order, cuts[0]...  1.3 us
    pallas_call x1, Pallas kernels, body_whole(): pl.pallas_call(functools.partial(head_kernel, n, hidden, order), out_shap...  1.09 us
    pallas_call x1, Pallas kernels, body_whole(): pl.pallas_call(load_kernel, out_shape=[pltpu.VMEM((2 * half, channels), b...  0.93 us
  transfers between devices with their start and end apart: 15, of which 0 were waited for; matrix products, arithmetic and copies ran while one was open for 0% of the time, Pallas kernels for 10%

profile of v9, /device:TPU:1, one launch (start us, length us, event | category | flops | bytes accessed | tf_op | source)
XLA Modules:
  0.0 23.6 jit_solution(15096579255101868897)
XLA Ops:
  0.6 0.9 %load.1 = (bf16[288,128]{1,0:T(8,128)(2,1)S(1)}, f32[1,128]{1,0:T(1,128)S(1)}, f32[1,128]{1,0:T(1,128)S(1)}, bf16[64,128]{1,0:T(8,128)(2,1)S(1)}, bf16[128,128]{...) custom-call(bf16[144,128]{1,0:T(8,128)(2,1)} %bitcast.8, ...), custom_call_target="tpu_custom_call" | custom-call | tf_op jit(solution)/shard_map/load/pallas_call | solution.py:346
  1.6 3.2 %collective-permute-start.1 = (bf16[288,128]{1,0:T(8,128)(2,1)S(1)}, bf16[288,128]{1,0:T(8,128)(2,1)S(1)}, u32[]{:S(2)}, u32[]{:S(2)}) collective-permute-start(bf16[288,128]{1,0:T(8,128)(2,1)S(1)} %get-tuple-element.52.refs_0_), channel_id=1, source_target_pairs={{0,8},{1,9},{2,10},{3,11},{4,12},{5,13},{6,14},{7,15},{8,0},{9,1},... | collective-permute-start | bytes 221192 | tf_op jit(solution)/shard_map/ppermute | solution.py:360
  4.8 1.2 %collective-permute-start.3 = (bf16[288,128]{1,0:T(8,128)(2,1)S(1)}, bf16[288,128]{1,0:T(8,128)(2,1)S(1)}, u32[]{:S(2)}, u32[]{:S(2)}) collective-permute-start(bf16[288,128]{1,0:T(8,128)(2,1)S(1)} %get-tuple-element.52.refs_0_), channel_id=1, source_target_pairs={{0,2},{1,3},{2,0},{3,1},{4,6},{5,7},{6,4},{7,5},{8,10},{9,11},{10,... | collective-permute-start | bytes 221192 | tf_op jit(solution)/shard_map/ppermute | solution.py:360
  6.0 1.3 %collective-permute-start.2 = (bf16[288,128]{1,0:T(8,128)(2,1)S(1)}, bf16[288,128]{1,0:T(8,128)(2,1)S(1)}, u32[]{:S(2)}, u32[]{:S(2)}) collective-permute-start(bf16[288,128]{1,0:T(8,128)(2,1)S(1)} %get-tuple-element.52.refs_0_), channel_id=1, source_target_pairs={{0,4},{1,5},{2,6},{3,7},{4,0},{5,1},{6,2},{7,3},{8,12},{9,13},{10,... | collective-permute-start | bytes 221192 | tf_op jit(solution)/shard_map/ppermute | solution.py:360
  7.3 1.5 %collective-permute-start = (bf16[288,128]{1,0:T(8,128)(2,1)S(1)}, bf16[288,128]{1,0:T(8,128)(2,1)S(1)}, u32[]{:S(2)}, u32[]{:S(2)}) collective-permute-start(bf16[288,128]{1,0:T(8,128)(2,1)S(1)} %get-tuple-element.52.refs_0_), channel_id=1, source_target_pairs={{0,1},{1,0},{2,3},{3,2},{4,5},{5,4},{6,7},{7,6},{8,9},{9,8},{10,11... | collective-permute-start | bytes 221192 | tf_op jit(solution)/shard_map/ppermute | solution.py:360
  8.8 0.0 collective-permute-done.1.refs_2_
  8.8 0.5 %collective-permute-start.6 = (bf16[288,128]{1,0:T(8,128)(2,1)S(1)}, bf16[288,128]{1,0:T(8,128)(2,1)S(1)}, u32[]{:S(2)}, u32[]{:S(2)}) collective-permute-start(bf16[288,128]{1,0:T(8,128)(2,1)S(1)} %collective-permute-done.1.refs_2_), channel_id=1, source_target_pairs={{0,4},{1,5},{2,6},{3,7},{4,0},{5,1},{6,2},{7,3},{8,12},{9,13},{10,... | collective-permute-start | bytes 221192 | tf_op jit(solution)/shard_map/ppermute | solution.py:360
  9.3 1.0 %collective-permute-start.9 = (bf16[288,128]{1,0:T(8,128)(2,1)S(1)}, bf16[288,128]{1,0:T(8,128)(2,1)S(1)}, u32[]{:S(2)}, u32[]{:S(2)}) collective-permute-start(bf16[288,128]{1,0:T(8,128)(2,1)S(1)} %collective-permute-done.3.refs_4_), channel_id=1, source_target_pairs={{0,4},{1,5},{2,6},{3,7},{4,0},{5,1},{6,2},{7,3},{8,12},{9,13},{10,... | collective-permute-start | bytes 221192 | tf_op jit(solution)/shard_map/ppermute | solution.py:360
  10.3 1.4 %collective-permute-start.5 = (bf16[288,128]{1,0:T(8,128)(2,1)S(1)}, bf16[288,128]{1,0:T(8,128)(2,1)S(1)}, u32[]{:S(2)}, u32[]{:S(2)}) collective-permute-start(bf16[288,128]{1,0:T(8,128)(2,1)S(1)} %collective-permute-done.2.refs_3_), channel_id=1, source_target_pairs={{0,1},{1,0},{2,3},{3,2},{4,5},{5,4},{6,7},{7,6},{8,9},{9,8},{10,11... | collective-permute-start | bytes 221192 | tf_op jit(solution)/shard_map/ppermute | solution.py:360
  11.7 1.2 %collective-permute-start.8 = (bf16[288,128]{1,0:T(8,128)(2,1)S(1)}, bf16[288,128]{1,0:T(8,128)(2,1)S(1)}, u32[]{:S(2)}, u32[]{:S(2)}) collective-permute-start(bf16[288,128]{1,0:T(8,128)(2,1)S(1)} %collective-permute-done.1.refs_2_), channel_id=1, source_target_pairs={{0,2},{1,3},{2,0},{3,1},{4,6},{5,7},{6,4},{7,5},{8,10},{9,11},{10,... | collective-permute-start | bytes 221192 | tf_op jit(solution)/shard_map/ppermute | solution.py:360
  12.9 0.3 %collective-permute-start.4 = (bf16[288,128]{1,0:T(8,128)(2,1)S(1)}, bf16[288,128]{1,0:T(8,128)(2,1)S(1)}, u32[]{:S(2)}, u32[]{:S(2)}) collective-permute-start(bf16[288,128]{1,0:T(8,128)(2,1)S(1)} %collective-permute-done.1.refs_2_), channel_id=1, source_target_pairs={{0,1},{1,0},{2,3},{3,2},{4,5},{5,4},{6,7},{7,6},{8,9},{9,8},{10,11... | collective-permute-start | bytes 221192 | tf_op jit(solution)/shard_map/ppermute | solution.py:360
  13.2 0.0 collective-permute-done.6.refs_7_
  13.2 0.3 %collective-permute-start.13 = (bf16[288,128]{1,0:T(8,128)(2,1)S(1)}, bf16[288,128]{1,0:T(8,128)(2,1)S(1)}, u32[]{:S(2)}, u32[]{:S(2)}) collective-permute-start(bf16[288,128]{1,0:T(8,128)(2,1)S(1)} %collective-permute-done.6.refs_7_), channel_id=1, source_target_pairs={{0,2},{1,3},{2,0},{3,1},{4,6},{5,7},{6,4},{7,5},{8,10},{9,11},{10,... | collective-permute-start | bytes 221192 | tf_op jit(solution)/shard_map/ppermute | solution.py:360
  14.1 0.0 collective-permute-done.9.refs_4_.refs_10_
  14.1 2.0 %collective-permute-start.7 = (bf16[288,128]{1,0:T(8,128)(2,1)S(1)}, bf16[288,128]{1,0:T(8,128)(2,1)S(1)}, u32[]{:S(2)}, u32[]{:S(2)}) collective-permute-start(bf16[288,128]{1,0:T(8,128)(2,1)S(1)} %collective-permute-done.3.refs_4_), channel_id=1, source_target_pairs={{0,1},{1,0},{2,3},{3,2},{4,5},{5,4},{6,7},{7,6},{8,9},{9,8},{10,11... | collective-permute-start | bytes 221192 | tf_op jit(solution)/shard_map/ppermute | solution.py:360
  16.1 0.0 collective-permute-done.5.refs_6_
  16.1 0.1 collective-permute-start.10
  16.2 0.4 %collective-permute-start.12 = (bf16[288,128]{1,0:T(8,128)(2,1)S(1)}, bf16[288,128]{1,0:T(8,128)(2,1)S(1)}, u32[]{:S(2)}, u32[]{:S(2)}) collective-permute-start(bf16[288,128]{1,0:T(8,128)(2,1)S(1)} %collective-permute-done.9.refs_4_.refs_10_), channel_id=1, source_target_pairs={{0,1},{1,0},{2,3},{3,2},{4,5},{5,4},{6,7},{7,6},{8,9},{9,8},{10,11... | collective-permute-start | bytes 221192 | tf_op jit(solution)/shard_map/ppermute | solution.py:360
  16.6 0.0 collective-permute-done.4.refs_5_
  16.6 0.1 collective-permute-start.11
  16.7 1.1 %head.1 = (bf16[144,128]{1,0:T(8,128)(2,1)S(1)}, bf16[144,128]{1,0:T(8,128)(2,1)S(1)}, f32[2,144,128]{2,1,0:T(8,128)S(1)}, f32[2,144,128]{2,1,0:T(8,128)S(1)}, b...) custom-call(bf16[288,128]{1,0:T(8,128)(2,1)S(1)} %get-tuple-element., ...), custom_call_target="tpu_custom_call" | custom-call | tf_op jit(solution)/shard_map/head/pallas_call | solution.py:403
  17.8 0.9 %collective-permute-start.14 = (bf16[288,128]{1,0:T(8,128)(2,1)S(1)}, bf16[288,128]{1,0:T(8,128)(2,1)S(1)}, u32[]{:S(2)}, u32[]{:S(2)}) collective-permute-start(bf16[288,128]{1,0:T(8,128)(2,1)S(1)} %collective-permute-done.13.refs_14_), channel_id=1, source_target_pairs={{0,1},{1,0},{2,3},{3,2},{4,5},{5,4},{6,7},{7,6},{8,9},{9,8},{10,11... | collective-permute-start | bytes 221192 | tf_op jit(solution)/shard_map/ppermute | solution.py:360
  18.7 1.3 %middle.1 = (bf16[96,128]{1,0:T(8,128)(2,1)S(1)}, bf16[96,128]{1,0:T(8,128)(2,1)S(1)}, f32[2,96,128]{2,1,0:T(8,128)S(1)}, f32[2,96,128]{2,1,0:T(8,128)S(1)}, bf1...) custom-call(bf16[144,128]{1,0:T(8,128)(2,1)S(1)} %get-tuple-element., ...), custom_call_target="tpu_custom_call" | custom-call | tf_op jit(solution)/shard_map/middle/pallas_call | solution.py:416
  20.0 3.7 %tail.1 = (bf16[3,48,128]{2,1,0:T(8,128)(2,1)}, f32[3,48,128]{2,1,0:T(8,128)}, f32[64,128]{1,0:T(8,128)}, f32[128,128]{1,0:T(8,128)}, f32[16,128]{1,0:T(8,128)}) custom-call(bf16[288,128]{1,0:T(8,128)(2,1)S(1)} %get-tuple-element.52.refs_0_, bf16[288,128]{1,0:T(8,128)(2,1)S(1)} %collective-permute-done.refs_1_, ...), custom_call_target="tpu_custom_call" | custom-call | tf_op jit(solution)/shard_map/tail/pallas_call | solution.py:425
  (10 shorter events, 0.0 us)
Async XLA Ops:
  1.6 7.2 %collective-permute-start.1 = (bf16[288,128]{1,0:T(8,128)(2,1)S(1)}, bf16[288,128]{1,0:T(8,128)(2,1)S(1)}, u32[]{:S(2)}, u32[]{:S(2)}) collective-permute-start(bf16[288,128]{1,0:T(8,128)(2,1)S(1)} %get-tuple-element.52.refs_0_), channel_id=1, source_target_pairs={{0,8},{1,9},{2,10},{3,11},{4,12},{5,13},{6,14},{7,15},{8,0},{9,1},... | collective-permute-start | bytes 221192 | tf_op jit(solution)/shard_map/ppermute | solution.py:360
  4.8 4.5 %collective-permute-start.3 = (bf16[288,128]{1,0:T(8,128)(2,1)S(1)}, bf16[288,128]{1,0:T(8,128)(2,1)S(1)}, u32[]{:S(2)}, u32[]{:S(2)}) collective-permute-start(bf16[288,128]{1,0:T(8,128)(2,1)S(1)} %get-tuple-element.52.refs_0_), channel_id=1, source_target_pairs={{0,2},{1,3},{2,0},{3,1},{4,6},{5,7},{6,4},{7,5},{8,10},{9,11},{10,... | collective-permute-start | bytes 221192 | tf_op jit(solution)/shard_map/ppermute | solution.py:360
  6.0 4.3 %collective-permute-start.2 = (bf16[288,128]{1,0:T(8,128)(2,1)S(1)}, bf16[288,128]{1,0:T(8,128)(2,1)S(1)}, u32[]{:S(2)}, u32[]{:S(2)}) collective-permute-start(bf16[288,128]{1,0:T(8,128)(2,1)S(1)} %get-tuple-element.52.refs_0_), channel_id=1, source_target_pairs={{0,4},{1,5},{2,6},{3,7},{4,0},{5,1},{6,2},{7,3},{8,12},{9,13},{10,... | collective-permute-start | bytes 221192 | tf_op jit(solution)/shard_map/ppermute | solution.py:360
  7.3 5.6 %collective-permute-start = (bf16[288,128]{1,0:T(8,128)(2,1)S(1)}, bf16[288,128]{1,0:T(8,128)(2,1)S(1)}, u32[]{:S(2)}, u32[]{:S(2)}) collective-permute-start(bf16[288,128]{1,0:T(8,128)(2,1)S(1)} %get-tuple-element.52.refs_0_), channel_id=1, source_target_pairs={{0,1},{1,0},{2,3},{3,2},{4,5},{5,4},{6,7},{7,6},{8,9},{9,8},{10,11... | collective-permute-start | bytes 221192 | tf_op jit(solution)/shard_map/ppermute | solution.py:360
  8.8 4.4 %collective-permute-start.6 = (bf16[288,128]{1,0:T(8,128)(2,1)S(1)}, bf16[288,128]{1,0:T(8,128)(2,1)S(1)}, u32[]{:S(2)}, u32[]{:S(2)}) collective-permute-start(bf16[288,128]{1,0:T(8,128)(2,1)S(1)} %collective-permute-done.1.refs_2_), channel_id=1, source_target_pairs={{0,4},{1,5},{2,6},{3,7},{4,0},{5,1},{6,2},{7,3},{8,12},{9,13},{10,... | collective-permute-start | bytes 221192 | tf_op jit(solution)/shard_map/ppermute | solution.py:360
  9.3 4.8 %collective-permute-start.9 = (bf16[288,128]{1,0:T(8,128)(2,1)S(1)}, bf16[288,128]{1,0:T(8,128)(2,1)S(1)}, u32[]{:S(2)}, u32[]{:S(2)}) collective-permute-start(bf16[288,128]{1,0:T(8,128)(2,1)S(1)} %collective-permute-done.3.refs_4_), channel_id=1, source_target_pairs={{0,4},{1,5},{2,6},{3,7},{4,0},{5,1},{6,2},{7,3},{8,12},{9,13},{10,... | collective-permute-start | bytes 221192 | tf_op jit(solution)/shard_map/ppermute | solution.py:360
  10.3 5.8 %collective-permute-start.5 = (bf16[288,128]{1,0:T(8,128)(2,1)S(1)}, bf16[288,128]{1,0:T(8,128)(2,1)S(1)}, u32[]{:S(2)}, u32[]{:S(2)}) collective-permute-start(bf16[288,128]{1,0:T(8,128)(2,1)S(1)} %collective-permute-done.2.refs_3_), channel_id=1, source_target_pairs={{0,1},{1,0},{2,3},{3,2},{4,5},{5,4},{6,7},{7,6},{8,9},{9,8},{10,11... | collective-permute-start | bytes 221192 | tf_op jit(solution)/shard_map/ppermute | solution.py:360
  11.7 4.5 %collective-permute-start.8 = (bf16[288,128]{1,0:T(8,128)(2,1)S(1)}, bf16[288,128]{1,0:T(8,128)(2,1)S(1)}, u32[]{:S(2)}, u32[]{:S(2)}) collective-permute-start(bf16[288,128]{1,0:T(8,128)(2,1)S(1)} %collective-permute-done.1.refs_2_), channel_id=1, source_target_pairs={{0,2},{1,3},{2,0},{3,1},{4,6},{5,7},{6,4},{7,5},{8,10},{9,11},{10,... | collective-permute-start | bytes 221192 | tf_op jit(solution)/shard_map/ppermute | solution.py:360
  12.9 3.7 %collective-permute-start.4 = (bf16[288,128]{1,0:T(8,128)(2,1)S(1)}, bf16[288,128]{1,0:T(8,128)(2,1)S(1)}, u32[]{:S(2)}, u32[]{:S(2)}) collective-permute-start(bf16[288,128]{1,0:T(8,128)(2,1)S(1)} %collective-permute-done.1.refs_2_), channel_id=1, source_target_pairs={{0,1},{1,0},{2,3},{3,2},{4,5},{5,4},{6,7},{7,6},{8,9},{9,8},{10,11... | collective-permute-start | bytes 221192 | tf_op jit(solution)/shard_map/ppermute | solution.py:360
  13.2 4.6 %collective-permute-start.13 = (bf16[288,128]{1,0:T(8,128)(2,1)S(1)}, bf16[288,128]{1,0:T(8,128)(2,1)S(1)}, u32[]{:S(2)}, u32[]{:S(2)}) collective-permute-start(bf16[288,128]{1,0:T(8,128)(2,1)S(1)} %collective-permute-done.6.refs_7_), channel_id=1, source_target_pairs={{0,2},{1,3},{2,0},{3,1},{4,6},{5,7},{6,4},{7,5},{8,10},{9,11},{10,... | collective-permute-start | bytes 221192 | tf_op jit(solution)/shard_map/ppermute | solution.py:360
  14.1 4.5 %collective-permute-start.7 = (bf16[288,128]{1,0:T(8,128)(2,1)S(1)}, bf16[288,128]{1,0:T(8,128)(2,1)S(1)}, u32[]{:S(2)}, u32[]{:S(2)}) collective-permute-start(bf16[288,128]{1,0:T(8,128)(2,1)S(1)} %collective-permute-done.3.refs_4_), channel_id=1, source_target_pairs={{0,1},{1,0},{2,3},{3,2},{4,5},{5,4},{6,7},{7,6},{8,9},{9,8},{10,11... | collective-permute-start | bytes 221192 | tf_op jit(solution)/shard_map/ppermute | solution.py:360
  16.1 2.6 %collective-permute-start.10 = (bf16[288,128]{1,0:T(8,128)(2,1)S(1)}, bf16[288,128]{1,0:T(8,128)(2,1)S(1)}, u32[]{:S(2)}, u32[]{:S(2)}) collective-permute-start(bf16[288,128]{1,0:T(8,128)(2,1)S(1)} %collective-permute-done.6.refs_7_), channel_id=1, source_target_pairs={{0,1},{1,0},{2,3},{3,2},{4,5},{5,4},{6,7},{7,6},{8,9},{9,8},{10,11... | collective-permute-start | bytes 221192 | tf_op jit(solution)/shard_map/ppermute | solution.py:360
  16.2 2.5 %collective-permute-start.12 = (bf16[288,128]{1,0:T(8,128)(2,1)S(1)}, bf16[288,128]{1,0:T(8,128)(2,1)S(1)}, u32[]{:S(2)}, u32[]{:S(2)}) collective-permute-start(bf16[288,128]{1,0:T(8,128)(2,1)S(1)} %collective-permute-done.9.refs_4_.refs_10_), channel_id=1, source_target_pairs={{0,1},{1,0},{2,3},{3,2},{4,5},{5,4},{6,7},{7,6},{8,9},{9,8},{10,11... | collective-permute-start | bytes 221192 | tf_op jit(solution)/shard_map/ppermute | solution.py:360
  16.6 2.1 %collective-permute-start.11 = (bf16[288,128]{1,0:T(8,128)(2,1)S(1)}, bf16[288,128]{1,0:T(8,128)(2,1)S(1)}, u32[]{:S(2)}, u32[]{:S(2)}) collective-permute-start(bf16[288,128]{1,0:T(8,128)(2,1)S(1)} %collective-permute-done.8.refs_3_.refs_9_), channel_id=1, source_target_pairs={{0,1},{1,0},{2,3},{3,2},{4,5},{5,4},{6,7},{7,6},{8,9},{9,8},{10,11... | collective-permute-start | bytes 221192 | tf_op jit(solution)/shard_map/ppermute | solution.py:360
  17.8 2.2 %collective-permute-start.14 = (bf16[288,128]{1,0:T(8,128)(2,1)S(1)}, bf16[288,128]{1,0:T(8,128)(2,1)S(1)}, u32[]{:S(2)}, u32[]{:S(2)}) collective-permute-start(bf16[288,128]{1,0:T(8,128)(2,1)S(1)} %collective-permute-done.13.refs_14_), channel_id=1, source_target_pairs={{0,1},{1,0},{2,3},{3,2},{4,5},{5,4},{6,7},{7,6},{8,9},{9,8},{10,11... | collective-permute-start | bytes 221192 | tf_op jit(solution)/shard_map/ppermute | solution.py:360

commit v10 on v8

--- a/solution.py
+++ b/solution.py
@@ -364,7 +364,6 @@
         if step == z[-1]:
             hop(x, [0])
     for k, step in enumerate(z[:-1]):
-        hop(step, [x])
         hop(step, [d for d in list(blocks) if 0 < d and d % (2 * step) == 0])
     hop(x, [d for d in list(blocks) if not d & x and d ^ x not in blocks])
     last = devices - 1 - core

time: 23.8 us -> 23.9 us (level)
  no operation moved by 1% of the time
where the time goes in v10:
time: 23.9 us; the launch traced here: 23.7 us
  starting transfers between devices  15.3 us (64%)
  Pallas kernels  6.99 us (29%)
  between operations  1.36 us (6%)
    ppermute x15, starting transfers between devices, hop(): blocks[d ^ step] = lax.ppermute(blocks[d], 'row', pairs)  15.3 us
    pallas_call x1, Pallas kernels, body_whole(): pl.pallas_call(functools.partial(tail_kernel, n, hidden, order, cuts), ou...  3.67 us
    pallas_call x1, Pallas kernels, body_whole(): pl.pallas_call(functools.partial(middle_kernel, n, hidden, order, cuts[0]...  1.3 us
    pallas_call x1, Pallas kernels, body_whole(): pl.pallas_call(functools.partial(head_kernel, n, hidden, order), out_shap...  1.09 us
    pallas_call x1, Pallas kernels, body_whole(): pl.pallas_call(load_kernel, out_shape=[pltpu.VMEM((2 * half, channels), b...  0.93 us
  transfers between devices with their start and end apart: 15, of which 0 were waited for; matrix products, arithmetic and copies ran while one was open for 0% of the time, Pallas kernels for 10%

profile of v10, /device:TPU:1, one launch (start us, length us, event | category | flops | bytes accessed | tf_op | source)
XLA Modules:
  0.0 23.7 jit_solution(3407681550456784530)
XLA Ops:
  0.6 0.9 %load.1 = (bf16[288,128]{1,0:T(8,128)(2,1)S(1)}, f32[1,128]{1,0:T(1,128)S(1)}, f32[1,128]{1,0:T(1,128)S(1)}, bf16[64,128]{1,0:T(8,128)(2,1)S(1)}, bf16[128,128]{...) custom-call(bf16[144,128]{1,0:T(8,128)(2,1)} %bitcast.8, ...), custom_call_target="tpu_custom_call" | custom-call | tf_op jit(solution)/shard_map/load/pallas_call | solution.py:346
  1.6 3.2 %collective-permute-start.1 = (bf16[288,128]{1,0:T(8,128)(2,1)S(1)}, bf16[288,128]{1,0:T(8,128)(2,1)S(1)}, u32[]{:S(2)}, u32[]{:S(2)}) collective-permute-start(bf16[288,128]{1,0:T(8,128)(2,1)S(1)} %get-tuple-element.52.refs_0_), channel_id=1, source_target_pairs={{0,8},{1,9},{2,10},{3,11},{4,12},{5,13},{6,14},{7,15},{8,0},{9,1},... | collective-permute-start | bytes 221192 | tf_op jit(solution)/shard_map/ppermute | solution.py:360
  4.8 1.3 %collective-permute-start.2 = (bf16[288,128]{1,0:T(8,128)(2,1)S(1)}, bf16[288,128]{1,0:T(8,128)(2,1)S(1)}, u32[]{:S(2)}, u32[]{:S(2)}) collective-permute-start(bf16[288,128]{1,0:T(8,128)(2,1)S(1)} %get-tuple-element.52.refs_0_), channel_id=1, source_target_pairs={{0,4},{1,5},{2,6},{3,7},{4,0},{5,1},{6,2},{7,3},{8,12},{9,13},{10,... | collective-permute-start | bytes 221192 | tf_op jit(solution)/shard_map/ppermute | solution.py:360
  6.1 1.2 %collective-permute-start.3 = (bf16[288,128]{1,0:T(8,128)(2,1)S(1)}, bf16[288,128]{1,0:T(8,128)(2,1)S(1)}, u32[]{:S(2)}, u32[]{:S(2)}) collective-permute-start(bf16[288,128]{1,0:T(8,128)(2,1)S(1)} %get-tuple-element.52.refs_0_), channel_id=1, source_target_pairs={{0,2},{1,3},{2,0},{3,1},{4,6},{5,7},{6,4},{7,5},{8,10},{9,11},{10,... | collective-permute-start | bytes 221192 | tf_op jit(solution)/shard_map/ppermute | solution.py:360
  7.3 1.5 %collective-permute-start = (bf16[288,128]{1,0:T(8,128)(2,1)S(1)}, bf16[288,128]{1,0:T(8,128)(2,1)S(1)}, u32[]{:S(2)}, u32[]{:S(2)}) collective-permute-start(bf16[288,128]{1,0:T(8,128)(2,1)S(1)} %get-tuple-element.52.refs_0_), channel_id=1, source_target_pairs={{0,1},{1,0},{2,3},{3,2},{4,5},{5,4},{6,7},{7,6},{8,9},{9,8},{10,11... | collective-permute-start | bytes 221192 | tf_op jit(solution)/shard_map/ppermute | solution.py:360
  8.8 0.0 collective-permute-done.1.refs_2_
  8.8 0.2 %collective-permute-start.6 = (bf16[288,128]{1,0:T(8,128)(2,1)S(1)}, bf16[288,128]{1,0:T(8,128)(2,1)S(1)}, u32[]{:S(2)}, u32[]{:S(2)}) collective-permute-start(bf16[288,128]{1,0:T(8,128)(2,1)S(1)} %collective-permute-done.1.refs_2_), channel_id=1, source_target_pairs={{0,4},{1,5},{2,6},{3,7},{4,0},{5,1},{6,2},{7,3},{8,12},{9,13},{10,... | collective-permute-start | bytes 221192 | tf_op jit(solution)/shard_map/ppermute | solution.py:360
  9.1 1.2 %collective-permute-start.9 = (bf16[288,128]{1,0:T(8,128)(2,1)S(1)}, bf16[288,128]{1,0:T(8,128)(2,1)S(1)}, u32[]{:S(2)}, u32[]{:S(2)}) collective-permute-start(bf16[288,128]{1,0:T(8,128)(2,1)S(1)} %collective-permute-done.2.refs_3_), channel_id=1, source_target_pairs={{0,2},{1,3},{2,0},{3,1},{4,6},{5,7},{6,4},{7,5},{8,10},{9,11},{10,... | collective-permute-start | bytes 221192 | tf_op jit(solution)/shard_map/ppermute | solution.py:360
  10.3 1.6 %collective-permute-start.5 = (bf16[288,128]{1,0:T(8,128)(2,1)S(1)}, bf16[288,128]{1,0:T(8,128)(2,1)S(1)}, u32[]{:S(2)}, u32[]{:S(2)}) collective-permute-start(bf16[288,128]{1,0:T(8,128)(2,1)S(1)} %collective-permute-done.2.refs_3_), channel_id=1, source_target_pairs={{0,1},{1,0},{2,3},{3,2},{4,5},{5,4},{6,7},{7,6},{8,9},{9,8},{10,11... | collective-permute-start | bytes 221192 | tf_op jit(solution)/shard_map/ppermute | solution.py:360
  11.9 0.0 collective-permute-done.3.refs_4_
  11.9 0.3 %collective-permute-start.8 = (bf16[288,128]{1,0:T(8,128)(2,1)S(1)}, bf16[288,128]{1,0:T(8,128)(2,1)S(1)}, u32[]{:S(2)}, u32[]{:S(2)}) collective-permute-start(bf16[288,128]{1,0:T(8,128)(2,1)S(1)} %collective-permute-done.1.refs_2_), channel_id=1, source_target_pairs={{0,2},{1,3},{2,0},{3,1},{4,6},{5,7},{6,4},{7,5},{8,10},{9,11},{10,... | collective-permute-start | bytes 221192 | tf_op jit(solution)/shard_map/ppermute | solution.py:360
  12.2 1.0 %collective-permute-start.4 = (bf16[288,128]{1,0:T(8,128)(2,1)S(1)}, bf16[288,128]{1,0:T(8,128)(2,1)S(1)}, u32[]{:S(2)}, u32[]{:S(2)}) collective-permute-start(bf16[288,128]{1,0:T(8,128)(2,1)S(1)} %collective-permute-done.1.refs_2_), channel_id=1, source_target_pairs={{0,1},{1,0},{2,3},{3,2},{4,5},{5,4},{6,7},{7,6},{8,9},{9,8},{10,11... | collective-permute-start | bytes 221192 | tf_op jit(solution)/shard_map/ppermute | solution.py:360
  13.2 0.5 %collective-permute-start.13 = (bf16[288,128]{1,0:T(8,128)(2,1)S(1)}, bf16[288,128]{1,0:T(8,128)(2,1)S(1)}, u32[]{:S(2)}, u32[]{:S(2)}) collective-permute-start(bf16[288,128]{1,0:T(8,128)(2,1)S(1)} %collective-permute-done.6.refs_7_), channel_id=1, source_target_pairs={{0,2},{1,3},{2,0},{3,1},{4,6},{5,7},{6,4},{7,5},{8,10},{9,11},{10,... | collective-permute-start | bytes 221192 | tf_op jit(solution)/shard_map/ppermute | solution.py:360
  14.3 0.0 collective-permute-done.9.refs_4_.refs_10_
  14.3 1.7 %collective-permute-start.7 = (bf16[288,128]{1,0:T(8,128)(2,1)S(1)}, bf16[288,128]{1,0:T(8,128)(2,1)S(1)}, u32[]{:S(2)}, u32[]{:S(2)}) collective-permute-start(bf16[288,128]{1,0:T(8,128)(2,1)S(1)} %collective-permute-done.3.refs_4_), channel_id=1, source_target_pairs={{0,1},{1,0},{2,3},{3,2},{4,5},{5,4},{6,7},{7,6},{8,9},{9,8},{10,11... | collective-permute-start | bytes 221192 | tf_op jit(solution)/shard_map/ppermute | solution.py:360
  16.1 0.1 collective-permute-start.10
  16.2 0.8 %collective-permute-start.12 = (bf16[288,128]{1,0:T(8,128)(2,1)S(1)}, bf16[288,128]{1,0:T(8,128)(2,1)S(1)}, u32[]{:S(2)}, u32[]{:S(2)}) collective-permute-start(bf16[288,128]{1,0:T(8,128)(2,1)S(1)} %collective-permute-done.9.refs_4_.refs_10_), channel_id=1, source_target_pairs={{0,1},{1,0},{2,3},{3,2},{4,5},{5,4},{6,7},{7,6},{8,9},{9,8},{10,11... | collective-permute-start | bytes 221192 | tf_op jit(solution)/shard_map/ppermute | solution.py:360
  17.0 0.0 collective-permute-done.4.refs_5_
  17.0 0.0 collective-permute-start.11
  17.0 1.1 %head.1 = (bf16[144,128]{1,0:T(8,128)(2,1)S(1)}, bf16[144,128]{1,0:T(8,128)(2,1)S(1)}, f32[2,144,128]{2,1,0:T(8,128)S(1)}, f32[2,144,128]{2,1,0:T(8,128)S(1)}, b...) custom-call(bf16[288,128]{1,0:T(8,128)(2,1)S(1)} %get-tuple-element., ...), custom_call_target="tpu_custom_call" | custom-call | tf_op jit(solution)/shard_map/head/pallas_call | solution.py:402
  18.1 0.6 %collective-permute-start.14 = (bf16[288,128]{1,0:T(8,128)(2,1)S(1)}, bf16[288,128]{1,0:T(8,128)(2,1)S(1)}, u32[]{:S(2)}, u32[]{:S(2)}) collective-permute-start(bf16[288,128]{1,0:T(8,128)(2,1)S(1)} %collective-permute-done.13.refs_14_), channel_id=1, source_target_pairs={{0,1},{1,0},{2,3},{3,2},{4,5},{5,4},{6,7},{7,6},{8,9},{9,8},{10,11... | collective-permute-start | bytes 221192 | tf_op jit(solution)/shard_map/ppermute | solution.py:360
  18.7 0.0 collective-permute-done.7.refs_2_.refs_8_
  18.7 1.3 %middle.1 = (bf16[96,128]{1,0:T(8,128)(2,1)S(1)}, bf16[96,128]{1,0:T(8,128)(2,1)S(1)}, f32[2,96,128]{2,1,0:T(8,128)S(1)}, f32[2,96,128]{2,1,0:T(8,128)S(1)}, bf1...) custom-call(bf16[144,128]{1,0:T(8,128)(2,1)S(1)} %get-tuple-element., ...), custom_call_target="tpu_custom_call" | custom-call | tf_op jit(solution)/shard_map/middle/pallas_call | solution.py:415
  20.0 3.7 %tail.1 = (bf16[3,48,128]{2,1,0:T(8,128)(2,1)}, f32[3,48,128]{2,1,0:T(8,128)}, f32[64,128]{1,0:T(8,128)}, f32[128,128]{1,0:T(8,128)}, f32[16,128]{1,0:T(8,128)}) custom-call(bf16[288,128]{1,0:T(8,128)(2,1)S(1)} %get-tuple-element.52.refs_0_, bf16[288,128]{1,0:T(8,128)(2,1)S(1)} %collective-permute-done.refs_1_, ...), custom_call_target="tpu_custom_call" | custom-call | tf_op jit(solution)/shard_map/tail/pallas_call | solution.py:424
  (10 shorter events, 0.0 us)
Async XLA Ops:
  1.6 7.2 %collective-permute-start.1 = (bf16[288,128]{1,0:T(8,128)(2,1)S(1)}, bf16[288,128]{1,0:T(8,128)(2,1)S(1)}, u32[]{:S(2)}, u32[]{:S(2)}) collective-permute-start(bf16[288,128]{1,0:T(8,128)(2,1)S(1)} %get-tuple-element.52.refs_0_), channel_id=1, source_target_pairs={{0,8},{1,9},{2,10},{3,11},{4,12},{5,13},{6,14},{7,15},{8,0},{9,1},... | collective-permute-start | bytes 221192 | tf_op jit(solution)/shard_map/ppermute | solution.py:360
  4.8 4.3 %collective-permute-start.2 = (bf16[288,128]{1,0:T(8,128)(2,1)S(1)}, bf16[288,128]{1,0:T(8,128)(2,1)S(1)}, u32[]{:S(2)}, u32[]{:S(2)}) collective-permute-start(bf16[288,128]{1,0:T(8,128)(2,1)S(1)} %get-tuple-element.52.refs_0_), channel_id=1, source_target_pairs={{0,4},{1,5},{2,6},{3,7},{4,0},{5,1},{6,2},{7,3},{8,12},{9,13},{10,... | collective-permute-start | bytes 221192 | tf_op jit(solution)/shard_map/ppermute | solution.py:360
  6.1 5.8 %collective-permute-start.3 = (bf16[288,128]{1,0:T(8,128)(2,1)S(1)}, bf16[288,128]{1,0:T(8,128)(2,1)S(1)}, u32[]{:S(2)}, u32[]{:S(2)}) collective-permute-start(bf16[288,128]{1,0:T(8,128)(2,1)S(1)} %get-tuple-element.52.refs_0_), channel_id=1, source_target_pairs={{0,2},{1,3},{2,0},{3,1},{4,6},{5,7},{6,4},{7,5},{8,10},{9,11},{10,... | collective-permute-start | bytes 221192 | tf_op jit(solution)/shard_map/ppermute | solution.py:360
  7.3 4.9 %collective-permute-start = (bf16[288,128]{1,0:T(8,128)(2,1)S(1)}, bf16[288,128]{1,0:T(8,128)(2,1)S(1)}, u32[]{:S(2)}, u32[]{:S(2)}) collective-permute-start(bf16[288,128]{1,0:T(8,128)(2,1)S(1)} %get-tuple-element.52.refs_0_), channel_id=1, source_target_pairs={{0,1},{1,0},{2,3},{3,2},{4,5},{5,4},{6,7},{7,6},{8,9},{9,8},{10,11... | collective-permute-start | bytes 221192 | tf_op jit(solution)/shard_map/ppermute | solution.py:360
  8.8 4.4 %collective-permute-start.6 = (bf16[288,128]{1,0:T(8,128)(2,1)S(1)}, bf16[288,128]{1,0:T(8,128)(2,1)S(1)}, u32[]{:S(2)}, u32[]{:S(2)}) collective-permute-start(bf16[288,128]{1,0:T(8,128)(2,1)S(1)} %collective-permute-done.1.refs_2_), channel_id=1, source_target_pairs={{0,4},{1,5},{2,6},{3,7},{4,0},{5,1},{6,2},{7,3},{8,12},{9,13},{10,... | collective-permute-start | bytes 221192 | tf_op jit(solution)/shard_map/ppermute | solution.py:360
  9.1 5.3 %collective-permute-start.9 = (bf16[288,128]{1,0:T(8,128)(2,1)S(1)}, bf16[288,128]{1,0:T(8,128)(2,1)S(1)}, u32[]{:S(2)}, u32[]{:S(2)}) collective-permute-start(bf16[288,128]{1,0:T(8,128)(2,1)S(1)} %collective-permute-done.2.refs_3_), channel_id=1, source_target_pairs={{0,2},{1,3},{2,0},{3,1},{4,6},{5,7},{6,4},{7,5},{8,10},{9,11},{10,... | collective-permute-start | bytes 221192 | tf_op jit(solution)/shard_map/ppermute | solution.py:360
  10.3 5.8 %collective-permute-start.5 = (bf16[288,128]{1,0:T(8,128)(2,1)S(1)}, bf16[288,128]{1,0:T(8,128)(2,1)S(1)}, u32[]{:S(2)}, u32[]{:S(2)}) collective-permute-start(bf16[288,128]{1,0:T(8,128)(2,1)S(1)} %collective-permute-done.2.refs_3_), channel_id=1, source_target_pairs={{0,1},{1,0},{2,3},{3,2},{4,5},{5,4},{6,7},{7,6},{8,9},{9,8},{10,11... | collective-permute-start | bytes 221192 | tf_op jit(solution)/shard_map/ppermute | solution.py:360
  11.9 4.2 %collective-permute-start.8 = (bf16[288,128]{1,0:T(8,128)(2,1)S(1)}, bf16[288,128]{1,0:T(8,128)(2,1)S(1)}, u32[]{:S(2)}, u32[]{:S(2)}) collective-permute-start(bf16[288,128]{1,0:T(8,128)(2,1)S(1)} %collective-permute-done.1.refs_2_), channel_id=1, source_target_pairs={{0,2},{1,3},{2,0},{3,1},{4,6},{5,7},{6,4},{7,5},{8,10},{9,11},{10,... | collective-permute-start | bytes 221192 | tf_op jit(solution)/shard_map/ppermute | solution.py:360
  12.2 4.8 %collective-permute-start.4 = (bf16[288,128]{1,0:T(8,128)(2,1)S(1)}, bf16[288,128]{1,0:T(8,128)(2,1)S(1)}, u32[]{:S(2)}, u32[]{:S(2)}) collective-permute-start(bf16[288,128]{1,0:T(8,128)(2,1)S(1)} %collective-permute-done.1.refs_2_), channel_id=1, source_target_pairs={{0,1},{1,0},{2,3},{3,2},{4,5},{5,4},{6,7},{7,6},{8,9},{9,8},{10,11... | collective-permute-start | bytes 221192 | tf_op jit(solution)/shard_map/ppermute | solution.py:360
  13.2 4.9 %collective-permute-start.13 = (bf16[288,128]{1,0:T(8,128)(2,1)S(1)}, bf16[288,128]{1,0:T(8,128)(2,1)S(1)}, u32[]{:S(2)}, u32[]{:S(2)}) collective-permute-start(bf16[288,128]{1,0:T(8,128)(2,1)S(1)} %collective-permute-done.6.refs_7_), channel_id=1, source_target_pairs={{0,2},{1,3},{2,0},{3,1},{4,6},{5,7},{6,4},{7,5},{8,10},{9,11},{10,... | collective-permute-start | bytes 221192 | tf_op jit(solution)/shard_map/ppermute | solution.py:360
  14.3 4.3 %collective-permute-start.7 = (bf16[288,128]{1,0:T(8,128)(2,1)S(1)}, bf16[288,128]{1,0:T(8,128)(2,1)S(1)}, u32[]{:S(2)}, u32[]{:S(2)}) collective-permute-start(bf16[288,128]{1,0:T(8,128)(2,1)S(1)} %collective-permute-done.3.refs_4_), channel_id=1, source_target_pairs={{0,1},{1,0},{2,3},{3,2},{4,5},{5,4},{6,7},{7,6},{8,9},{9,8},{10,11... | collective-permute-start | bytes 221192 | tf_op jit(solution)/shard_map/ppermute | solution.py:360
  16.1 2.6 %collective-permute-start.10 = (bf16[288,128]{1,0:T(8,128)(2,1)S(1)}, bf16[288,128]{1,0:T(8,128)(2,1)S(1)}, u32[]{:S(2)}, u32[]{:S(2)}) collective-permute-start(bf16[288,128]{1,0:T(8,128)(2,1)S(1)} %collective-permute-done.6.refs_7_), channel_id=1, source_target_pairs={{0,1},{1,0},{2,3},{3,2},{4,5},{5,4},{6,7},{7,6},{8,9},{9,8},{10,11... | collective-permute-start | bytes 221192 | tf_op jit(solution)/shard_map/ppermute | solution.py:360
  16.2 2.5 %collective-permute-start.12 = (bf16[288,128]{1,0:T(8,128)(2,1)S(1)}, bf16[288,128]{1,0:T(8,128)(2,1)S(1)}, u32[]{:S(2)}, u32[]{:S(2)}) collective-permute-start(bf16[288,128]{1,0:T(8,128)(2,1)S(1)} %collective-permute-done.9.refs_4_.refs_10_), channel_id=1, source_target_pairs={{0,1},{1,0},{2,3},{3,2},{4,5},{5,4},{6,7},{7,6},{8,9},{9,8},{10,11... | collective-permute-start | bytes 221192 | tf_op jit(solution)/shard_map/ppermute | solution.py:360
  17.0 1.7 %collective-permute-start.11 = (bf16[288,128]{1,0:T(8,128)(2,1)S(1)}, bf16[288,128]{1,0:T(8,128)(2,1)S(1)}, u32[]{:S(2)}, u32[]{:S(2)}) collective-permute-start(bf16[288,128]{1,0:T(8,128)(2,1)S(1)} %collective-permute-done.8.refs_3_.refs_9_), channel_id=1, source_target_pairs={{0,1},{1,0},{2,3},{3,2},{4,5},{5,4},{6,7},{7,6},{8,9},{9,8},{10,11... | collective-permute-start | bytes 221192 | tf_op jit(solution)/shard_map/ppermute | solution.py:360
  18.1 1.9 %collective-permute-start.14 = (bf16[288,128]{1,0:T(8,128)(2,1)S(1)}, bf16[288,128]{1,0:T(8,128)(2,1)S(1)}, u32[]{:S(2)}, u32[]{:S(2)}) collective-permute-start(bf16[288,128]{1,0:T(8,128)(2,1)S(1)} %collective-permute-done.13.refs_14_), channel_id=1, source_target_pairs={{0,1},{1,0},{2,3},{3,2},{4,5},{5,4},{6,7},{7,6},{8,9},{9,8},{10,11... | collective-permute-start | bytes 221192 | tf_op jit(solution)/shard_map/ppermute | solution.py:360
